TPU v7x, 512 devices: a whole 4x8x8 slice. The times are simulated.
512 devices in a mesh: store: 8 (over y), ctx: 16 (over z, core), tensor: 4 (over x).
Axes of the slice: x: 4, y: 8, z: 8, core: 2. Of those that a mesh axis runs over, the one named last changes fastest.
Arguments:
- queries: bfloat16 [65536, 4096], P(('store', 'ctx', 'tensor')), may hold values from -21 to 21
- grad_out: bfloat16 [65536, 4096], P(('store', 'ctx', 'tensor')), may hold values from -6 to 6
- attn_out: bfloat16 [65536, 4096], P(('store', 'ctx', 'tensor')), may hold values from -3 to 3
- passage_keys: bfloat16 [512, 16, 512], P(('store', 'ctx'), None, 'tensor'), may hold values from -9 to 9
- passage_values: bfloat16 [512, 16, 512], P(('store', 'ctx'), None, 'tensor'), may hold values from -6 to 6
- block_lists: int32 [512, 16], replicated, may hold values from 0 to 511, as said below
- passage_lengths: int32 [512], replicated, may hold values from 4 to 16, as said below
Outputs:
- query_grad: bfloat16 [65536, 4096], P(('store', 'ctx', 'tensor'))
- key_grad: bfloat16 [512, 16, 512], P(('store', 'ctx'), None, 'tensor')
- value_grad: bfloat16 [512, 16, 512], P(('store', 'ctx'), None, 'tensor')
Inputs may be any that keep to these rules, and one draw needn't show every extreme that they name: `block_lists`: passage p belongs to owner floor(p / 4). The rows of query shard c (rows c * 4 to (c + 1) * 4 - 1) together name 64 passages of as many different owners. `passage_lengths`: some passage has exactly 16 live slots.
All inputs are finite; a program needn't handle non-finite values.
Results may differ from a plain program's by a relative error of at most 0.02.
Values may be sent and summed in bfloat16 or wider, within the bound.
No kernel may reach another device: no remote copies, remote signals or barrier semaphores. Data moves between devices by JAX's collectives and lax.ppermute only.
A program may use at most 64 MiB of HBM per device.

v0:
```python
import jax
import jax.numpy as jnp
from jax import lax
from jax.sharding import PartitionSpec as P

DH = 128
QBLK = 128


def local(queries, grad_out, attn_out, passage_keys, passage_values, block_lists, passage_lengths):
    store_count = lax.axis_size("store")
    ctx_count = lax.axis_size("ctx")
    shard_count = store_count * ctx_count
    my_shard = lax.axis_index("store") * ctx_count + lax.axis_index("ctx")
    pass_dev, key_len, key_width = passage_keys.shape
    head_queries, head_grads, head_outs = (
        lax.all_to_all(queries, "tensor", split_axis=1, concat_axis=0, tiled=True),
        lax.all_to_all(grad_out, "tensor", split_axis=1, concat_axis=0, tiled=True),
        lax.all_to_all(attn_out, "tensor", split_axis=1, concat_axis=0, tiled=True),
    )
    tok_rows = head_queries.shape[0]
    head_count = head_queries.shape[1] // DH
    group_count = key_width // DH
    share = head_count // group_count
    blocks_here = tok_rows // QBLK
    list_len = block_lists.shape[1]
    key_count = list_len * key_len
    key_scale = DH ** (-0.5)
    dest_lists = block_lists.reshape(shard_count, blocks_here * list_len)
    my_passages = my_shard * pass_dev + jnp.arange(pass_dev, dtype=jnp.int32)
    send_pick = jnp.any(dest_lists[:, :, None] == my_passages[None, None, :], axis=1).astype(
        jnp.bfloat16
    )
    stacked = jnp.stack([passage_keys, passage_values])
    outgoing = jnp.einsum(
        "nk,akpc->anpc", send_pick, stacked, preferred_element_type=jnp.float32
    ).astype(jnp.bfloat16)
    incoming = lax.all_to_all(outgoing, ("store", "ctx"), split_axis=1, concat_axis=1, tiled=True)
    own_lists = lax.dynamic_slice_in_dim(block_lists, my_shard * blocks_here, blocks_here, 0)
    slot_of = (own_lists // pass_dev).reshape(blocks_here * list_len)
    passage_ids = jnp.arange(passage_lengths.shape[0], dtype=jnp.int32)
    listed_length = jnp.sum(
        jnp.where(
            own_lists[:, :, None] == passage_ids[None, None, :], passage_lengths[None, None, :], 0
        ),
        axis=2,
    )
    live = (
        jnp.arange(key_len, dtype=jnp.int32)[None, None, :] < listed_length[:, :, None]
    ).reshape(blocks_here, key_count)
    block_keys = (
        incoming[0][slot_of].reshape(blocks_here, key_count, group_count, DH).transpose(0, 2, 1, 3)
    )
    block_values = (
        incoming[1][slot_of].reshape(blocks_here, key_count, group_count, DH).transpose(0, 2, 1, 3)
    )

    def head_layout(rows):
        return rows.reshape(blocks_here, QBLK, group_count, share, DH).transpose(0, 2, 3, 1, 4)

    query_blocks = head_layout(head_queries)
    grad_blocks = head_layout(head_grads)
    row_delta = jnp.sum(
        head_grads.astype(jnp.float32).reshape(tok_rows, head_count, DH)
        * head_outs.astype(jnp.float32).reshape(tok_rows, head_count, DH),
        axis=2,
    )
    row_delta = row_delta.reshape(blocks_here, QBLK, group_count, share).transpose(0, 2, 3, 1)

    def block_step(carry, inputs):
        query_group, grad_group, delta_group, group_keys, group_values, live_row = inputs
        mask = live_row[None, None, None, :]
        scores = (
            jnp.einsum(
                "gjqd,gkd->gjqk", query_group, group_keys, preferred_element_type=jnp.float32
            )
            * key_scale
        )
        masked = jnp.where(mask, scores, jnp.float32(-1e30))
        row_top = jnp.max(masked, axis=3, keepdims=True)
        row_total = jnp.sum(
            jnp.where(mask, jnp.exp(masked - row_top), jnp.float32(0.0)), axis=3, keepdims=True
        )
        log_total = row_top + jnp.log(row_total)
        weights = jnp.where(mask, jnp.exp(scores - log_total), jnp.float32(0.0))
        weights_half = weights.astype(jnp.bfloat16)
        weight_grads = jnp.einsum(
            "gjqd,gkd->gjqk", grad_group, group_values, preferred_element_type=jnp.float32
        )
        score_grads = (weights * (weight_grads - delta_group[:, :, :, None])).astype(jnp.bfloat16)
        query_part = (
            jnp.einsum(
                "gjqk,gkd->gjqd", score_grads, group_keys, preferred_element_type=jnp.float32
            )
            * key_scale
        )
        key_term = (
            jnp.einsum(
                "gjqk,gjqd->gkd", score_grads, query_group, preferred_element_type=jnp.float32
            )
            * key_scale
        )
        value_term = jnp.einsum(
            "gjqk,gjqd->gkd", weights_half, grad_group, preferred_element_type=jnp.float32
        )
        return (
            carry,
            (
                query_part.astype(jnp.bfloat16),
                key_term.astype(jnp.bfloat16),
                value_term.astype(jnp.bfloat16),
            ),
        )

    _, (query_parts, key_terms, value_terms) = lax.scan(
        block_step,
        jnp.float32(0.0),
        (query_blocks, grad_blocks, row_delta, block_keys, block_values, live),
    )

    def slot_layout(terms):
        return (
            terms.reshape(blocks_here, group_count, list_len, key_len, DH)
            .transpose(0, 2, 3, 1, 4)
            .reshape(blocks_here * list_len, key_len, key_width)
        )

    partials = jnp.stack([slot_layout(key_terms), slot_layout(value_terms)])
    outgoing_grads = (
        jnp.zeros((2, shard_count, key_len, key_width), jnp.bfloat16).at[:, slot_of].set(partials)
    )
    returned = lax.all_to_all(
        outgoing_grads, ("store", "ctx"), split_axis=1, concat_axis=1, tiled=True
    )
    grad_sums = jnp.einsum(
        "nk,anpc->akpc", send_pick, returned, preferred_element_type=jnp.float32
    ).astype(jnp.bfloat16)
    query_rows = query_parts.transpose(0, 3, 1, 2, 4).reshape(tok_rows, head_count * DH)
    query_grad = lax.all_to_all(query_rows, "tensor", split_axis=0, concat_axis=1, tiled=True)
    return (query_grad, grad_sums[0], grad_sums[1])


def solution(mesh):
    return jax.shard_map(
        local,
        mesh=mesh,
        in_specs=(
            P(("store", "ctx", "tensor"), None),
            P(("store", "ctx", "tensor"), None),
            P(("store", "ctx", "tensor"), None),
            P(("store", "ctx"), None, "tensor"),
            P(("store", "ctx"), None, "tensor"),
            P(),
            P(),
        ),
        out_specs=(
            P(("store", "ctx", "tensor"), None),
            P(("store", "ctx"), None, "tensor"),
            P(("store", "ctx"), None, "tensor"),
        ),
        check_vma=False,
    )
```

profile of v0, /device:TPU:1, one launch (start us, length us, event | category | flops | bytes accessed | tf_op | source)
XLA Modules:
  0.0 194.2 jit_solution(9733910168425280447)
XLA Ops:
  0.6 2.4 %copy.78 = bf16[128,4096]{0,1:T(8,128)(2,1)} copy(bf16[128,4096]{1,0:T(8,128)(2,1)} %param.10) | data formatting | bytes 2097152 | tf_op args[1]
  3.0 4.8 %all-to-all-start.2 = ((bf16[128,4,1024]{0,2,1:T(8,128)(2,1)}), bf16[128,4,1024]{0,2,1:T(8,128)(2,1)}, u32[]{:S(2)}, u32[]{:S(2)}) async-start(bf16[128,4,1024]{0,2,1:T(8,128)(2,1)} %bitcast.25), calls=%async_computation.2 | async-start | bytes 2097152 | tf_op jit(solution)/shard_map/all_to_all | solution.py:18
  7.9 1.3 copy.80
  9.2 8.5 %all-to-all-done.2 = bf16[128,4,1024]{0,2,1:T(8,128)(2,1)} async-done(((bf16[128,4,1024]{0,2,1:T(8,128)(2,1)}), bf16[128,4,1024]{0,2,1:T(8,128)(2,1)}, u32[]{:S(2)}, u32[]{:S(2)}) %all-to-all-start.2) | async-done | bytes 1048608 | tf_op jit(solution)/shard_map/all_to_all | solution.py:18
  17.7 3.5 %all-to-all-start.3 = ((bf16[128,4,1024]{0,2,1:T(8,128)(2,1)}), bf16[128,4,1024]{0,2,1:T(8,128)(2,1)S(1)}, u32[]{:S(2)}, u32[]{:S(2)}) async-start(bf16[128,4,1024]{0,2,1:T(8,128)(2,1)} %bitcast.32), calls=%async_computation.3 | async-start | bytes 2097152 | tf_op jit(solution)/shard_map/all_to_all | solution.py:19
  21.7 0.5 fusion.36
  22.3 1.7 copy.75
  24.0 6.9 %all-to-all-done.3 = bf16[128,4,1024]{0,2,1:T(8,128)(2,1)S(1)} async-done(((bf16[128,4,1024]{0,2,1:T(8,128)(2,1)}), bf16[128,4,1024]{0,2,1:T(8,128)(2,1)S(1)}, u32[]{:S(2)}, u32[]{:S(2)}) %all-to-all-start.3) | async-done | bytes 1048608 | tf_op jit(solution)/shard_map/all_to_all | solution.py:19
  30.9 28.1 %all-to-all-start.1 = ((bf16[2,128,16,128]{3,2,0,1:T(8,128)(2,1)}), bf16[2,128,16,128]{3,2,0,1:T(8,128)(2,1)S(1)}, u32[]{:S(2)}, u32[]{:S(2)}) async-start(bf16[2,128,16,128]{3,2,0,1:T(8,128)(2,1)} %copy.75), calls=%async_computation.1 | async-start | bytes 2097152 | tf_op jit(solution)/shard_map/all_to_all | solution.py:38
  59.4 0.2 select_reduce_fusion.2
  59.8 1.3 copy.70
  61.2 28.3 %all-to-all-done.1 = bf16[2,128,16,128]{3,2,0,1:T(8,128)(2,1)S(1)} async-done(((bf16[2,128,16,128]{3,2,0,1:T(8,128)(2,1)}), bf16[2,128,16,128]{3,2,0,1:T(8,128)(2,1)S(1)}, u32[]{:S(2)}, u32[]{:S(2)}) %all-to-all-start.1) | async-done | bytes 1048608 | tf_op jit(solution)/shard_map/all_to_all | solution.py:38
  89.4 1.0 copy-done
  90.4 3.5 %all-to-all-start = ((bf16[128,4,1024]{0,2,1:T(8,128)(2,1)}), bf16[128,4,1024]{0,2,1:T(8,128)(2,1)S(1)}, u32[]{:S(2)}, u32[]{:S(2)}) async-start(bf16[128,4,1024]{0,2,1:T(8,128)(2,1)} %bitcast.12), calls=%async_computation | async-start | bytes 2097152 | tf_op jit(solution)/shard_map/all_to_all | solution.py:17
  93.9 1.7 bitcast_multiply_fusion
  95.7 1.9 copy.81
  97.5 2.1 %copy.103 = f32[64,8,8,128]{3,2,1,0:T(8,128)S(1)} copy(f32[64,8,8,128]{3,1,2,0:T(8,128)} %bitcast.161) | data formatting | bytes 4194304
  99.6 0.6 reduce_sum.28
  100.3 1.4 slice_bitcast_fusion
  101.7 0.6 gather_fusion
  102.3 0.6 gather_fusion.1
  103.0 4.7 %all-to-all-done = bf16[128,4,1024]{0,2,1:T(8,128)(2,1)S(1)} async-done(((bf16[128,4,1024]{0,2,1:T(8,128)(2,1)}), bf16[128,4,1024]{0,2,1:T(8,128)(2,1)S(1)}, u32[]{:S(2)}, u32[]{:S(2)}) %all-to-all-start) | async-done | bytes 1048608 | tf_op jit(solution)/shard_map/all_to_all | solution.py:17
  107.7 26.9 %while.14 = (s32[]{:T(128)}, bf16[4,1,8,128,128]{3,4,2,0,1:T(8,128)(2,1)}, bf16[4,1,256,128]{3,2,1,0:T(8,128)(2,1)}, bf16[4,1,256,128]{3,2,1,0:T(8,128)(2,1)}, p...) while((s32[]{:T(128)}, ...), condition=%wide.region_6.7_spmd, body=%wide.region_3.6_spmd.sunk | while | flops 339835904 | bytes 10603185 | solution.py:115
  107.7 0.4 select_reduce_fusion.5
  108.1 0.4 select_reduce_fusion.6
  108.6 1.4 fusion.70
  110.0 0.3 fusion.71
  110.3 0.2 copy.109
  110.5 0.7 constant_dynamic-update-slice_fusion.2
  111.2 2.2 %fusion.73 = bf16[4,1,256,128]{3,2,1,0:T(8,128)(2,1)} fusion(bf16[4,1,256,128]{3,2,1,0:T(8,128)(2,1)} %get-tuple-element.211, s32[]{:T(128)} %get-tuple-element.208, f32[8,128,256]{2,1,0:T(8,128)S(1)} %get-tuple-element.195, f32[8,128]{1,0:T(8,128)S(1)} %log_add_fusion.2, pred[256]{0:T(512)(128)(4,1)S(1)} %dynamic-slice_reduce_fusion.2, ...), kind=kOutput, calls=%fused_computation.16.clone.1 | convolution fusion | flops 67928064 | bytes 1381632 | tf_op jit(solution)/shard_map/while/body/eval_jaxpr/gjqk,gjqd->gkd/dot_general | solution.py:103
  113.4 1.0 fusion.72
  114.4 0.4 select_reduce_fusion.5
  114.8 0.4 select_reduce_fusion.6
  115.3 1.4 fusion.70
  116.7 0.3 fusion.71
  117.0 0.2 copy.109
  117.2 0.7 constant_dynamic-update-slice_fusion.2
  117.9 2.2 %fusion.73 = bf16[4,1,256,128]{3,2,1,0:T(8,128)(2,1)} fusion(bf16[4,1,256,128]{3,2,1,0:T(8,128)(2,1)} %get-tuple-element.211, s32[]{:T(128)} %get-tuple-element.208, f32[8,128,256]{2,1,0:T(8,128)S(1)} %get-tuple-element.195, f32[8,128]{1,0:T(8,128)S(1)} %log_add_fusion.2, pred[256]{0:T(512)(128)(4,1)S(1)} %dynamic-slice_reduce_fusion.2, ...), kind=kOutput, calls=%fused_computation.16.clone.1 | convolution fusion | flops 67928064 | bytes 1381632 | tf_op jit(solution)/shard_map/while/body/eval_jaxpr/gjqk,gjqd->gkd/dot_general | solution.py:103
  120.1 1.0 fusion.72
  121.1 0.4 select_reduce_fusion.5
  121.6 0.4 select_reduce_fusion.6
  122.0 1.4 fusion.70
  123.4 0.3 fusion.71
  123.7 0.2 copy.109
  123.9 0.7 constant_dynamic-update-slice_fusion.2
  124.7 2.2 %fusion.73 = bf16[4,1,256,128]{3,2,1,0:T(8,128)(2,1)} fusion(bf16[4,1,256,128]{3,2,1,0:T(8,128)(2,1)} %get-tuple-element.211, s32[]{:T(128)} %get-tuple-element.208, f32[8,128,256]{2,1,0:T(8,128)S(1)} %get-tuple-element.195, f32[8,128]{1,0:T(8,128)S(1)} %log_add_fusion.2, pred[256]{0:T(512)(128)(4,1)S(1)} %dynamic-slice_reduce_fusion.2, ...), kind=kOutput, calls=%fused_computation.16.clone.1 | convolution fusion | flops 67928064 | bytes 1381632 | tf_op jit(solution)/shard_map/while/body/eval_jaxpr/gjqk,gjqd->gkd/dot_general | solution.py:103
  126.8 1.0 fusion.72
  127.9 0.4 select_reduce_fusion.5
  128.3 0.4 select_reduce_fusion.6
  128.8 1.4 fusion.70
  130.2 0.3 fusion.71
  130.7 0.7 constant_dynamic-update-slice_fusion.2
  131.4 2.2 %fusion.73 = bf16[4,1,256,128]{3,2,1,0:T(8,128)(2,1)} fusion(bf16[4,1,256,128]{3,2,1,0:T(8,128)(2,1)} %get-tuple-element.211, s32[]{:T(128)} %get-tuple-element.208, f32[8,128,256]{2,1,0:T(8,128)S(1)} %get-tuple-element.195, f32[8,128]{1,0:T(8,128)S(1)} %log_add_fusion.2, pred[256]{0:T(512)(128)(4,1)S(1)} %dynamic-slice_reduce_fusion.2, ...), kind=kOutput, calls=%fused_computation.16.clone.1 | convolution fusion | flops 67928064 | bytes 1381632 | tf_op jit(solution)/shard_map/while/body/eval_jaxpr/gjqk,gjqd->gkd/dot_general | solution.py:103
  133.6 1.0 fusion.72
  134.6 3.6 %all-to-all-start.4 = ((bf16[4,128,1024]{1,2,0:T(8,128)(2,1)}), bf16[4,128,1024]{1,2,0:T(8,128)(2,1)S(1)}, u32[]{:S(2)}, u32[]{:S(2)}) async-start(bf16[4,128,1024]{1,2,0:T(8,128)(2,1)} %bitcast.165), calls=%async_computation.4 | async-start | bytes 2097152 | tf_op jit(solution)/shard_map/all_to_all | solution.py:139
  138.5 3.3 %scatter_fusion = bf16[2,128,16,128]{3,2,1,0:T(8,128)(2,1)S(1)} fusion(bf16[2,128,16,128]{3,2,1,0:T(8,128)(2,1)S(1)} %broadcast_in_dim.69, s32[64]{0:T(128)S(1)} %fusion.46, bf16[64,2,16,128]{3,2,1,0:T(8,128)(2,1)S(1)} %copy.88), kind=kCustom, calls=%fused_computation.2 | custom fusion | bytes 1573120 | tf_op jit(solution)/shard_map/scatter | solution.py:130
  141.8 1.2 copy.89
  142.9 8.1 %all-to-all-done.4 = bf16[4,128,1024]{1,2,0:T(8,128)(2,1)S(1)} async-done(((bf16[4,128,1024]{1,2,0:T(8,128)(2,1)}), bf16[4,128,1024]{1,2,0:T(8,128)(2,1)S(1)}, u32[]{:S(2)}, u32[]{:S(2)}) %all-to-all-start.4) | async-done | bytes 1048608 | tf_op jit(solution)/shard_map/all_to_all | solution.py:139
  151.0 11.0 %all-to-all-start.5 = ((bf16[2,128,16,128]{3,2,0,1:T(8,128)(2,1)}), bf16[2,128,16,128]{3,2,0,1:T(8,128)(2,1)S(1)}, u32[]{:S(2)}, u32[]{:S(2)}) async-start(bf16[2,128,16,128]{3,2,0,1:T(8,128)(2,1)} %copy.89), calls=%async_computation.5 | async-start | bytes 2097152 | tf_op jit(solution)/shard_map/all_to_all | solution.py:132
  162.1 1.3 copy.91
  163.4 29.1 %all-to-all-done.5 = bf16[2,128,16,128]{3,2,0,1:T(8,128)(2,1)S(1)} async-done(((bf16[2,128,16,128]{3,2,0,1:T(8,128)(2,1)}), bf16[2,128,16,128]{3,2,0,1:T(8,128)(2,1)S(1)}, u32[]{:S(2)}, u32[]{:S(2)}) %all-to-all-start.5) | async-done | bytes 1048608 | tf_op jit(solution)/shard_map/all_to_all | solution.py:132
  192.5 0.4 fusion.37
  193.0 0.6 copy.92
  193.6 0.6 copy.93
  (73 shorter events, 1.8 us)
Async XLA Ops:
  0.6 7.2 %copy-start.4 = (bf16[128,4096]{1,0:T(8,128)(2,1)S(1)}, bf16[128,4096]{1,0:T(8,128)(2,1)}, u32[]{:S(2)}) copy-start(bf16[128,4096]{1,0:T(8,128)(2,1)} %param.11) | copy-start | bytes 3145732
  3.0 14.7 %all-to-all-start.2 = ((bf16[128,4,1024]{0,2,1:T(8,128)(2,1)}), bf16[128,4,1024]{0,2,1:T(8,128)(2,1)}, u32[]{:S(2)}, u32[]{:S(2)}) async-start(bf16[128,4,1024]{0,2,1:T(8,128)(2,1)} %bitcast.25), calls=%async_computation.2 | async-start | bytes 2097152 | tf_op jit(solution)/shard_map/all_to_all | solution.py:18
  7.8 13.4 %copy-start.8 = (s32[512,16]{0,1:T(8,128)S(1)}, s32[512,16]{0,1:T(8,128)}, u32[]{:S(2)}) copy-start(s32[512,16]{0,1:T(8,128)} %param.14) | copy-start | bytes 98308
  7.8 13.8 %copy-start.9 = (bf16[4,16,128]{2,1,0:T(8,128)(2,1)S(1)}, bf16[4,16,128]{2,1,0:T(8,128)(2,1)}, u32[]{:S(2)}) copy-start(bf16[4,16,128]{2,1,0:T(8,128)(2,1)} %param.13) | copy-start | bytes 49156
  7.8 13.8 %copy-start.10 = (bf16[4,16,128]{2,1,0:T(8,128)(2,1)S(1)}, bf16[4,16,128]{2,1,0:T(8,128)(2,1)}, u32[]{:S(2)}) copy-start(bf16[4,16,128]{2,1,0:T(8,128)(2,1)} %param.12) | copy-start | bytes 49156
  17.7 13.2 %all-to-all-start.3 = ((bf16[128,4,1024]{0,2,1:T(8,128)(2,1)}), bf16[128,4,1024]{0,2,1:T(8,128)(2,1)S(1)}, u32[]{:S(2)}, u32[]{:S(2)}) async-start(bf16[128,4,1024]{0,2,1:T(8,128)(2,1)} %bitcast.32), calls=%async_computation.3 | async-start | bytes 2097152 | tf_op jit(solution)/shard_map/all_to_all | solution.py:19
  22.2 37.1 %copy-start.11 = (s32[512]{0:T(512)S(1)}, s32[512]{0:T(512)}, u32[]{:S(2)}) copy-start(s32[512]{0:T(512)} %param.15) | copy-start | bytes 6148
  22.3 37.6 %copy-start.5 = (bf16[128,4096]{1,0:T(8,128)(2,1)S(1)}, bf16[128,4096]{1,0:T(8,128)(2,1)}, u32[]{:S(2)}) copy-start(bf16[128,4096]{1,0:T(8,128)(2,1)} %param.9) | copy-start | bytes 3145732
  30.9 30.2 %copy-start.1 = (bf16[128,4,1024]{0,2,1:T(8,128)(2,1)}, bf16[128,4,1024]{0,2,1:T(8,128)(2,1)S(1)}, u32[]{:S(2)}) copy-start(bf16[128,4,1024]{0,2,1:T(8,128)(2,1)S(1)} %all-to-all-done.3) | copy-start | bytes 3145732
  30.9 58.5 %all-to-all-start.1 = ((bf16[2,128,16,128]{3,2,0,1:T(8,128)(2,1)}), bf16[2,128,16,128]{3,2,0,1:T(8,128)(2,1)S(1)}, u32[]{:S(2)}, u32[]{:S(2)}) async-start(bf16[2,128,16,128]{3,2,0,1:T(8,128)(2,1)} %copy.75), calls=%async_computation.1 | async-start | bytes 2097152 | tf_op jit(solution)/shard_map/all_to_all | solution.py:38
  89.4 1.0 copy-start
  90.4 17.3 %all-to-all-start = ((bf16[128,4,1024]{0,2,1:T(8,128)(2,1)}), bf16[128,4,1024]{0,2,1:T(8,128)(2,1)S(1)}, u32[]{:S(2)}, u32[]{:S(2)}) async-start(bf16[128,4,1024]{0,2,1:T(8,128)(2,1)} %bitcast.12), calls=%async_computation | async-start | bytes 2097152 | tf_op jit(solution)/shard_map/all_to_all | solution.py:17
  107.7 2.3 %copy-start.2 = (bf16[4,1,256,128]{3,2,1,0:T(8,128)(2,1)}, bf16[4,1,256,128]{3,2,1,0:T(8,128)(2,1)S(1)}, u32[]{:S(2)}) copy-start(bf16[4,1,256,128]{3,2,1,0:T(8,128)(2,1)S(1)} %get-tuple-element.227) | copy-start | bytes 786436 | tf_op jit(solution)/shard_map/while
  111.2 3.2 %copy-start.3 = (bf16[4,1,256,128]{3,2,1,0:T(8,128)(2,1)S(1)}, bf16[4,1,256,128]{3,2,1,0:T(8,128)(2,1)}, u32[]{:S(2)}) copy-start(bf16[4,1,256,128]{3,2,1,0:T(8,128)(2,1)} %copy-done.2) | copy-start | bytes 786436 | tf_op jit(solution)/shard_map/while
  114.4 2.3 %copy-start.2 = (bf16[4,1,256,128]{3,2,1,0:T(8,128)(2,1)}, bf16[4,1,256,128]{3,2,1,0:T(8,128)(2,1)S(1)}, u32[]{:S(2)}) copy-start(bf16[4,1,256,128]{3,2,1,0:T(8,128)(2,1)S(1)} %get-tuple-element.227) | copy-start | bytes 786436 | tf_op jit(solution)/shard_map/while
  117.9 3.2 %copy-start.3 = (bf16[4,1,256,128]{3,2,1,0:T(8,128)(2,1)S(1)}, bf16[4,1,256,128]{3,2,1,0:T(8,128)(2,1)}, u32[]{:S(2)}) copy-start(bf16[4,1,256,128]{3,2,1,0:T(8,128)(2,1)} %copy-done.2) | copy-start | bytes 786436 | tf_op jit(solution)/shard_map/while
  121.1 2.3 %copy-start.2 = (bf16[4,1,256,128]{3,2,1,0:T(8,128)(2,1)}, bf16[4,1,256,128]{3,2,1,0:T(8,128)(2,1)S(1)}, u32[]{:S(2)}) copy-start(bf16[4,1,256,128]{3,2,1,0:T(8,128)(2,1)S(1)} %get-tuple-element.227) | copy-start | bytes 786436 | tf_op jit(solution)/shard_map/while
  124.7 3.2 %copy-start.3 = (bf16[4,1,256,128]{3,2,1,0:T(8,128)(2,1)S(1)}, bf16[4,1,256,128]{3,2,1,0:T(8,128)(2,1)}, u32[]{:S(2)}) copy-start(bf16[4,1,256,128]{3,2,1,0:T(8,128)(2,1)} %copy-done.2) | copy-start | bytes 786436 | tf_op jit(solution)/shard_map/while
  127.8 2.3 %copy-start.2 = (bf16[4,1,256,128]{3,2,1,0:T(8,128)(2,1)}, bf16[4,1,256,128]{3,2,1,0:T(8,128)(2,1)S(1)}, u32[]{:S(2)}) copy-start(bf16[4,1,256,128]{3,2,1,0:T(8,128)(2,1)S(1)} %get-tuple-element.227) | copy-start | bytes 786436 | tf_op jit(solution)/shard_map/while
  131.4 3.2 %copy-start.3 = (bf16[4,1,256,128]{3,2,1,0:T(8,128)(2,1)S(1)}, bf16[4,1,256,128]{3,2,1,0:T(8,128)(2,1)}, u32[]{:S(2)}) copy-start(bf16[4,1,256,128]{3,2,1,0:T(8,128)(2,1)} %copy-done.2) | copy-start | bytes 786436 | tf_op jit(solution)/shard_map/while
  134.6 3.7 %copy-start.6 = (bf16[4,1,256,128]{3,2,1,0:T(8,128)(2,1)S(1)}, bf16[4,1,256,128]{3,2,1,0:T(8,128)(2,1)}, u32[]{:S(2)}) copy-start(bf16[4,1,256,128]{3,2,1,0:T(8,128)(2,1)} %get-tuple-element.58) | copy-start | bytes 786436
  134.6 3.7 %copy-start.7 = (bf16[4,1,256,128]{3,2,1,0:T(8,128)(2,1)S(1)}, bf16[4,1,256,128]{3,2,1,0:T(8,128)(2,1)}, u32[]{:S(2)}) copy-start(bf16[4,1,256,128]{3,2,1,0:T(8,128)(2,1)} %get-tuple-element.59) | copy-start | bytes 786436
  134.6 16.5 %all-to-all-start.4 = ((bf16[4,128,1024]{1,2,0:T(8,128)(2,1)}), bf16[4,128,1024]{1,2,0:T(8,128)(2,1)S(1)}, u32[]{:S(2)}, u32[]{:S(2)}) async-start(bf16[4,128,1024]{1,2,0:T(8,128)(2,1)} %bitcast.165), calls=%async_computation.4 | async-start | bytes 2097152 | tf_op jit(solution)/shard_map/all_to_all | solution.py:139
  151.0 41.5 %all-to-all-start.5 = ((bf16[2,128,16,128]{3,2,0,1:T(8,128)(2,1)}), bf16[2,128,16,128]{3,2,0,1:T(8,128)(2,1)S(1)}, u32[]{:S(2)}, u32[]{:S(2)}) async-start(bf16[2,128,16,128]{3,2,0,1:T(8,128)(2,1)} %copy.89), calls=%async_computation.5 | async-start | bytes 2097152 | tf_op jit(solution)/shard_map/all_to_all | solution.py:132
where the time goes:
time: 195 us; the launch traced here: 194 us
  waiting for transfers between devices  85.7 us (44%)
  starting transfers between devices  54.6 us (28%)
  local copies, waits for them, and re-layouts  26.1 us (13%)
  matrix products  22.1 us (11%)
  other arithmetic  4.61 us (2%)
    all_to_all x1, waiting for transfers between devices, local(): lax.all_to_all(outgoing_grads, ('store', 'ctx'), split_axis=1, concat_axi...  29.1 us
    all_to_all x1, waiting for transfers between devices, local(): lax.all_to_all(outgoing, ('store', 'ctx'), split_axis=1, concat_axis=1, t...  28.3 us
    all_to_all x1, starting transfers between devices, local(): lax.all_to_all(outgoing, ('store', 'ctx'), split_axis=1, concat_axis=1, t...  28.1 us
    all_to_all x1, starting transfers between devices, local(): lax.all_to_all(outgoing_grads, ('store', 'ctx'), split_axis=1, concat_axi...  11 us
    unnamed x28, local copies, waits for them, and re-layouts  10.7 us
    dot_general x4, matrix products, block_step(): jnp.einsum('gjqk,gjqd->gkd', weights_half, grad_group, preferred_element_...  8.7 us
    all_to_all x1, waiting for transfers between devices, local(): lax.all_to_all(grad_out, 'tensor', split_axis=1, concat_axis=0, tiled=True)  8.5 us
    all_to_all x1, waiting for transfers between devices, local(): lax.all_to_all(query_rows, 'tensor', split_axis=0, concat_axis=1, tiled=T...  8.12 us
  transfers between devices with their start and end apart: 6, of which 6 were waited for; matrix products, arithmetic and copies ran while one was open for 11% of the time, Pallas kernels for 0%

commit v1 on v0

v1 whole, which is shorter than its diff:
```python
import jax
import jax.numpy as jnp
from jax import lax
from jax.experimental import pallas as pl
from jax.experimental.pallas import tpu as pltpu
from jax.sharding import PartitionSpec as P

DH = 128
QBLK = 128
BF16 = jnp.bfloat16
F32 = jnp.float32
MASKED = -1e30
NT = (((1,), (1,)), ((), ()))
TN = (((0,), (0,)), ((), ()))
VMEM_LIMIT = 48 * 1024 * 1024


def vmem():
    return pl.BlockSpec(memory_space=pltpu.VMEM)


def smem():
    return pl.BlockSpec(memory_space=pltpu.SMEM)


def params():
    return pltpu.CompilerParams(vmem_limit_bytes=VMEM_LIMIT)


def send_kernel(pick_ref, keys_ref, values_ref, out_ref):
    plen = keys_ref.shape[1]

    def body(n, carry):
        k = jnp.maximum(pick_ref[n], 0)
        out_ref[n, 0:plen, :] = keys_ref[k]
        out_ref[n, plen : 2 * plen, :] = values_ref[k]
        return carry

    lax.fori_loop(0, out_ref.shape[0], body, 0, unroll=8)


def prep_kernel(place_ref, q_ref, g_ref, o_ref, *rest):
    *message_refs, delta_ref = rest
    parts = len(message_refs)
    width = q_ref.shape[1] // parts
    heads = q_ref.shape[1] // DH
    share = heads // parts
    lane = lax.broadcasted_iota(jnp.int32, (QBLK, DH), 1)
    delta = jnp.zeros((QBLK, DH), F32)
    for h in range(heads):
        cols = slice(h * DH, (h + 1) * DH)
        term = jnp.sum(g_ref[:, cols].astype(F32) * o_ref[:, cols].astype(F32), axis=1, keepdims=True)
        delta = jnp.where(lane == h, term, delta)
    delta_ref[...] = delta.T
    for j, message_ref in enumerate(message_refs):
        to = lax.rem(place_ref[0] + j, parts)
        cols = pl.ds(pl.multiple_of(to * width, width), width)
        message_ref[0:QBLK, :] = q_ref[:, cols]
        message_ref[QBLK : 2 * QBLK, :] = g_ref[:, cols]
        rows = delta_ref[pl.ds(pl.multiple_of(to * share, share), share), :]
        high = rows.astype(BF16).astype(F32)
        message_ref[2 * QBLK : 2 * QBLK + 2 * share, :] = jnp.zeros((2 * share, width), BF16)
        message_ref[2 * QBLK : 2 * QBLK + 2 * share, 0:DH] = jnp.concatenate(
            [high, rows - high], axis=0
        ).astype(BF16)


def main_kernel(place_ref, lists_ref, lengths_ref, pass_dev, incoming_ref, *rest):
    parts = lists_ref.shape[0]
    message_refs = rest[:parts]
    dq_refs = rest[parts : 2 * parts]
    out_ref, k_ref, v_ref, bias_ref = rest[2 * parts :]
    list_len = lists_ref.shape[1]
    plen = incoming_ref.shape[1] // 2
    width = message_refs[0].shape[1]
    share = width // DH
    scale = DH ** (-0.5)
    out_ref[...] = jnp.zeros_like(out_ref)
    slot_row = lax.broadcasted_iota(jnp.int32, (plen, DH), 0)
    for j, (message_ref, dq_ref) in enumerate(zip(message_refs, dq_refs)):
        block = lax.rem(place_ref[0] + parts - j, parts)
        owners = []
        for p in range(list_len):
            passage = lists_ref[block, p]
            owner = passage // pass_dev
            owners.append(owner)
            rows = slice(p * plen, (p + 1) * plen)
            k_ref[rows, :] = incoming_ref[owner, 0:plen, :]
            v_ref[rows, :] = incoming_ref[owner, plen : 2 * plen, :]
            bias_ref[rows, :] = jnp.where(slot_row < lengths_ref[passage], 0.0, MASKED)
        keys = k_ref[...]
        values = v_ref[...]
        heads = [slice(h * DH, (h + 1) * DH) for h in range(share)]
        queries = jnp.concatenate([message_ref[0:QBLK, c] for c in heads], axis=0)
        grads = jnp.concatenate([message_ref[QBLK : 2 * QBLK, c] for c in heads], axis=0)
        delta_parts = message_ref[2 * QBLK : 2 * QBLK + 2 * share, 0:DH].astype(F32)
        delta = delta_parts[:share] + delta_parts[share:]
        delta = jnp.concatenate([delta[h : h + 1] for h in range(share)], axis=1)
        bias = jnp.concatenate([bias_ref[...]] * share, axis=1)
        scores = lax.dot_general(keys, queries, NT, preferred_element_type=F32) * scale + bias
        weights = jnp.exp(scores - jnp.max(scores, axis=0, keepdims=True))
        weights = weights * (1.0 / jnp.sum(weights, axis=0, keepdims=True))
        weight_grads = lax.dot_general(values, grads, NT, preferred_element_type=F32)
        score_grads = (weights * (weight_grads - delta)).astype(BF16)
        value_term = jnp.dot(weights.astype(BF16), grads, preferred_element_type=F32).astype(BF16)
        key_term = (jnp.dot(score_grads, queries, preferred_element_type=F32) * scale).astype(BF16)
        for p, owner in enumerate(owners):
            rows = slice(p * plen, (p + 1) * plen)
            out_ref[owner, 0:plen, :] = key_term[rows]
            out_ref[owner, plen : 2 * plen, :] = value_term[rows]
        query_part = lax.dot_general(keys, score_grads, TN, preferred_element_type=F32) * scale
        for c in heads:
            dq_ref[:, c] = query_part[:, c].T.astype(BF16)


def place_kernel(place_ref, *rest):
    *piece_refs, out_ref, sems = rest
    parts = len(piece_refs)
    width = out_ref.shape[1] // parts
    copies = []
    for j, piece_ref in enumerate(piece_refs):
        to = lax.rem(place_ref[0] + j, parts)
        cols = pl.ds(pl.multiple_of(to * width, width), width)
        copies.append(pltpu.make_async_copy(piece_ref, out_ref.at[:, cols], sems.at[j]))
    for copy in copies:
        copy.start()
    for copy in copies:
        copy.wait()


def sum_kernel(pick_ref, terms_ref, keys_ref, values_ref):
    pass_dev, plen, _ = keys_ref.shape

    def body(n, sums):
        k = pick_ref[n]
        term = terms_ref[n].astype(F32)
        return tuple(s + jnp.where(k == i, term, 0.0) for i, s in enumerate(sums))

    zero = jnp.zeros((2 * plen, DH), F32)
    sums = lax.fori_loop(0, terms_ref.shape[0], body, (zero,) * pass_dev, unroll=8)
    for i, s in enumerate(sums):
        keys_ref[i] = s[:plen].astype(BF16)
        values_ref[i] = s[plen:].astype(BF16)


def local(queries, grad_out, attn_out, passage_keys, passage_values, block_lists, passage_lengths):
    shards = lax.axis_size("store") * lax.axis_size("ctx")
    parts = lax.axis_size("tensor")
    my_shard = lax.axis_index("store") * lax.axis_size("ctx") + lax.axis_index("ctx")
    place = lax.axis_index("tensor").astype(jnp.int32).reshape(1)
    pass_dev, plen, _ = passage_keys.shape
    rows, columns = queries.shape
    width = columns // parts
    list_len = block_lists.shape[1]
    all_shape = jax.ShapeDtypeStruct((shards, 2 * plen, DH), BF16)

    picked = jnp.where(block_lists // pass_dev == my_shard, block_lists % pass_dev + 1, 0)
    pick = jnp.sum(picked.reshape(shards, parts * list_len), axis=1) - 1

    outgoing = pl.pallas_call(
        send_kernel,
        out_shape=all_shape,
        in_specs=[smem(), vmem(), vmem()],
        out_specs=vmem(),
        compiler_params=params(),
        name="send",
    )(pick, passage_keys, passage_values)
    incoming = lax.all_to_all(outgoing, ("store", "ctx"), split_axis=0, concat_axis=0, tiled=True)

    message = jax.ShapeDtypeStruct((2 * QBLK + 2 * (width // DH), width), BF16)
    messages = pl.pallas_call(
        prep_kernel,
        out_shape=[message] * parts,
        in_specs=[smem(), vmem(), vmem(), vmem()],
        out_specs=[vmem()] * parts,
        scratch_shapes=[pltpu.VMEM((DH, QBLK), F32)],
        compiler_params=params(),
        cost_estimate=pl.CostEstimate(flops=2 * rows * columns, bytes_accessed=10 * rows * columns, transcendentals=0),
        name="prep",
    )(place, queries, grad_out, attn_out)

    def shift(piece, by):
        if by == 0:
            return piece
        return lax.ppermute(piece, "tensor", [(i, (i + by) % parts) for i in range(parts)])

    messages = [shift(piece, j) for j, piece in enumerate(messages)]
    own_lists = lax.dynamic_slice_in_dim(block_lists, my_shard * parts, parts, 0)

    def main(place_ref, lists_ref, lengths_ref, *refs):
        main_kernel(place_ref, lists_ref, lengths_ref, pass_dev, *refs)

    keys = list_len * plen
    pairs = parts * QBLK * (width // DH) * keys
    *query_parts, outgoing_grads = pl.pallas_call(
        main,
        out_shape=[jax.ShapeDtypeStruct((QBLK, width), BF16)] * parts + [all_shape],
        in_specs=[smem(), smem(), smem(), vmem()] + [vmem()] * parts,
        out_specs=[vmem()] * (parts + 1),
        scratch_shapes=[
            pltpu.VMEM((keys, DH), BF16),
            pltpu.VMEM((keys, DH), BF16),
            pltpu.VMEM((keys, DH), F32),
        ],
        compiler_params=params(),
        cost_estimate=pl.CostEstimate(flops=10 * pairs * DH, bytes_accessed=8 * rows * columns, transcendentals=pairs),
        name="attention",
    )(place, own_lists, passage_lengths, incoming, *messages)

    returned = lax.all_to_all(outgoing_grads, ("store", "ctx"), split_axis=0, concat_axis=0, tiled=True)
    query_parts = [shift(piece, (parts - j) % parts) for j, piece in enumerate(query_parts)]
    query_grad = pl.pallas_call(
        place_kernel,
        out_shape=jax.ShapeDtypeStruct((rows, columns), BF16),
        in_specs=[smem()] + [pl.BlockSpec(memory_space=pl.ANY)] * parts,
        out_specs=pl.BlockSpec(memory_space=pl.ANY),
        scratch_shapes=[pltpu.SemaphoreType.DMA((parts,))],
        cost_estimate=pl.CostEstimate(flops=0, bytes_accessed=4 * rows * columns, transcendentals=0),
        name="place",
    )(place, *query_parts)
    grad_shape = jax.ShapeDtypeStruct(passage_keys.shape, BF16)
    key_grad, value_grad = pl.pallas_call(
        sum_kernel,
        out_shape=[grad_shape, grad_shape],
        in_specs=[smem(), vmem()],
        out_specs=[vmem(), vmem()],
        compiler_params=params(),
        name="sum",
    )(pick, returned)
    return query_grad, key_grad, value_grad


def solution(mesh):
    tokens = P(("store", "ctx", "tensor"), None)
    passages = P(("store", "ctx"), None, "tensor")
    return jax.shard_map(
        local,
        mesh=mesh,
        in_specs=(tokens, tokens, tokens, passages, passages, P(), P()),
        out_specs=(tokens, passages, passages),
        check_vma=False,
    )
```

time: 195 us -> 137 us (0.70)
  waiting for transfers between devices: 85.7 us -> 31.3 us
  Pallas kernels: 0 us -> 44.8 us
  matrix products: 22.1 us -> 0 us
  local copies, waits for them, and re-layouts: 26.1 us -> 4.82 us
  other arithmetic: 4.61 us -> 0.92 us
    all_to_all x6 -> x2, waiting for transfers between devices: 85.7 us -> 0.01 us  [the longest x1 0.01 us: local(): lax.all_to_all(outgoing, ('store', 'ctx'), split_axis=0, concat_axis=0, t...]
    pallas_call x0 -> x5, Pallas kernels: none -> 44.8 us  [the longest x1 32.9 us: local(): pl.pallas_call(place_kernel, out_shape=jax.ShapeDtypeStruct((rows, column...]
    ppermute x0 -> x6, waiting for transfers between devices: none -> 31.3 us  [shift(): lax.ppermute(piece, 'tensor', [(i, (i + by) % parts) for i in range(parts)])]
    dot_general x22 -> x0, matrix products: 22.1 us -> none  [the longest x4 8.7 us: block_step(): jnp.einsum('gjqk,gjqd->gkd', weights_half, grad_group, preferred_element_...]
    all_to_all x6 -> x2, starting transfers between devices: 54.6 us -> 33.8 us  [the longest x1 19 us: local(): lax.all_to_all(outgoing, ('store', 'ctx'), split_axis=0, concat_axis=0, t...]
    ppermute x0 -> x6, starting transfers between devices: none -> 20.1 us  [shift(): lax.ppermute(piece, 'tensor', [(i, (i + by) % parts) for i in range(parts)])]
    unnamed x28 -> x25, local copies, waits for them, and re-layouts: 10.7 us -> 3.94 us
    scatter x2 -> x0, local copies, waits for them, and re-layouts: 4.43 us -> none  [local(): jnp.zeros((2, shard_count, key_len, key_width), jnp.bfloat16).at[:, slot_of]]
  transfers between devices with their start and end apart: 6 -> 8, of which waited for: 6 -> 6; matrix products, arithmetic and copies ran while one was open for 11% -> 1% of each run, Pallas kernels for 0% -> 25%
where the time goes in v1:
time: 137 us
  starting transfers between devices  54 us (39%)
  Pallas kernels  44.8 us (33%)
  waiting for transfers between devices  31.3 us (23%)
  local copies, waits for them, and re-layouts  4.82 us (4%)
    pallas_call x1, Pallas kernels, local(): pl.pallas_call(place_kernel, out_shape=jax.ShapeDtypeStruct((rows, column...  32.9 us
    ppermute x6, waiting for transfers between devices, shift(): lax.ppermute(piece, 'tensor', [(i, (i + by) % parts) for i in range(parts)])  31.3 us
    ppermute x6, starting transfers between devices, shift(): lax.ppermute(piece, 'tensor', [(i, (i + by) % parts) for i in range(parts)])  20.1 us
    all_to_all x1, starting transfers between devices, local(): lax.all_to_all(outgoing, ('store', 'ctx'), split_axis=0, concat_axis=0, t...  19 us
    all_to_all x1, starting transfers between devices, local(): lax.all_to_all(outgoing_grads, ('store', 'ctx'), split_axis=0, concat_axi...  14.8 us
    pallas_call x1, Pallas kernels, local(): pl.pallas_call(main, out_shape=[jax.ShapeDtypeStruct((QBLK, width), BF16)...  6.23 us
    unnamed x25, local copies, waits for them, and re-layouts  3.94 us
  transfers between devices with their start and end apart: 8, of which 6 were waited for; matrix products, arithmetic and copies ran while one was open for 1% of the time, Pallas kernels for 25%

profile of v1, /device:TPU:1, one launch (start us, length us, event | category | flops | bytes accessed | tf_op | source)
XLA Modules:
  0.0 136.6 jit_solution(756856708144375371)
XLA Ops:
  0.6 0.8 fusion.3
  1.4 0.1 reduce_sum.14
  1.6 0.0 copy-start.4
  1.6 0.0 copy-start.5
  1.6 0.1 reduce_sum.18
  1.7 0.6 copy-done.4
  2.3 0.0 copy-done.5
  2.3 0.0 copy-start.2
  2.3 1.8 %send.1 = bf16[128,32,128]{2,1,0:T(8,128)(2,1)} custom-call(s32[128]{0:T(128)S(1)} %broadcast_add_fusion.pick_ref, bf16[4,16,128]{2,1,0:T(8,128)(2,1)S(1)} %copy-done.4, bf16[4,16,128]{2,1,0:T(8,128)(2,1)S(1)} %copy-done.5), custom_call_target="tpu_custom_call" | custom-call | tf_op jit(solution)/shard_map/send/pallas_call | solution.py:160
  4.1 0.0 copy-start
  4.1 0.0 copy-start.1
  4.1 19.0 %all-to-all-start = ((bf16[128,32,128]{2,1,0:T(8,128)(2,1)}), bf16[128,32,128]{2,1,0:T(8,128)(2,1)}, u32[]{:S(2)}, u32[]{:S(2)}) async-start(bf16[128,32,128]{2,1,0:T(8,128)(2,1)} %send.1), calls=%async_computation | async-start | bytes 2097152 | tf_op jit(solution)/shard_map/all_to_all | solution.py:168
  23.1 0.0 copy-done.2
  23.2 0.0 copy-done
  23.2 0.0 copy-done.1
  23.2 1.9 %prep.1 = (bf16[272,1024]{1,0:T(8,128)(2,1)S(1)}, bf16[272,1024]{1,0:T(8,128)(2,1)}, bf16[272,1024]{1,0:T(8,128)(2,1)}, bf16[272,1024]{1,0:T(8,128)(2,1)}) custom-call(s32[1]{0:T(128)} %bitcast.place_ref, bf16[128,4096]{1,0:T(8,128)(2,1)S(1)} %copy-done, bf16[128,4096]{1,0:T(8,128)(2,1)S(1)} %copy-done.1, bf16[128,4096]{1,0:T(8,128)(2,1)S(1)} %copy-done.2), custom_call_target="tpu_custom_call" | custom-call | flops 1048576 | bytes 5242880 | tf_op jit(solution)/shard_map/prep/pallas_call | solution.py:171
  25.0 0.0 copy-start.6
  25.1 0.8 copy-done.6
  25.9 3.1 %collective-permute-start = (bf16[272,1024]{1,0:T(8,128)(2,1)}, bf16[272,1024]{1,0:T(8,128)(2,1)S(1)}, u32[]{:S(2)}, u32[]{:S(2)}) collective-permute-start(bf16[272,1024]{1,0:T(8,128)(2,1)} %get-tuple-element.15), channel_id=1, source_target_pairs={{0,1},{1,2},{2,3},{3,0},{4,5},{5,6},{6,7},{7,4},{8,9},{9,10},{10,1... | collective-permute-start | bytes 1671176 | tf_op jit(solution)/shard_map/ppermute | solution.py:185
  29.0 4.4 %collective-permute-start.1 = (bf16[272,1024]{1,0:T(8,128)(2,1)}, bf16[272,1024]{1,0:T(8,128)(2,1)S(1)}, u32[]{:S(2)}, u32[]{:S(2)}) collective-permute-start(bf16[272,1024]{1,0:T(8,128)(2,1)} %get-tuple-element.16), channel_id=1, source_target_pairs={{0,2},{1,3},{2,0},{3,1},{4,6},{5,7},{6,4},{7,5},{8,10},{9,11},{10,... | collective-permute-start | bytes 1671176 | tf_op jit(solution)/shard_map/ppermute | solution.py:185
  33.3 3.1 %collective-permute-start.2 = (bf16[272,1024]{1,0:T(8,128)(2,1)}, bf16[272,1024]{1,0:T(8,128)(2,1)S(1)}, u32[]{:S(2)}, u32[]{:S(2)}) collective-permute-start(bf16[272,1024]{1,0:T(8,128)(2,1)} %get-tuple-element.17), channel_id=1, source_target_pairs={{0,3},{1,0},{2,1},{3,2},{4,7},{5,4},{6,5},{7,6},{8,11},{9,8},{10,9... | collective-permute-start | bytes 1671176 | tf_op jit(solution)/shard_map/ppermute | solution.py:185
  36.4 0.8 constant_dynamic-slice_fusion
  37.2 0.0 copy-start.8
  37.2 0.1 copy.12.lists_ref
  37.3 5.2 %collective-permute-done.refs_2_ = bf16[272,1024]{1,0:T(8,128)(2,1)S(1)} collective-permute-done((bf16[272,1024]{1,0:T(8,128)(2,1)}, bf16[272,1024]{1,0:T(8,128)(2,1)S(1)}, u32[]{:S(2)}, u32[]{:S(2)}) %collective-permute-start) | collective-permute-done | bytes 557088 | tf_op jit(solution)/shard_map/ppermute | solution.py:185
  42.4 12.8 %collective-permute-done.1.refs_3_ = bf16[272,1024]{1,0:T(8,128)(2,1)S(1)} collective-permute-done((bf16[272,1024]{1,0:T(8,128)(2,1)}, bf16[272,1024]{1,0:T(8,128)(2,1)S(1)}, u32[]{:S(2)}, u32[]{:S(2)}) %collective-permute-start.1) | collective-permute-done | bytes 557088 | tf_op jit(solution)/shard_map/ppermute | solution.py:185
  55.2 2.0 %collective-permute-done.2.refs_4_ = bf16[272,1024]{1,0:T(8,128)(2,1)S(1)} collective-permute-done((bf16[272,1024]{1,0:T(8,128)(2,1)}, bf16[272,1024]{1,0:T(8,128)(2,1)S(1)}, u32[]{:S(2)}, u32[]{:S(2)}) %collective-permute-start.2) | collective-permute-done | bytes 557088 | tf_op jit(solution)/shard_map/ppermute | solution.py:185
  57.2 0.0 all-to-all-done.refs_0_
  57.2 0.0 copy-done.8
  57.2 0.0 copy-start.7
  57.2 1.1 copy-done.7
  58.3 6.2 %attention.1 = (bf16[128,1024]{1,0:T(8,128)(2,1)S(1)}, bf16[128,1024]{1,0:T(8,128)(2,1)S(1)}, bf16[128,1024]{1,0:T(8,128)(2,1)S(1)}, bf16[128,1024]{1,0:T(8,128)(2,1)S(1)}, bf16[128,32,128]{2,1,0:T(8,128)(2,1)}) custom-call(s32[1]{0:T(128)} %bitcast.place_ref, s32[4,16]{1,0:T(4,128)S(1)} %copy.12.lists_ref, s32[512]{0:T(512)S(1)} %copy-done.8, ...), custom_call_target="tpu_custom_call" | custom-call | flops 1342177280 | bytes 4194304 | tf_op jit(solution)/shard_map/attention/pallas_call | solution.py:195
  64.5 0.0 copy-start.3
  64.5 0.7 copy-done.3
  65.2 14.8 %all-to-all-start.1 = ((bf16[128,32,128]{2,1,0:T(8,128)(2,1)}), bf16[128,32,128]{2,1,0:T(8,128)(2,1)S(1)}, u32[]{:S(2)}, u32[]{:S(2)}) async-start(bf16[128,32,128]{2,1,0:T(8,128)(2,1)} %get-tuple-element.22), calls=%async_computation.1 | async-start | bytes 2097152 | tf_op jit(solution)/shard_map/all_to_all | solution.py:210
  80.0 4.3 %collective-permute-start.3 = (bf16[128,1024]{1,0:T(8,128)(2,1)S(1)}, bf16[128,1024]{1,0:T(8,128)(2,1)S(1)}, u32[]{:S(2)}, u32[]{:S(2)}) collective-permute-start(bf16[128,1024]{1,0:T(8,128)(2,1)S(1)} %get-tuple-element.19), channel_id=1, source_target_pairs={{0,3},{1,0},{2,1},{3,2},{4,7},{5,4},{6,5},{7,6},{8,11},{9,8},{10,9... | collective-permute-start | bytes 786440 | tf_op jit(solution)/shard_map/ppermute | solution.py:185
  84.3 3.4 %collective-permute-start.4 = (bf16[128,1024]{1,0:T(8,128)(2,1)S(1)}, bf16[128,1024]{1,0:T(8,128)(2,1)S(1)}, u32[]{:S(2)}, u32[]{:S(2)}) collective-permute-start(bf16[128,1024]{1,0:T(8,128)(2,1)S(1)} %get-tuple-element.20), channel_id=1, source_target_pairs={{0,2},{1,3},{2,0},{3,1},{4,6},{5,7},{6,4},{7,5},{8,10},{9,11},{10,... | collective-permute-start | bytes 786440 | tf_op jit(solution)/shard_map/ppermute | solution.py:185
  87.7 1.9 %collective-permute-start.5 = (bf16[128,1024]{1,0:T(8,128)(2,1)S(1)}, bf16[128,1024]{1,0:T(8,128)(2,1)S(1)}, u32[]{:S(2)}, u32[]{:S(2)}) collective-permute-start(bf16[128,1024]{1,0:T(8,128)(2,1)S(1)} %get-tuple-element.21), channel_id=1, source_target_pairs={{0,1},{1,2},{2,3},{3,0},{4,5},{5,6},{6,7},{7,4},{8,9},{9,10},{10,1... | collective-permute-start | bytes 786440 | tf_op jit(solution)/shard_map/ppermute | solution.py:185
  89.7 0.1 collective-permute-done.3.rest_1_
  89.8 0.0 copy-start.9
  89.8 4.5 %collective-permute-done.4.rest_2_ = bf16[128,1024]{1,0:T(8,128)(2,1)S(1)} collective-permute-done((bf16[128,1024]{1,0:T(8,128)(2,1)S(1)}, bf16[128,1024]{1,0:T(8,128)(2,1)S(1)}, u32[]{:S(2)}, u32[]{:S(2)}) %collective-permute-start.4) | collective-permute-done | bytes 262176 | tf_op jit(solution)/shard_map/ppermute | solution.py:185
  94.3 0.0 copy-start.10
  94.3 6.7 %collective-permute-done.5.rest_3_ = bf16[128,1024]{1,0:T(8,128)(2,1)S(1)} collective-permute-done((bf16[128,1024]{1,0:T(8,128)(2,1)S(1)}, bf16[128,1024]{1,0:T(8,128)(2,1)S(1)}, u32[]{:S(2)}, u32[]{:S(2)}) %collective-permute-start.5) | collective-permute-done | bytes 262176 | tf_op jit(solution)/shard_map/ppermute | solution.py:185
  101.0 0.0 copy-start.11
  101.0 0.0 copy-done.9
  101.0 0.0 copy-done.10
  101.0 0.7 copy-done.11
  101.7 32.9 %place.1 = bf16[128,4096]{1,0:T(8,128)(2,1)} custom-call(s32[1]{0:T(128)} %bitcast.place_ref, bf16[128,1024]{1,0:T(8,128)(2,1)} %copy-done.3, bf16[128,1024]{1,0:T(8,128)(2,1)} %copy-done.9, bf16[128,1024]{1,0:T(8,128)(2,1)} %copy-done.10, bf16[128,1024]{1,0:T(8,128)(2,1)} %copy-done.11), custom_call_target="tpu_custom_call" | custom-call | bytes 2097152 | tf_op jit(solution)/shard_map/place/pallas_call | solution.py:212
  134.6 0.0 all-to-all-done.1.terms_ref
  134.6 2.0 %sum.1 = (bf16[4,16,128]{2,1,0:T(8,128)(2,1)}, bf16[4,16,128]{2,1,0:T(8,128)(2,1)}) custom-call(s32[128]{0:T(128)S(1)} %broadcast_add_fusion.pick_ref, bf16[128,32,128]{2,1,0:T(8,128)(2,1)S(1)} %all-to-all-done.1.terms_ref), custom_call_target="tpu_custom_call" | custom-call | tf_op jit(solution)/shard_map/sum/pallas_call | solution.py:222
  (1 shorter events, 0.0 us)
Async XLA Ops:
  1.6 0.7 copy-start.4
  1.6 0.7 copy-start.5
  2.3 20.9 %copy-start.2 = (bf16[128,4096]{1,0:T(8,128)(2,1)S(1)}, bf16[128,4096]{1,0:T(8,128)(2,1)}, u32[]{:S(2)}) copy-start(bf16[128,4096]{1,0:T(8,128)(2,1)} %o_ref.1) | copy-start | bytes 3145732
  4.1 19.0 %copy-start = (bf16[128,4096]{1,0:T(8,128)(2,1)S(1)}, bf16[128,4096]{1,0:T(8,128)(2,1)}, u32[]{:S(2)}) copy-start(bf16[128,4096]{1,0:T(8,128)(2,1)} %q_ref.1) | copy-start | bytes 3145732
  4.1 19.0 %copy-start.1 = (bf16[128,4096]{1,0:T(8,128)(2,1)S(1)}, bf16[128,4096]{1,0:T(8,128)(2,1)}, u32[]{:S(2)}) copy-start(bf16[128,4096]{1,0:T(8,128)(2,1)} %g_ref.1) | copy-start | bytes 3145732
  4.1 53.1 %all-to-all-start = ((bf16[128,32,128]{2,1,0:T(8,128)(2,1)}), bf16[128,32,128]{2,1,0:T(8,128)(2,1)}, u32[]{:S(2)}, u32[]{:S(2)}) async-start(bf16[128,32,128]{2,1,0:T(8,128)(2,1)} %send.1), calls=%async_computation | async-start | bytes 2097152 | tf_op jit(solution)/shard_map/all_to_all | solution.py:168
  25.0 0.8 copy-start.6
  25.9 16.6 %collective-permute-start = (bf16[272,1024]{1,0:T(8,128)(2,1)}, bf16[272,1024]{1,0:T(8,128)(2,1)S(1)}, u32[]{:S(2)}, u32[]{:S(2)}) collective-permute-start(bf16[272,1024]{1,0:T(8,128)(2,1)} %get-tuple-element.15), channel_id=1, source_target_pairs={{0,1},{1,2},{2,3},{3,0},{4,5},{5,6},{6,7},{7,4},{8,9},{9,10},{10,1... | collective-permute-start | bytes 1671176 | tf_op jit(solution)/shard_map/ppermute | solution.py:185
  29.0 26.3 %collective-permute-start.1 = (bf16[272,1024]{1,0:T(8,128)(2,1)}, bf16[272,1024]{1,0:T(8,128)(2,1)S(1)}, u32[]{:S(2)}, u32[]{:S(2)}) collective-permute-start(bf16[272,1024]{1,0:T(8,128)(2,1)} %get-tuple-element.16), channel_id=1, source_target_pairs={{0,2},{1,3},{2,0},{3,1},{4,6},{5,7},{6,4},{7,5},{8,10},{9,11},{10,... | collective-permute-start | bytes 1671176 | tf_op jit(solution)/shard_map/ppermute | solution.py:185
  33.3 23.9 %collective-permute-start.2 = (bf16[272,1024]{1,0:T(8,128)(2,1)}, bf16[272,1024]{1,0:T(8,128)(2,1)S(1)}, u32[]{:S(2)}, u32[]{:S(2)}) collective-permute-start(bf16[272,1024]{1,0:T(8,128)(2,1)} %get-tuple-element.17), channel_id=1, source_target_pairs={{0,3},{1,0},{2,1},{3,2},{4,7},{5,4},{6,5},{7,6},{8,11},{9,8},{10,9... | collective-permute-start | bytes 1671176 | tf_op jit(solution)/shard_map/ppermute | solution.py:185
  37.2 20.0 %copy-start.8 = (s32[512]{0:T(512)S(1)}, s32[512]{0:T(512)}, u32[]{:S(2)}) copy-start(s32[512]{0:T(512)} %lengths_ref.1) | copy-start | bytes 6148
  57.2 1.1 copy-start.7
  64.5 0.7 copy-start.3
  65.2 69.4 %all-to-all-start.1 = ((bf16[128,32,128]{2,1,0:T(8,128)(2,1)}), bf16[128,32,128]{2,1,0:T(8,128)(2,1)S(1)}, u32[]{:S(2)}, u32[]{:S(2)}) async-start(bf16[128,32,128]{2,1,0:T(8,128)(2,1)} %get-tuple-element.22), calls=%async_computation.1 | async-start | bytes 2097152 | tf_op jit(solution)/shard_map/all_to_all | solution.py:210
  80.0 9.8 %collective-permute-start.3 = (bf16[128,1024]{1,0:T(8,128)(2,1)S(1)}, bf16[128,1024]{1,0:T(8,128)(2,1)S(1)}, u32[]{:S(2)}, u32[]{:S(2)}) collective-permute-start(bf16[128,1024]{1,0:T(8,128)(2,1)S(1)} %get-tuple-element.19), channel_id=1, source_target_pairs={{0,3},{1,0},{2,1},{3,2},{4,7},{5,4},{6,5},{7,6},{8,11},{9,8},{10,9... | collective-permute-start | bytes 786440 | tf_op jit(solution)/shard_map/ppermute | solution.py:185
  84.3 10.0 %collective-permute-start.4 = (bf16[128,1024]{1,0:T(8,128)(2,1)S(1)}, bf16[128,1024]{1,0:T(8,128)(2,1)S(1)}, u32[]{:S(2)}, u32[]{:S(2)}) collective-permute-start(bf16[128,1024]{1,0:T(8,128)(2,1)S(1)} %get-tuple-element.20), channel_id=1, source_target_pairs={{0,2},{1,3},{2,0},{3,1},{4,6},{5,7},{6,4},{7,5},{8,10},{9,11},{10,... | collective-permute-start | bytes 786440 | tf_op jit(solution)/shard_map/ppermute | solution.py:185
  87.7 13.2 %collective-permute-start.5 = (bf16[128,1024]{1,0:T(8,128)(2,1)S(1)}, bf16[128,1024]{1,0:T(8,128)(2,1)S(1)}, u32[]{:S(2)}, u32[]{:S(2)}) collective-permute-start(bf16[128,1024]{1,0:T(8,128)(2,1)S(1)} %get-tuple-element.21), channel_id=1, source_target_pairs={{0,1},{1,2},{2,3},{3,0},{4,5},{5,6},{6,7},{7,4},{8,9},{9,10},{10,1... | collective-permute-start | bytes 786440 | tf_op jit(solution)/shard_map/ppermute | solution.py:185
  89.8 11.2 %copy-start.9 = (bf16[128,1024]{1,0:T(8,128)(2,1)}, bf16[128,1024]{1,0:T(8,128)(2,1)S(1)}, u32[]{:S(2)}) copy-start(bf16[128,1024]{1,0:T(8,128)(2,1)S(1)} %collective-permute-done.3.rest_1_) | copy-start | bytes 786436
  94.3 6.7 %copy-start.10 = (bf16[128,1024]{1,0:T(8,128)(2,1)}, bf16[128,1024]{1,0:T(8,128)(2,1)S(1)}, u32[]{:S(2)}) copy-start(bf16[128,1024]{1,0:T(8,128)(2,1)S(1)} %collective-permute-done.4.rest_2_) | copy-start | bytes 786436
  101.0 0.7 copy-start.11

commit v2 on v1

--- a/solution.py
+++ b/solution.py
@@ -3,6 +3,7 @@
 from jax import lax
 from jax.experimental import pallas as pl
 from jax.experimental.pallas import tpu as pltpu
+from jax.sharding import Mesh
 from jax.sharding import PartitionSpec as P
 
 DH = 128
@@ -12,7 +13,24 @@
 MASKED = -1e30
 NT = (((1,), (1,)), ((), ()))
 TN = (((0,), (0,)), ((), ()))
-VMEM_LIMIT = 48 * 1024 * 1024
+VMEM_LIMIT = 24 * 1024 * 1024
+
+
+SHARD_AXES = ("y2", "y1", "y0", "z2", "z1", "z0", "core")
+EXCHANGE_AXES = ("core", "y0", "z0", "y1", "z1", "y2", "z2")
+
+
+def slot_of(shard):
+    bits = len(SHARD_AXES)
+    slot = 0
+    for i, name in enumerate(EXCHANGE_AXES):
+        bit = (shard >> (bits - 1 - SHARD_AXES.index(name))) & 1
+        slot = slot | (bit << (bits - 1 - i))
+    return slot
+
+
+def exchange(pieces):
+    return lax.all_to_all(pieces, EXCHANGE_AXES, split_axis=0, concat_axis=0, tiled=True)
 
 
 def vmem():
@@ -32,8 +50,9 @@
 
     def body(n, carry):
         k = jnp.maximum(pick_ref[n], 0)
-        out_ref[n, 0:plen, :] = keys_ref[k]
-        out_ref[n, plen : 2 * plen, :] = values_ref[k]
+        slot = slot_of(n)
+        out_ref[slot, 0:plen, :] = keys_ref[k]
+        out_ref[slot, plen : 2 * plen, :] = values_ref[k]
         return carry
 
     lax.fori_loop(0, out_ref.shape[0], body, 0, unroll=8)
@@ -79,14 +98,14 @@
     slot_row = lax.broadcasted_iota(jnp.int32, (plen, DH), 0)
     for j, (message_ref, dq_ref) in enumerate(zip(message_refs, dq_refs)):
         block = lax.rem(place_ref[0] + parts - j, parts)
-        owners = []
+        slots = []
         for p in range(list_len):
             passage = lists_ref[block, p]
-            owner = passage // pass_dev
-            owners.append(owner)
+            slot = slot_of(passage // pass_dev)
+            slots.append(slot)
             rows = slice(p * plen, (p + 1) * plen)
-            k_ref[rows, :] = incoming_ref[owner, 0:plen, :]
-            v_ref[rows, :] = incoming_ref[owner, plen : 2 * plen, :]
+            k_ref[rows, :] = incoming_ref[slot, 0:plen, :]
+            v_ref[rows, :] = incoming_ref[slot, plen : 2 * plen, :]
             bias_ref[rows, :] = jnp.where(slot_row < lengths_ref[passage], 0.0, MASKED)
         keys = k_ref[...]
         values = v_ref[...]
@@ -104,28 +123,22 @@
         score_grads = (weights * (weight_grads - delta)).astype(BF16)
         value_term = jnp.dot(weights.astype(BF16), grads, preferred_element_type=F32).astype(BF16)
         key_term = (jnp.dot(score_grads, queries, preferred_element_type=F32) * scale).astype(BF16)
-        for p, owner in enumerate(owners):
+        for p, slot in enumerate(slots):
             rows = slice(p * plen, (p + 1) * plen)
-            out_ref[owner, 0:plen, :] = key_term[rows]
-            out_ref[owner, plen : 2 * plen, :] = value_term[rows]
+            out_ref[slot, 0:plen, :] = key_term[rows]
+            out_ref[slot, plen : 2 * plen, :] = value_term[rows]
         query_part = lax.dot_general(keys, score_grads, TN, preferred_element_type=F32) * scale
         for c in heads:
             dq_ref[:, c] = query_part[:, c].T.astype(BF16)
 
 
 def place_kernel(place_ref, *rest):
-    *piece_refs, out_ref, sems = rest
+    *piece_refs, out_ref = rest
     parts = len(piece_refs)
     width = out_ref.shape[1] // parts
-    copies = []
     for j, piece_ref in enumerate(piece_refs):
         to = lax.rem(place_ref[0] + j, parts)
-        cols = pl.ds(pl.multiple_of(to * width, width), width)
-        copies.append(pltpu.make_async_copy(piece_ref, out_ref.at[:, cols], sems.at[j]))
-    for copy in copies:
-        copy.start()
-    for copy in copies:
-        copy.wait()
+        out_ref[:, pl.ds(pl.multiple_of(to * width, width), width)] = piece_ref[...]
 
 
 def sum_kernel(pick_ref, terms_ref, keys_ref, values_ref):
@@ -133,7 +146,7 @@
 
     def body(n, sums):
         k = pick_ref[n]
-        term = terms_ref[n].astype(F32)
+        term = terms_ref[slot_of(n)].astype(F32)
         return tuple(s + jnp.where(k == i, term, 0.0) for i, s in enumerate(sums))
 
     zero = jnp.zeros((2 * plen, DH), F32)
@@ -144,9 +157,9 @@
 
 
 def local(queries, grad_out, attn_out, passage_keys, passage_values, block_lists, passage_lengths):
-    shards = lax.axis_size("store") * lax.axis_size("ctx")
+    shards = lax.axis_size(SHARD_AXES)
     parts = lax.axis_size("tensor")
-    my_shard = lax.axis_index("store") * lax.axis_size("ctx") + lax.axis_index("ctx")
+    my_shard = lax.axis_index(SHARD_AXES)
     place = lax.axis_index("tensor").astype(jnp.int32).reshape(1)
     pass_dev, plen, _ = passage_keys.shape
     rows, columns = queries.shape
@@ -165,7 +178,7 @@
         compiler_params=params(),
         name="send",
     )(pick, passage_keys, passage_values)
-    incoming = lax.all_to_all(outgoing, ("store", "ctx"), split_axis=0, concat_axis=0, tiled=True)
+    incoming = exchange(outgoing)
 
     message = jax.ShapeDtypeStruct((2 * QBLK + 2 * (width // DH), width), BF16)
     messages = pl.pallas_call(
@@ -207,14 +220,14 @@
         name="attention",
     )(place, own_lists, passage_lengths, incoming, *messages)
 
-    returned = lax.all_to_all(outgoing_grads, ("store", "ctx"), split_axis=0, concat_axis=0, tiled=True)
+    returned = exchange(outgoing_grads)
     query_parts = [shift(piece, (parts - j) % parts) for j, piece in enumerate(query_parts)]
     query_grad = pl.pallas_call(
         place_kernel,
         out_shape=jax.ShapeDtypeStruct((rows, columns), BF16),
-        in_specs=[smem()] + [pl.BlockSpec(memory_space=pl.ANY)] * parts,
-        out_specs=pl.BlockSpec(memory_space=pl.ANY),
-        scratch_shapes=[pltpu.SemaphoreType.DMA((parts,))],
+        in_specs=[smem()] + [vmem()] * parts,
+        out_specs=vmem(),
+        compiler_params=params(),
         cost_estimate=pl.CostEstimate(flops=0, bytes_accessed=4 * rows * columns, transcendentals=0),
         name="place",
     )(place, *query_parts)
@@ -231,11 +244,13 @@
 
 
 def solution(mesh):
-    tokens = P(("store", "ctx", "tensor"), None)
-    passages = P(("store", "ctx"), None, "tensor")
+    parts = mesh.shape["tensor"]
+    fine = Mesh(mesh.devices.reshape((2,) * len(SHARD_AXES) + (parts,)), SHARD_AXES + ("tensor",))
+    tokens = P(SHARD_AXES + ("tensor",), None)
+    passages = P(SHARD_AXES, None, "tensor")
     return jax.shard_map(
         local,
-        mesh=mesh,
+        mesh=fine,
         in_specs=(tokens, tokens, tokens, passages, passages, P(), P()),
         out_specs=(tokens, passages, passages),
         check_vma=False,

time: 137 us -> 116 us (0.85)
  Pallas kernels: 44.8 us -> 14.8 us
  waiting for transfers between devices: 31.3 us -> 41.8 us
    pallas_call x1, Pallas kernels: 32.9 us -> 1.05 us  [local(): pl.pallas_call(place_kernel, out_shape=jax.ShapeDtypeStruct((rows, column...]
    all_to_all x2, waiting for transfers between devices: 0.01 us -> 9.4 us  [exchange(): lax.all_to_all(pieces, EXCHANGE_AXES, split_axis=0, concat_axis=0, tiled=...]
    unnamed x25 -> x19, local copies, waits for them, and re-layouts: 3.94 us -> 3.29 us
  transfers between devices with their start and end apart: 8 -> 8, of which waited for: 6 -> 7; matrix products, arithmetic and copies ran while one was open for 1% -> 0% of each run, Pallas kernels for 25% -> 3%
where the time goes in v2:
time: 116 us; the launch traced here: 115 us
  starting transfers between devices  54.2 us (47%)
  waiting for transfers between devices  41.8 us (36%)
  Pallas kernels  14.8 us (13%)
  local copies, waits for them, and re-layouts  3.47 us (3%)
    all_to_all x2, starting transfers between devices, exchange(): lax.all_to_all(pieces, EXCHANGE_AXES, split_axis=0, concat_axis=0, tiled=...  34.1 us
    ppermute x6, waiting for transfers between devices, shift(): lax.ppermute(piece, 'tensor', [(i, (i + by) % parts) for i in range(parts)])  32.4 us
    ppermute x6, starting transfers between devices, shift(): lax.ppermute(piece, 'tensor', [(i, (i + by) % parts) for i in range(parts)])  20.1 us
    all_to_all x2, waiting for transfers between devices, exchange(): lax.all_to_all(pieces, EXCHANGE_AXES, split_axis=0, concat_axis=0, tiled=...  9.4 us
    pallas_call x1, Pallas kernels, local(): pl.pallas_call(main, out_shape=[jax.ShapeDtypeStruct((QBLK, width), BF16)...  6.45 us
    unnamed x19, local copies, waits for them, and re-layouts  3.29 us
    pallas_call x1, Pallas kernels, local(): pl.pallas_call(send_kernel, out_shape=all_shape, in_specs=[smem(), vmem()...  2.75 us
    pallas_call x1, Pallas kernels, local(): pl.pallas_call(sum_kernel, out_shape=[grad_shape, grad_shape], in_specs=[...  2.72 us
  transfers between devices with their start and end apart: 8, of which 7 were waited for; matrix products, arithmetic and copies ran while one was open for 0% of the time, Pallas kernels for 3%

profile of v2, /device:TPU:1, one launch (start us, length us, event | category | flops | bytes accessed | tf_op | source)
XLA Modules:
  0.0 115.3 jit_solution(5798252119151495396)
XLA Ops:
  0.6 0.0 copy-start.8
  0.7 0.7 copy-done.8
  1.4 0.1 fusion.3
  1.4 0.1 reduce_sum.14
  1.6 0.0 copy-start.3
  1.6 0.0 copy-start.4
  1.6 0.1 reduce_sum.18
  1.7 0.6 copy-done.3
  2.3 0.0 copy-done.4
  2.3 0.0 copy-start.2
  2.3 2.7 %send.1 = bf16[128,32,128]{2,1,0:T(8,128)(2,1)} custom-call(s32[128]{0:T(128)S(1)} %broadcast_add_fusion.pick_ref, bf16[4,16,128]{2,1,0:T(8,128)(2,1)S(1)} %copy-done.3, bf16[4,16,128]{2,1,0:T(8,128)(2,1)S(1)} %copy-done.4), custom_call_target="tpu_custom_call" | custom-call | tf_op jit(solution)/shard_map/send/pallas_call | solution.py:173
  5.0 0.0 copy-start
  5.0 0.0 copy-start.1
  5.0 19.3 %all-to-all-start = ((bf16[128,32,128]{2,1,0:T(8,128)(2,1)}), bf16[128,32,128]{2,1,0:T(8,128)(2,1)}, u32[]{:S(2)}, u32[]{:S(2)}) async-start(bf16[128,32,128]{2,1,0:T(8,128)(2,1)} %send.1), calls=%async_computation | async-start | bytes 2097152 | tf_op jit(solution)/shard_map/all_to_all | solution.py:33
  24.4 0.0 copy-done.2
  24.4 0.0 copy-done
  24.4 0.0 copy-done.1
  24.4 1.9 %prep.1 = (bf16[272,1024]{1,0:T(8,128)(2,1)S(1)}, bf16[272,1024]{1,0:T(8,128)(2,1)}, bf16[272,1024]{1,0:T(8,128)(2,1)}, bf16[272,1024]{1,0:T(8,128)(2,1)}) custom-call(s32[1]{0:T(128)} %bitcast.place_ref, bf16[128,4096]{1,0:T(8,128)(2,1)S(1)} %copy-done, bf16[128,4096]{1,0:T(8,128)(2,1)S(1)} %copy-done.1, bf16[128,4096]{1,0:T(8,128)(2,1)S(1)} %copy-done.2), custom_call_target="tpu_custom_call" | custom-call | flops 1048576 | bytes 5242880 | tf_op jit(solution)/shard_map/prep/pallas_call | solution.py:184
  26.3 0.0 copy-start.5
  26.3 0.8 copy-done.5
  27.1 3.1 %collective-permute-start = (bf16[272,1024]{1,0:T(8,128)(2,1)}, bf16[272,1024]{1,0:T(8,128)(2,1)S(1)}, u32[]{:S(2)}, u32[]{:S(2)}) collective-permute-start(bf16[272,1024]{1,0:T(8,128)(2,1)} %get-tuple-element.15), channel_id=1, source_target_pairs={{0,1},{1,2},{2,3},{3,0},{4,5},{5,6},{6,7},{7,4},{8,9},{9,10},{10,1... | collective-permute-start | bytes 1671176 | tf_op jit(solution)/shard_map/ppermute | solution.py:198
  30.2 4.4 %collective-permute-start.1 = (bf16[272,1024]{1,0:T(8,128)(2,1)}, bf16[272,1024]{1,0:T(8,128)(2,1)S(1)}, u32[]{:S(2)}, u32[]{:S(2)}) collective-permute-start(bf16[272,1024]{1,0:T(8,128)(2,1)} %get-tuple-element.16), channel_id=1, source_target_pairs={{0,2},{1,3},{2,0},{3,1},{4,6},{5,7},{6,4},{7,5},{8,10},{9,11},{10,... | collective-permute-start | bytes 1671176 | tf_op jit(solution)/shard_map/ppermute | solution.py:198
  34.6 3.1 %collective-permute-start.2 = (bf16[272,1024]{1,0:T(8,128)(2,1)}, bf16[272,1024]{1,0:T(8,128)(2,1)S(1)}, u32[]{:S(2)}, u32[]{:S(2)}) collective-permute-start(bf16[272,1024]{1,0:T(8,128)(2,1)} %get-tuple-element.17), channel_id=1, source_target_pairs={{0,3},{1,0},{2,1},{3,2},{4,7},{5,4},{6,5},{7,6},{8,11},{9,8},{10,9... | collective-permute-start | bytes 1671176 | tf_op jit(solution)/shard_map/ppermute | solution.py:198
  37.7 0.1 constant_dynamic-slice_fusion
  37.7 0.0 copy-start.7
  37.7 0.1 copy.12.lists_ref
  37.8 6.2 %collective-permute-done.refs_2_ = bf16[272,1024]{1,0:T(8,128)(2,1)S(1)} collective-permute-done((bf16[272,1024]{1,0:T(8,128)(2,1)}, bf16[272,1024]{1,0:T(8,128)(2,1)S(1)}, u32[]{:S(2)}, u32[]{:S(2)}) %collective-permute-start) | collective-permute-done | bytes 557088 | tf_op jit(solution)/shard_map/ppermute | solution.py:198
  44.0 12.8 %collective-permute-done.1.refs_3_ = bf16[272,1024]{1,0:T(8,128)(2,1)S(1)} collective-permute-done((bf16[272,1024]{1,0:T(8,128)(2,1)}, bf16[272,1024]{1,0:T(8,128)(2,1)S(1)}, u32[]{:S(2)}, u32[]{:S(2)}) %collective-permute-start.1) | collective-permute-done | bytes 557088 | tf_op jit(solution)/shard_map/ppermute | solution.py:198
  56.9 1.6 %collective-permute-done.2.refs_4_ = bf16[272,1024]{1,0:T(8,128)(2,1)S(1)} collective-permute-done((bf16[272,1024]{1,0:T(8,128)(2,1)}, bf16[272,1024]{1,0:T(8,128)(2,1)S(1)}, u32[]{:S(2)}, u32[]{:S(2)}) %collective-permute-start.2) | collective-permute-done | bytes 557088 | tf_op jit(solution)/shard_map/ppermute | solution.py:198
  58.5 0.0 all-to-all-done.refs_0_
  58.5 0.0 copy-done.7
  58.5 0.0 copy-start.6
  58.5 1.1 copy-done.6
  59.5 6.5 %attention.1 = (bf16[128,1024]{1,0:T(8,128)(2,1)S(1)}, bf16[128,1024]{1,0:T(8,128)(2,1)S(1)}, bf16[128,1024]{1,0:T(8,128)(2,1)S(1)}, bf16[128,1024]{1,0:T(8,128)(2,1)S(1)}, bf16[128,32,128]{2,1,0:T(8,128)(2,1)}) custom-call(s32[1]{0:T(128)} %bitcast.place_ref, s32[4,16]{1,0:T(4,128)S(1)} %copy.12.lists_ref, s32[512]{0:T(512)S(1)} %copy-done.7, ...), custom_call_target="tpu_custom_call" | custom-call | flops 1342177280 | bytes 4194304 | tf_op jit(solution)/shard_map/attention/pallas_call | solution.py:208
  66.0 14.8 %all-to-all-start.1 = ((bf16[128,32,128]{2,1,0:T(8,128)(2,1)}), bf16[128,32,128]{2,1,0:T(8,128)(2,1)S(1)}, u32[]{:S(2)}, u32[]{:S(2)}) async-start(bf16[128,32,128]{2,1,0:T(8,128)(2,1)} %get-tuple-element.22), calls=%async_computation.1 | async-start | bytes 2097152 | tf_op jit(solution)/shard_map/all_to_all | solution.py:33
  80.7 4.3 %collective-permute-start.3 = (bf16[128,1024]{1,0:T(8,128)(2,1)S(1)}, bf16[128,1024]{1,0:T(8,128)(2,1)S(1)}, u32[]{:S(2)}, u32[]{:S(2)}) collective-permute-start(bf16[128,1024]{1,0:T(8,128)(2,1)S(1)} %get-tuple-element.19), channel_id=1, source_target_pairs={{0,3},{1,0},{2,1},{3,2},{4,7},{5,4},{6,5},{7,6},{8,11},{9,8},{10,9... | collective-permute-start | bytes 786440 | tf_op jit(solution)/shard_map/ppermute | solution.py:198
  85.0 3.4 %collective-permute-start.4 = (bf16[128,1024]{1,0:T(8,128)(2,1)S(1)}, bf16[128,1024]{1,0:T(8,128)(2,1)S(1)}, u32[]{:S(2)}, u32[]{:S(2)}) collective-permute-start(bf16[128,1024]{1,0:T(8,128)(2,1)S(1)} %get-tuple-element.20), channel_id=1, source_target_pairs={{0,2},{1,3},{2,0},{3,1},{4,6},{5,7},{6,4},{7,5},{8,10},{9,11},{10,... | collective-permute-start | bytes 786440 | tf_op jit(solution)/shard_map/ppermute | solution.py:198
  88.4 1.9 %collective-permute-start.5 = (bf16[128,1024]{1,0:T(8,128)(2,1)S(1)}, bf16[128,1024]{1,0:T(8,128)(2,1)S(1)}, u32[]{:S(2)}, u32[]{:S(2)}) collective-permute-start(bf16[128,1024]{1,0:T(8,128)(2,1)S(1)} %get-tuple-element.21), channel_id=1, source_target_pairs={{0,1},{1,2},{2,3},{3,0},{4,5},{5,6},{6,7},{7,4},{8,9},{9,10},{10,1... | collective-permute-start | bytes 786440 | tf_op jit(solution)/shard_map/ppermute | solution.py:198
  90.4 0.5 collective-permute-done.3.rest_1_
  90.9 4.5 %collective-permute-done.4.rest_2_ = bf16[128,1024]{1,0:T(8,128)(2,1)S(1)} collective-permute-done((bf16[128,1024]{1,0:T(8,128)(2,1)S(1)}, bf16[128,1024]{1,0:T(8,128)(2,1)S(1)}, u32[]{:S(2)}, u32[]{:S(2)}) %collective-permute-start.4) | collective-permute-done | bytes 262176 | tf_op jit(solution)/shard_map/ppermute | solution.py:198
  95.4 6.7 %collective-permute-done.5.rest_3_ = bf16[128,1024]{1,0:T(8,128)(2,1)S(1)} collective-permute-done((bf16[128,1024]{1,0:T(8,128)(2,1)S(1)}, bf16[128,1024]{1,0:T(8,128)(2,1)S(1)}, u32[]{:S(2)}, u32[]{:S(2)}) %collective-permute-start.5) | collective-permute-done | bytes 262176 | tf_op jit(solution)/shard_map/ppermute | solution.py:198
  102.1 1.0 place.1
  103.2 9.4 %all-to-all-done.1.terms_ref = bf16[128,32,128]{2,1,0:T(8,128)(2,1)S(1)} async-done(((bf16[128,32,128]{2,1,0:T(8,128)(2,1)}), bf16[128,32,128]{2,1,0:T(8,128)(2,1)S(1)}, u32[]{:S(2)}, u32[]{:S(2)}) %all-to-all-start.1) | async-done | bytes 1048608 | tf_op jit(solution)/shard_map/all_to_all | solution.py:33
  112.6 2.7 %sum.1 = (bf16[4,16,128]{2,1,0:T(8,128)(2,1)}, bf16[4,16,128]{2,1,0:T(8,128)(2,1)}) custom-call(s32[128]{0:T(128)S(1)} %broadcast_add_fusion.pick_ref, bf16[128,32,128]{2,1,0:T(8,128)(2,1)S(1)} %all-to-all-done.1.terms_ref), custom_call_target="tpu_custom_call" | custom-call | tf_op jit(solution)/shard_map/sum/pallas_call | solution.py:235
  (1 shorter events, 0.0 us)
Async XLA Ops:
  0.6 0.8 copy-start.8
  1.6 0.7 copy-start.3
  1.6 0.7 copy-start.4
  2.3 22.1 %copy-start.2 = (bf16[128,4096]{1,0:T(8,128)(2,1)S(1)}, bf16[128,4096]{1,0:T(8,128)(2,1)}, u32[]{:S(2)}) copy-start(bf16[128,4096]{1,0:T(8,128)(2,1)} %o_ref.1) | copy-start | bytes 3145732
  5.0 19.4 %copy-start = (bf16[128,4096]{1,0:T(8,128)(2,1)S(1)}, bf16[128,4096]{1,0:T(8,128)(2,1)}, u32[]{:S(2)}) copy-start(bf16[128,4096]{1,0:T(8,128)(2,1)} %q_ref.1) | copy-start | bytes 3145732
  5.0 19.4 %copy-start.1 = (bf16[128,4096]{1,0:T(8,128)(2,1)S(1)}, bf16[128,4096]{1,0:T(8,128)(2,1)}, u32[]{:S(2)}) copy-start(bf16[128,4096]{1,0:T(8,128)(2,1)} %g_ref.1) | copy-start | bytes 3145732
  5.0 53.4 %all-to-all-start = ((bf16[128,32,128]{2,1,0:T(8,128)(2,1)}), bf16[128,32,128]{2,1,0:T(8,128)(2,1)}, u32[]{:S(2)}, u32[]{:S(2)}) async-start(bf16[128,32,128]{2,1,0:T(8,128)(2,1)} %send.1), calls=%async_computation | async-start | bytes 2097152 | tf_op jit(solution)/shard_map/all_to_all | solution.py:33
  26.3 0.8 copy-start.5
  27.1 16.9 %collective-permute-start = (bf16[272,1024]{1,0:T(8,128)(2,1)}, bf16[272,1024]{1,0:T(8,128)(2,1)S(1)}, u32[]{:S(2)}, u32[]{:S(2)}) collective-permute-start(bf16[272,1024]{1,0:T(8,128)(2,1)} %get-tuple-element.15), channel_id=1, source_target_pairs={{0,1},{1,2},{2,3},{3,0},{4,5},{5,6},{6,7},{7,4},{8,9},{9,10},{10,1... | collective-permute-start | bytes 1671176 | tf_op jit(solution)/shard_map/ppermute | solution.py:198
  30.2 26.6 %collective-permute-start.1 = (bf16[272,1024]{1,0:T(8,128)(2,1)}, bf16[272,1024]{1,0:T(8,128)(2,1)S(1)}, u32[]{:S(2)}, u32[]{:S(2)}) collective-permute-start(bf16[272,1024]{1,0:T(8,128)(2,1)} %get-tuple-element.16), channel_id=1, source_target_pairs={{0,2},{1,3},{2,0},{3,1},{4,6},{5,7},{6,4},{7,5},{8,10},{9,11},{10,... | collective-permute-start | bytes 1671176 | tf_op jit(solution)/shard_map/ppermute | solution.py:198
  34.6 23.9 %collective-permute-start.2 = (bf16[272,1024]{1,0:T(8,128)(2,1)}, bf16[272,1024]{1,0:T(8,128)(2,1)S(1)}, u32[]{:S(2)}, u32[]{:S(2)}) collective-permute-start(bf16[272,1024]{1,0:T(8,128)(2,1)} %get-tuple-element.17), channel_id=1, source_target_pairs={{0,3},{1,0},{2,1},{3,2},{4,7},{5,4},{6,5},{7,6},{8,11},{9,8},{10,9... | collective-permute-start | bytes 1671176 | tf_op jit(solution)/shard_map/ppermute | solution.py:198
  37.7 20.7 %copy-start.7 = (s32[512]{0:T(512)S(1)}, s32[512]{0:T(512)}, u32[]{:S(2)}) copy-start(s32[512]{0:T(512)} %lengths_ref.1) | copy-start | bytes 6148
  58.5 1.1 copy-start.6
  66.0 46.6 %all-to-all-start.1 = ((bf16[128,32,128]{2,1,0:T(8,128)(2,1)}), bf16[128,32,128]{2,1,0:T(8,128)(2,1)S(1)}, u32[]{:S(2)}, u32[]{:S(2)}) async-start(bf16[128,32,128]{2,1,0:T(8,128)(2,1)} %get-tuple-element.22), calls=%async_computation.1 | async-start | bytes 2097152 | tf_op jit(solution)/shard_map/all_to_all | solution.py:33
  80.7 10.1 %collective-permute-start.3 = (bf16[128,1024]{1,0:T(8,128)(2,1)S(1)}, bf16[128,1024]{1,0:T(8,128)(2,1)S(1)}, u32[]{:S(2)}, u32[]{:S(2)}) collective-permute-start(bf16[128,1024]{1,0:T(8,128)(2,1)S(1)} %get-tuple-element.19), channel_id=1, source_target_pairs={{0,3},{1,0},{2,1},{3,2},{4,7},{5,4},{6,5},{7,6},{8,11},{9,8},{10,9... | collective-permute-start | bytes 786440 | tf_op jit(solution)/shard_map/ppermute | solution.py:198
  85.0 10.4 %collective-permute-start.4 = (bf16[128,1024]{1,0:T(8,128)(2,1)S(1)}, bf16[128,1024]{1,0:T(8,128)(2,1)S(1)}, u32[]{:S(2)}, u32[]{:S(2)}) collective-permute-start(bf16[128,1024]{1,0:T(8,128)(2,1)S(1)} %get-tuple-element.20), channel_id=1, source_target_pairs={{0,2},{1,3},{2,0},{3,1},{4,6},{5,7},{6,4},{7,5},{8,10},{9,11},{10,... | collective-permute-start | bytes 786440 | tf_op jit(solution)/shard_map/ppermute | solution.py:198
  88.4 13.7 %collective-permute-start.5 = (bf16[128,1024]{1,0:T(8,128)(2,1)S(1)}, bf16[128,1024]{1,0:T(8,128)(2,1)S(1)}, u32[]{:S(2)}, u32[]{:S(2)}) collective-permute-start(bf16[128,1024]{1,0:T(8,128)(2,1)S(1)} %get-tuple-element.21), channel_id=1, source_target_pairs={{0,1},{1,2},{2,3},{3,0},{4,5},{5,6},{6,7},{7,4},{8,9},{9,10},{10,1... | collective-permute-start | bytes 786440 | tf_op jit(solution)/shard_map/ppermute | solution.py:198

commit v3 on v2

v3 whole, which is shorter than its diff:
```python
import jax
import jax.numpy as jnp
from jax import lax
from jax.experimental import pallas as pl
from jax.experimental.pallas import tpu as pltpu
from jax.sharding import Mesh
from jax.sharding import PartitionSpec as P

DH = 128
QBLK = 128
BF16 = jnp.bfloat16
F32 = jnp.float32
MASKED = -1e30
NT = (((1,), (1,)), ((), ()))
TN = (((0,), (0,)), ((), ()))
SMALL_VMEM = 24 * 1024 * 1024
LARGE_VMEM = 60 * 1024 * 1024


SHARD_AXES = ("y2", "y1", "y0", "z2", "z1", "z0", "core")
EXCHANGE_AXES = ("core", "y0", "z0", "y1", "z1", "y2", "z2")


def slot_of(shard):
    bits = len(SHARD_AXES)
    slot = 0
    for i, name in enumerate(EXCHANGE_AXES):
        bit = (shard >> (bits - 1 - SHARD_AXES.index(name))) & 1
        slot = slot | (bit << (bits - 1 - i))
    return slot


def exchange(pieces):
    return lax.all_to_all(pieces, EXCHANGE_AXES, split_axis=0, concat_axis=0, tiled=True)


def vmem():
    return pl.BlockSpec(memory_space=pltpu.VMEM)


def hbm():
    return pl.BlockSpec(memory_space=pltpu.HBM)


def smem():
    return pl.BlockSpec(memory_space=pltpu.SMEM)


def params(limit=SMALL_VMEM):
    return pltpu.CompilerParams(vmem_limit_bytes=limit)


def send_kernel(base_ref, lists_ref, keys_ref, values_ref, out_ref, pick_ref, row_ref, scalar_ref, built_ref, sems):
    pass_dev, plen, _ = keys_ref.shape
    shards = out_ref.shape[0]
    blocks = lists_ref.shape[1] // shards
    here = lists_ref[...] - base_ref[0]
    here = jnp.where((here >= 0) & (here < pass_dev), here + 1, 0)
    row_ref[...] = jnp.sum(here, axis=0, keepdims=True)
    copy = pltpu.make_async_copy(row_ref, scalar_ref, sems.at[0])
    copy.start()
    copy.wait()
    for n in range(shards):
        k = scalar_ref[0, n * blocks]
        for b in range(1, blocks):
            k = k + scalar_ref[0, n * blocks + b]
        k = k - 1
        pick_ref[n] = k
        k = jnp.maximum(k, 0)
        slot = slot_of(n)
        built_ref[slot, 0:plen, :] = keys_ref[k]
        built_ref[slot, plen : 2 * plen, :] = values_ref[k]
    copy = pltpu.make_async_copy(built_ref, out_ref, sems.at[1])
    copy.start()
    copy.wait()


def prep_kernel(place_ref, q_ref, g_ref, o_ref, message_ref, o_piece, sems):
    width = message_ref.shape[1]
    share = width // DH
    cols = pl.ds(pl.multiple_of(place_ref[0] * width, width), width)
    copies = [
        pltpu.make_async_copy(g_ref.at[:, cols], message_ref.at[QBLK : 2 * QBLK, :], sems.at[0]),
        pltpu.make_async_copy(o_ref.at[:, cols], o_piece, sems.at[1]),
        pltpu.make_async_copy(q_ref.at[:, cols], message_ref.at[0:QBLK, :], sems.at[2]),
    ]
    for copy in copies:
        copy.start()
    copies[0].wait()
    copies[1].wait()
    lane = lax.broadcasted_iota(jnp.int32, (QBLK, DH), 1)
    delta = jnp.zeros((QBLK, DH), F32)
    for h in range(share):
        c = slice(h * DH, (h + 1) * DH)
        term = message_ref[QBLK : 2 * QBLK, c].astype(F32) * o_piece[:, c].astype(F32)
        delta = jnp.where(lane == h, jnp.sum(term, axis=1, keepdims=True), delta)
    delta = delta.T[:share]
    high = delta.astype(BF16).astype(F32)
    message_ref[2 * QBLK :, :] = jnp.zeros((2 * share, width), BF16)
    message_ref[2 * QBLK :, 0:DH] = jnp.concatenate([high, delta - high], axis=0).astype(BF16)
    copies[2].wait()


def main_kernel(place_ref, slots_ref, lists_ref, lengths_ref, incoming_ref, *rest):
    parts, list_len = lists_ref.shape
    message_refs = rest[:parts]
    dq_refs = rest[parts : 2 * parts]
    out_ref, messages_ref, kv_ref, terms_ref, bias_ref, kv_sems, message_sems, out_sems = rest[2 * parts :]
    plen = incoming_ref.shape[1] // 2
    keys_here = list_len * plen
    share = message_refs[0].shape[1] // DH
    scale = DH ** (-0.5)
    slot_row = lax.broadcasted_iota(jnp.int32, (plen, DH), 0)
    blocks = [lax.rem(place_ref[0] + parts - j, parts) for j in range(parts)]
    slots = [[slots_ref[block, p] for p in range(list_len)] for block in blocks]
    loads = []
    for j in range(parts):
        copies = [pltpu.make_async_copy(message_refs[j], messages_ref.at[j], message_sems.at[j])]
        for p, slot in enumerate(slots[j]):
            copies.append(pltpu.make_async_copy(incoming_ref.at[slot], kv_ref.at[j, p], kv_sems.at[j, p]))
        for copy in copies:
            copy.start()
        loads.append(copies)
    stores = []
    for j, dq_ref in enumerate(dq_refs):
        message_ref = messages_ref.at[j]
        for p in range(list_len):
            rows = slice(p * plen, (p + 1) * plen)
            bias_ref[rows, :] = jnp.where(slot_row < lengths_ref[lists_ref[blocks[j], p]], 0.0, MASKED)
        for copy in loads[j]:
            copy.wait()
        keys = kv_ref[j, :, 0:plen, :].reshape(keys_here, DH)
        values = kv_ref[j, :, plen : 2 * plen, :].reshape(keys_here, DH)
        heads = [slice(h * DH, (h + 1) * DH) for h in range(share)]
        queries = jnp.concatenate([message_ref[0:QBLK, c] for c in heads], axis=0)
        grads = jnp.concatenate([message_ref[QBLK : 2 * QBLK, c] for c in heads], axis=0)
        delta_parts = message_ref[2 * QBLK : 2 * QBLK + 2 * share, 0:DH].astype(F32)
        delta = delta_parts[:share] + delta_parts[share:]
        delta = jnp.concatenate([delta[h : h + 1] for h in range(share)], axis=1)
        bias = jnp.concatenate([bias_ref[...]] * share, axis=1)
        scores = lax.dot_general(keys, queries, NT, preferred_element_type=F32) * scale + bias
        weights = jnp.exp(scores - jnp.max(scores, axis=0, keepdims=True))
        weights = weights * (1.0 / jnp.sum(weights, axis=0, keepdims=True))
        weight_grads = lax.dot_general(values, grads, NT, preferred_element_type=F32)
        score_grads = (weights * (weight_grads - delta)).astype(BF16)
        value_term = jnp.dot(weights.astype(BF16), grads, preferred_element_type=F32).astype(BF16)
        key_term = (jnp.dot(score_grads, queries, preferred_element_type=F32) * scale).astype(BF16)
        terms_ref[j, :, 0:plen, :] = key_term.reshape(list_len, plen, DH)
        terms_ref[j, :, plen : 2 * plen, :] = value_term.reshape(list_len, plen, DH)
        for p, slot in enumerate(slots[j]):
            copy = pltpu.make_async_copy(terms_ref.at[j, p], out_ref.at[slot], out_sems.at[j, p])
            copy.start()
            stores.append(copy)
        query_part = lax.dot_general(keys, score_grads, TN, preferred_element_type=F32) * scale
        for c in heads:
            dq_ref[:, c] = query_part[:, c].T.astype(BF16)
    for copy in stores:
        copy.wait()


def place_kernel(place_ref, *rest):
    *piece_refs, out_ref = rest
    parts = len(piece_refs)
    width = out_ref.shape[1] // parts
    for j, piece_ref in enumerate(piece_refs):
        to = lax.rem(place_ref[0] + j, parts)
        out_ref[:, pl.ds(pl.multiple_of(to * width, width), width)] = piece_ref[...]


def sum_kernel(pick_ref, terms_ref, keys_ref, values_ref):
    pass_dev, plen, _ = keys_ref.shape
    sums = [jnp.zeros((2 * plen, DH), F32)] * pass_dev
    for n in range(terms_ref.shape[0]):
        k = pick_ref[n]
        term = terms_ref[slot_of(n)].astype(F32)
        sums = [s + jnp.where(k == i, term, 0.0) for i, s in enumerate(sums)]
    for i, s in enumerate(sums):
        keys_ref[i] = s[:plen].astype(BF16)
        values_ref[i] = s[plen:].astype(BF16)


def local(queries, grad_out, attn_out, passage_keys, passage_values, block_lists, passage_lengths):
    shards = lax.axis_size(SHARD_AXES)
    parts = lax.axis_size("tensor")
    my_shard = lax.axis_index(SHARD_AXES)
    place = lax.axis_index("tensor").astype(jnp.int32).reshape(1)
    pass_dev, plen, _ = passage_keys.shape
    rows, columns = queries.shape
    width = columns // parts
    list_len = block_lists.shape[1]
    all_shape = jax.ShapeDtypeStruct((shards, 2 * plen, DH), BF16)

    share = width // DH
    message = jax.ShapeDtypeStruct((2 * QBLK + 2 * share, width), BF16)

    def prep(by):
        to = lax.rem(place + by, parts)
        return pl.pallas_call(
            prep_kernel,
            out_shape=message,
            in_specs=[smem(), hbm(), hbm(), hbm()],
            out_specs=vmem(),
            scratch_shapes=[pltpu.VMEM((QBLK, width), BF16), pltpu.SemaphoreType.DMA((3,))],
            compiler_params=params(LARGE_VMEM),
            cost_estimate=pl.CostEstimate(flops=2 * rows * width, bytes_accessed=10 * rows * width, transcendentals=0),
            name="prep",
        )(to, queries, grad_out, attn_out)

    def shift(piece, by):
        if by == 0:
            return piece
        return lax.ppermute(piece, "tensor", [(i, (i + by) % parts) for i in range(parts)])

    outgoing, pick = pl.pallas_call(
        send_kernel,
        out_shape=[all_shape, jax.ShapeDtypeStruct((shards,), jnp.int32)],
        in_specs=[smem(), vmem(), vmem(), vmem()],
        out_specs=[hbm(), smem()],
        scratch_shapes=[
            pltpu.VMEM((1, shards * parts), jnp.int32),
            pltpu.SMEM((1, shards * parts), jnp.int32),
            pltpu.VMEM(all_shape.shape, BF16),
            pltpu.SemaphoreType.DMA((2,)),
        ],
        compiler_params=params(LARGE_VMEM),
        name="send",
    )((my_shard * pass_dev).astype(jnp.int32).reshape(1), block_lists.T, passage_keys, passage_values)
    incoming = exchange(outgoing)
    messages = [shift(prep(j), j) for j in range(parts)]
    own_lists = lax.dynamic_slice_in_dim(block_lists, my_shard * parts, parts, 0)

    own_slots = slot_of(own_lists // pass_dev)
    keys = list_len * plen
    pairs = parts * QBLK * share * keys
    *query_parts, outgoing_grads = pl.pallas_call(
        main_kernel,
        out_shape=[jax.ShapeDtypeStruct((QBLK, width), BF16)] * parts + [all_shape],
        in_specs=[smem()] * 4 + [hbm()] + [pl.BlockSpec(memory_space=pl.ANY)] * parts,
        out_specs=[vmem()] * parts + [hbm()],
        scratch_shapes=[
            pltpu.VMEM((parts,) + message.shape, BF16),
            pltpu.VMEM((parts, list_len, 2 * plen, DH), BF16),
            pltpu.VMEM((parts, list_len, 2 * plen, DH), BF16),
            pltpu.VMEM((keys, DH), F32),
            pltpu.SemaphoreType.DMA((parts, list_len)),
            pltpu.SemaphoreType.DMA((parts,)),
            pltpu.SemaphoreType.DMA((parts, list_len)),
        ],
        compiler_params=params(),
        cost_estimate=pl.CostEstimate(flops=10 * pairs * DH, bytes_accessed=8 * rows * columns, transcendentals=pairs),
        name="attention",
    )(place, own_slots, own_lists, passage_lengths, incoming, *messages)

    returned = exchange(outgoing_grads)
    query_parts = [shift(piece, (parts - j) % parts) for j, piece in enumerate(query_parts)]
    query_grad = pl.pallas_call(
        place_kernel,
        out_shape=jax.ShapeDtypeStruct((rows, columns), BF16),
        in_specs=[smem()] + [vmem()] * parts,
        out_specs=vmem(),
        compiler_params=params(),
        cost_estimate=pl.CostEstimate(flops=0, bytes_accessed=4 * rows * columns, transcendentals=0),
        name="place",
    )(place, *query_parts)
    grad_shape = jax.ShapeDtypeStruct(passage_keys.shape, BF16)
    key_grad, value_grad = pl.pallas_call(
        sum_kernel,
        out_shape=[grad_shape, grad_shape],
        in_specs=[smem(), vmem()],
        out_specs=[vmem(), vmem()],
        compiler_params=params(),
        name="sum",
    )(pick, returned)
    return query_grad, key_grad, value_grad


def solution(mesh):
    parts = mesh.shape["tensor"]
    fine = Mesh(mesh.devices.reshape((2,) * len(SHARD_AXES) + (parts,)), SHARD_AXES + ("tensor",))
    tokens = P(SHARD_AXES + ("tensor",), None)
    passages = P(SHARD_AXES, None, "tensor")
    return jax.shard_map(
        local,
        mesh=fine,
        in_specs=(tokens, tokens, tokens, passages, passages, P(), P()),
        out_specs=(tokens, passages, passages),
        check_vma=False,
    )
```

time: 116 us -> 114 us (0.983)
  Pallas kernels: 14.8 us -> 23.2 us
  waiting for transfers between devices: 41.8 us -> 34 us
  starting transfers between devices: 54.2 us -> 52.4 us
    pallas_call x3 -> x6, Pallas kernels: 11.1 us -> 20 us  [the longest x4 8.48 us: prep(): pl.pallas_call(prep_kernel, out_shape=message, in_specs=[smem(), hbm(), h...]
    ppermute x6, waiting for transfers between devices: 32.4 us -> 24.6 us  [shift(): lax.ppermute(piece, 'tensor', [(i, (i + by) % parts) for i in range(parts)])]
    unnamed x19 -> x11, local copies, waits for them, and re-layouts: 3.29 us -> 1.84 us
  transfers between devices with their start and end apart: 8 -> 8, of which waited for: 7 -> 7; matrix products, arithmetic and copies ran while one was open for 0% -> 1% of each run, Pallas kernels for 3% -> 8%
where the time goes in v3:
time: 114 us; the launch traced here: 113 us
  starting transfers between devices  52.4 us (46%)
  waiting for transfers between devices  34 us (30%)
  Pallas kernels  23.2 us (20%)
  local copies, waits for them, and re-layouts  2.62 us (2%)
    all_to_all x2, starting transfers between devices, exchange(): lax.all_to_all(pieces, EXCHANGE_AXES, split_axis=0, concat_axis=0, tiled=...  33.2 us
    ppermute x6, waiting for transfers between devices, shift(): lax.ppermute(piece, 'tensor', [(i, (i + by) % parts) for i in range(parts)])  24.6 us
    ppermute x6, starting transfers between devices, shift(): lax.ppermute(piece, 'tensor', [(i, (i + by) % parts) for i in range(parts)])  19.1 us
    all_to_all x2, waiting for transfers between devices, exchange(): lax.all_to_all(pieces, EXCHANGE_AXES, split_axis=0, concat_axis=0, tiled=...  9.34 us
    pallas_call x4, Pallas kernels, prep(): pl.pallas_call(prep_kernel, out_shape=message, in_specs=[smem(), hbm(), h...  8.48 us
    pallas_call x1, Pallas kernels, local(): pl.pallas_call(main_kernel, out_shape=[jax.ShapeDtypeStruct((QBLK, width)...  8.19 us
    pallas_call x1, Pallas kernels, local(): pl.pallas_call(send_kernel, out_shape=[all_shape, jax.ShapeDtypeStruct((s...  3.34 us
  transfers between devices with their start and end apart: 8, of which 7 were waited for; matrix products, arithmetic and copies ran while one was open for 1% of the time, Pallas kernels for 8%

profile of v3, /device:TPU:1, one launch (start us, length us, event | category | flops | bytes accessed | tf_op | source)
XLA Modules:
  0.0 113.0 jit_solution(2383355013834552747)
XLA Ops:
  0.6 3.3 %send.1 = (bf16[128,32,128]{2,1,0:T(8,128)(2,1)}, s32[128]{0:T(128)}) custom-call(s32[1]{0:T(128)} %bitcast.1.base_ref, s32[16,512]{1,0:T(8,128)} %bitcast.3, bf16[4,16,128]{2,1,0:T(8,128)(2,1)} %keys_ref.1, bf16[4,16,128]{2,1,0:T(8,128)(2,1)} %values_ref.1), custom_call_target="tpu_custom_call" | custom-call | tf_op jit(solution)/shard_map/send/pallas_call | solution.py:214
  4.0 18.8 %all-to-all-start = ((bf16[128,32,128]{2,1,0:T(8,128)(2,1)}), bf16[128,32,128]{2,1,0:T(8,128)(2,1)S(1)}, u32[]{:S(2)}, u32[]{:S(2)}) async-start(bf16[128,32,128]{2,1,0:T(8,128)(2,1)} %get-tuple-element.12), calls=%async_computation | async-start | bytes 2097152 | tf_op jit(solution)/shard_map/all_to_all | solution.py:34
  22.8 2.1 %prep.6 = bf16[272,1024]{1,0:T(8,128)(2,1)} custom-call(s32[1]{0:T(128)S(6)} %rem.97.place_ref, bf16[128,4096]{1,0:T(8,128)(2,1)} %q_ref.7, bf16[128,4096]{1,0:T(8,128)(2,1)} %g_ref.7, bf16[128,4096]{1,0:T(8,128)(2,1)} %o_ref.7), custom_call_target="tpu_custom_call" | custom-call | flops 262144 | bytes 1310720 | tf_op jit(solution)/shard_map/prep/pallas_call | solution.py:198
  24.9 4.7 %collective-permute-start.1 = (bf16[272,1024]{1,0:T(8,128)(2,1)}, bf16[272,1024]{1,0:T(8,128)(2,1)S(1)}, u32[]{:S(2)}, u32[]{:S(2)}) collective-permute-start(bf16[272,1024]{1,0:T(8,128)(2,1)} %prep.6), channel_id=1, source_target_pairs={{0,2},{1,3},{2,0},{3,1},{4,6},{5,7},{6,4},{7,5},{8,10},{9,11},{10,... | collective-permute-start | bytes 1671176 | tf_op jit(solution)/shard_map/ppermute | solution.py:212
  29.6 2.1 %prep.7 = bf16[272,1024]{1,0:T(8,128)(2,1)} custom-call(s32[1]{0:T(128)S(6)} %rem.103.place_ref, bf16[128,4096]{1,0:T(8,128)(2,1)} %q_ref.7, bf16[128,4096]{1,0:T(8,128)(2,1)} %g_ref.7, bf16[128,4096]{1,0:T(8,128)(2,1)} %o_ref.7), custom_call_target="tpu_custom_call" | custom-call | flops 262144 | bytes 1310720 | tf_op jit(solution)/shard_map/prep/pallas_call | solution.py:198
  31.7 2.8 %collective-permute-start.2 = (bf16[272,1024]{1,0:T(8,128)(2,1)}, bf16[272,1024]{1,0:T(8,128)(2,1)S(1)}, u32[]{:S(2)}, u32[]{:S(2)}) collective-permute-start(bf16[272,1024]{1,0:T(8,128)(2,1)} %prep.7), channel_id=1, source_target_pairs={{0,3},{1,0},{2,1},{3,2},{4,7},{5,4},{6,5},{7,6},{8,11},{9,8},{10,9... | collective-permute-start | bytes 1671176 | tf_op jit(solution)/shard_map/ppermute | solution.py:212
  34.5 2.1 %prep.5 = bf16[272,1024]{1,0:T(8,128)(2,1)} custom-call(s32[1]{0:T(128)S(6)} %rem.91.place_ref, bf16[128,4096]{1,0:T(8,128)(2,1)} %q_ref.7, bf16[128,4096]{1,0:T(8,128)(2,1)} %g_ref.7, bf16[128,4096]{1,0:T(8,128)(2,1)} %o_ref.7), custom_call_target="tpu_custom_call" | custom-call | flops 262144 | bytes 1310720 | tf_op jit(solution)/shard_map/prep/pallas_call | solution.py:198
  36.6 2.5 %collective-permute-start = (bf16[272,1024]{1,0:T(8,128)(2,1)}, bf16[272,1024]{1,0:T(8,128)(2,1)S(1)}, u32[]{:S(2)}, u32[]{:S(2)}) collective-permute-start(bf16[272,1024]{1,0:T(8,128)(2,1)} %prep.5), channel_id=1, source_target_pairs={{0,1},{1,2},{2,3},{3,0},{4,5},{5,6},{6,7},{7,4},{8,9},{9,10},{10,1... | collective-permute-start | bytes 1671176 | tf_op jit(solution)/shard_map/ppermute | solution.py:212
  39.1 2.1 %prep.4.rest_0_ = bf16[272,1024]{1,0:T(8,128)(2,1)} custom-call(s32[1]{0:T(128)S(6)} %rem.85.place_ref, bf16[128,4096]{1,0:T(8,128)(2,1)} %q_ref.7, bf16[128,4096]{1,0:T(8,128)(2,1)} %g_ref.7, bf16[128,4096]{1,0:T(8,128)(2,1)} %o_ref.7), custom_call_target="tpu_custom_call" | custom-call | flops 262144 | bytes 1310720 | tf_op jit(solution)/shard_map/prep/pallas_call | solution.py:198
  41.2 0.8 constant_dynamic-slice_fusion
  42.0 0.1 copy.11.lists_ref
  42.1 0.0 copy-start.4
  42.1 0.0 collective-permute-done.1.rest_2_
  42.1 12.1 %collective-permute-done.2.rest_3_ = bf16[272,1024]{1,0:T(8,128)(2,1)S(1)} collective-permute-done((bf16[272,1024]{1,0:T(8,128)(2,1)}, bf16[272,1024]{1,0:T(8,128)(2,1)S(1)}, u32[]{:S(2)}, u32[]{:S(2)}) %collective-permute-start.2) | collective-permute-done | bytes 557088 | tf_op jit(solution)/shard_map/ppermute | solution.py:212
  54.2 0.3 collective-permute-done.rest_1_
  54.5 0.1 all-to-all-done.incoming_ref
  54.6 0.0 copy-done.4
  54.6 0.0 copy-start
  54.6 1.1 copy-done
  55.6 8.2 %attention.1 = (bf16[128,1024]{1,0:T(8,128)(2,1)S(1)}, bf16[128,1024]{1,0:T(8,128)(2,1)S(1)}, bf16[128,1024]{1,0:T(8,128)(2,1)S(1)}, bf16[128,1024]{1,0:T(8,128)(2,1)S(1)}, bf16[128,32,128]{2,1,0:T(8,128)(2,1)}) custom-call(s32[1]{0:T(128)} %bitcast.place_ref, s32[4,16]{1,0:T(4,128)S(1)} %shift-left_or_fusion.slots_ref, s32[4,16]{1,0:T(4,128)S(1)} %copy.11.lists_ref, ...), custom_call_target="tpu_custom_call" | custom-call | flops 1342177280 | bytes 4194304 | tf_op jit(solution)/shard_map/attention/pallas_call | solution.py:235
  63.8 0.0 copy-start.2
  63.8 0.7 copy-done.2
  64.5 0.0 copy-start.3
  64.5 14.5 %all-to-all-start.1 = ((bf16[128,32,128]{2,1,0:T(8,128)(2,1)}), bf16[128,32,128]{2,1,0:T(8,128)(2,1)S(1)}, u32[]{:S(2)}, u32[]{:S(2)}) async-start(bf16[128,32,128]{2,1,0:T(8,128)(2,1)} %get-tuple-element.18), calls=%async_computation.1 | async-start | bytes 2097152 | tf_op jit(solution)/shard_map/all_to_all | solution.py:34
  79.0 0.0 copy-done.3
  79.0 4.3 %collective-permute-start.3 = (bf16[128,1024]{1,0:T(8,128)(2,1)S(1)}, bf16[128,1024]{1,0:T(8,128)(2,1)S(1)}, u32[]{:S(2)}, u32[]{:S(2)}) collective-permute-start(bf16[128,1024]{1,0:T(8,128)(2,1)S(1)} %copy-done.3), channel_id=1, source_target_pairs={{0,3},{1,0},{2,1},{3,2},{4,7},{5,4},{6,5},{7,6},{8,11},{9,8},{10,9... | collective-permute-start | bytes 786440 | tf_op jit(solution)/shard_map/ppermute | solution.py:212
  83.3 2.5 %collective-permute-start.4 = (bf16[128,1024]{1,0:T(8,128)(2,1)S(1)}, bf16[128,1024]{1,0:T(8,128)(2,1)S(1)}, u32[]{:S(2)}, u32[]{:S(2)}) collective-permute-start(bf16[128,1024]{1,0:T(8,128)(2,1)S(1)} %get-tuple-element.15), channel_id=1, source_target_pairs={{0,2},{1,3},{2,0},{3,1},{4,6},{5,7},{6,4},{7,5},{8,10},{9,11},{10,... | collective-permute-start | bytes 786440 | tf_op jit(solution)/shard_map/ppermute | solution.py:212
  85.8 2.4 %collective-permute-start.5 = (bf16[128,1024]{1,0:T(8,128)(2,1)S(1)}, bf16[128,1024]{1,0:T(8,128)(2,1)S(1)}, u32[]{:S(2)}, u32[]{:S(2)}) collective-permute-start(bf16[128,1024]{1,0:T(8,128)(2,1)S(1)} %get-tuple-element.16), channel_id=1, source_target_pairs={{0,1},{1,2},{2,3},{3,0},{4,5},{5,6},{6,7},{7,4},{8,9},{9,10},{10,1... | collective-permute-start | bytes 786440 | tf_op jit(solution)/shard_map/ppermute | solution.py:212
  88.3 0.8 collective-permute-done.3.rest_1_
  89.0 4.7 %collective-permute-done.4.rest_2_ = bf16[128,1024]{1,0:T(8,128)(2,1)S(1)} collective-permute-done((bf16[128,1024]{1,0:T(8,128)(2,1)S(1)}, bf16[128,1024]{1,0:T(8,128)(2,1)S(1)}, u32[]{:S(2)}, u32[]{:S(2)}) %collective-permute-start.4) | collective-permute-done | bytes 262176 | tf_op jit(solution)/shard_map/ppermute | solution.py:212
  93.7 6.8 %collective-permute-done.5.rest_3_ = bf16[128,1024]{1,0:T(8,128)(2,1)S(1)} collective-permute-done((bf16[128,1024]{1,0:T(8,128)(2,1)S(1)}, bf16[128,1024]{1,0:T(8,128)(2,1)S(1)}, u32[]{:S(2)}, u32[]{:S(2)}) %collective-permute-start.5) | collective-permute-done | bytes 262176 | tf_op jit(solution)/shard_map/ppermute | solution.py:212
  100.6 1.0 place.1
  101.6 0.0 copy-start.1
  101.6 9.2 %all-to-all-done.1.terms_ref = bf16[128,32,128]{2,1,0:T(8,128)(2,1)S(1)} async-done(((bf16[128,32,128]{2,1,0:T(8,128)(2,1)}), bf16[128,32,128]{2,1,0:T(8,128)(2,1)S(1)}, u32[]{:S(2)}, u32[]{:S(2)}) %all-to-all-start.1) | async-done | bytes 1048608 | tf_op jit(solution)/shard_map/all_to_all | solution.py:34
  110.8 0.0 copy-done.1
  110.8 2.2 %sum.1 = (bf16[4,16,128]{2,1,0:T(8,128)(2,1)}, bf16[4,16,128]{2,1,0:T(8,128)(2,1)}) custom-call(s32[128]{0:T(128)S(1)} %copy-done.1, bf16[128,32,128]{2,1,0:T(8,128)(2,1)S(1)} %all-to-all-done.1.terms_ref), custom_call_target="tpu_custom_call" | custom-call | tf_op jit(solution)/shard_map/sum/pallas_call | solution.py:266
  (1 shorter events, 0.0 us)
Async XLA Ops:
  4.0 50.6 %all-to-all-start = ((bf16[128,32,128]{2,1,0:T(8,128)(2,1)}), bf16[128,32,128]{2,1,0:T(8,128)(2,1)S(1)}, u32[]{:S(2)}, u32[]{:S(2)}) async-start(bf16[128,32,128]{2,1,0:T(8,128)(2,1)} %get-tuple-element.12), calls=%async_computation | async-start | bytes 2097152 | tf_op jit(solution)/shard_map/all_to_all | solution.py:34
  24.9 17.2 %collective-permute-start.1 = (bf16[272,1024]{1,0:T(8,128)(2,1)}, bf16[272,1024]{1,0:T(8,128)(2,1)S(1)}, u32[]{:S(2)}, u32[]{:S(2)}) collective-permute-start(bf16[272,1024]{1,0:T(8,128)(2,1)} %prep.6), channel_id=1, source_target_pairs={{0,2},{1,3},{2,0},{3,1},{4,6},{5,7},{6,4},{7,5},{8,10},{9,11},{10,... | collective-permute-start | bytes 1671176 | tf_op jit(solution)/shard_map/ppermute | solution.py:212
  31.7 22.5 %collective-permute-start.2 = (bf16[272,1024]{1,0:T(8,128)(2,1)}, bf16[272,1024]{1,0:T(8,128)(2,1)S(1)}, u32[]{:S(2)}, u32[]{:S(2)}) collective-permute-start(bf16[272,1024]{1,0:T(8,128)(2,1)} %prep.7), channel_id=1, source_target_pairs={{0,3},{1,0},{2,1},{3,2},{4,7},{5,4},{6,5},{7,6},{8,11},{9,8},{10,9... | collective-permute-start | bytes 1671176 | tf_op jit(solution)/shard_map/ppermute | solution.py:212
  36.6 17.9 %collective-permute-start = (bf16[272,1024]{1,0:T(8,128)(2,1)}, bf16[272,1024]{1,0:T(8,128)(2,1)S(1)}, u32[]{:S(2)}, u32[]{:S(2)}) collective-permute-start(bf16[272,1024]{1,0:T(8,128)(2,1)} %prep.5), channel_id=1, source_target_pairs={{0,1},{1,2},{2,3},{3,0},{4,5},{5,6},{6,7},{7,4},{8,9},{9,10},{10,1... | collective-permute-start | bytes 1671176 | tf_op jit(solution)/shard_map/ppermute | solution.py:212
  42.1 12.5 %copy-start.4 = (s32[512]{0:T(512)S(1)}, s32[512]{0:T(512)}, u32[]{:S(2)}) copy-start(s32[512]{0:T(512)} %lengths_ref.1) | copy-start | bytes 6148
  54.6 1.1 copy-start
  63.8 0.7 copy-start.2
  64.5 14.5 %copy-start.3 = (bf16[128,1024]{1,0:T(8,128)(2,1)S(1)}, bf16[128,1024]{1,0:T(8,128)(2,1)}, u32[]{:S(2)}) copy-start(bf16[128,1024]{1,0:T(8,128)(2,1)} %copy-done.2) | copy-start | bytes 786436
  64.5 46.3 %all-to-all-start.1 = ((bf16[128,32,128]{2,1,0:T(8,128)(2,1)}), bf16[128,32,128]{2,1,0:T(8,128)(2,1)S(1)}, u32[]{:S(2)}, u32[]{:S(2)}) async-start(bf16[128,32,128]{2,1,0:T(8,128)(2,1)} %get-tuple-element.18), calls=%async_computation.1 | async-start | bytes 2097152 | tf_op jit(solution)/shard_map/all_to_all | solution.py:34
  79.0 10.0 %collective-permute-start.3 = (bf16[128,1024]{1,0:T(8,128)(2,1)S(1)}, bf16[128,1024]{1,0:T(8,128)(2,1)S(1)}, u32[]{:S(2)}, u32[]{:S(2)}) collective-permute-start(bf16[128,1024]{1,0:T(8,128)(2,1)S(1)} %copy-done.3), channel_id=1, source_target_pairs={{0,3},{1,0},{2,1},{3,2},{4,7},{5,4},{6,5},{7,6},{8,11},{9,8},{10,9... | collective-permute-start | bytes 786440 | tf_op jit(solution)/shard_map/ppermute | solution.py:212
  83.3 10.4 %collective-permute-start.4 = (bf16[128,1024]{1,0:T(8,128)(2,1)S(1)}, bf16[128,1024]{1,0:T(8,128)(2,1)S(1)}, u32[]{:S(2)}, u32[]{:S(2)}) collective-permute-start(bf16[128,1024]{1,0:T(8,128)(2,1)S(1)} %get-tuple-element.15), channel_id=1, source_target_pairs={{0,2},{1,3},{2,0},{3,1},{4,6},{5,7},{6,4},{7,5},{8,10},{9,11},{10,... | collective-permute-start | bytes 786440 | tf_op jit(solution)/shard_map/ppermute | solution.py:212
  85.8 14.8 %collective-permute-start.5 = (bf16[128,1024]{1,0:T(8,128)(2,1)S(1)}, bf16[128,1024]{1,0:T(8,128)(2,1)S(1)}, u32[]{:S(2)}, u32[]{:S(2)}) collective-permute-start(bf16[128,1024]{1,0:T(8,128)(2,1)S(1)} %get-tuple-element.16), channel_id=1, source_target_pairs={{0,1},{1,2},{2,3},{3,0},{4,5},{5,6},{6,7},{7,4},{8,9},{9,10},{10,1... | collective-permute-start | bytes 786440 | tf_op jit(solution)/shard_map/ppermute | solution.py:212
  101.6 9.2 %copy-start.1 = (s32[128]{0:T(128)S(1)}, s32[128]{0:T(128)}, u32[]{:S(2)}) copy-start(s32[128]{0:T(128)} %get-tuple-element.17.pick_ref) | copy-start | bytes 1540

commit v4 on v2

v4 whole, which is shorter than its diff:
```python
import jax
import jax.numpy as jnp
from jax import lax
from jax.experimental import pallas as pl
from jax.experimental.pallas import tpu as pltpu
from jax.sharding import Mesh
from jax.sharding import PartitionSpec as P

DH = 128
QBLK = 128
BF16 = jnp.bfloat16
F32 = jnp.float32
MASKED = -1e30
LOG2E = 1.4426950408889634
NT = (((1,), (1,)), ((), ()))
TN = (((0,), (0,)), ((), ()))
SMALL_VMEM = 24 * 1024 * 1024
LARGE_VMEM = 60 * 1024 * 1024


SHARD_AXES = ("y2", "y1", "y0", "z2", "z1", "z0", "core")
EXCHANGE_AXES = ("core", "y0", "z0", "y1", "z1", "y2", "z2")


def slot_of(shard):
    bits = len(SHARD_AXES)
    slot = 0
    for i, name in enumerate(EXCHANGE_AXES):
        bit = (shard >> (bits - 1 - SHARD_AXES.index(name))) & 1
        slot = slot | (bit << (bits - 1 - i))
    return slot


def exchange(pieces):
    return lax.all_to_all(pieces, EXCHANGE_AXES, split_axis=0, concat_axis=0, tiled=True)


def vmem():
    return pl.BlockSpec(memory_space=pltpu.VMEM)


def hbm():
    return pl.BlockSpec(memory_space=pltpu.HBM)


def smem():
    return pl.BlockSpec(memory_space=pltpu.SMEM)


def params(limit=SMALL_VMEM):
    return pltpu.CompilerParams(vmem_limit_bytes=limit)


def send_kernel(base_ref, lists_ref, keys_ref, values_ref, out_ref, pick_ref):
    pass_dev = keys_ref.shape[0]
    shards = out_ref.shape[0]
    blocks = lists_ref.shape[1] // shards
    here = lists_ref[...] - base_ref[0]
    here = jnp.where((here >= 0) & (here < pass_dev), here + 1, 0)
    here = jnp.sum(here, axis=0, keepdims=True)
    pick = here
    for b in range(1, blocks):
        pick = pick + pltpu.roll(here, here.shape[1] - b, 1)
    pick_ref[...] = pick
    tiles = [jnp.concatenate([keys_ref[i], values_ref[i]], axis=0) for i in range(pass_dev)]
    for n in range(shards):
        k = jnp.broadcast_to(pick[:, n * blocks : n * blocks + 1], tiles[0].shape)
        tile = tiles[0]
        for i in range(1, pass_dev):
            tile = jnp.where(k == i + 1, tiles[i], tile)
        out_ref[slot_of(n)] = tile


def prep_kernel(place_ref, q_ref, g_ref, o_ref, *rest):
    *message_refs, own_ref, delta_ref = rest
    parts = len(message_refs) + 1
    width = q_ref.shape[1] // parts
    share = width // DH
    lane = lax.broadcasted_iota(jnp.int32, (QBLK, DH), 1)
    delta = jnp.zeros((QBLK, DH), F32)
    for h in range(parts * share):
        cols = slice(h * DH, (h + 1) * DH)
        term = jnp.sum(g_ref[:, cols].astype(F32) * o_ref[:, cols].astype(F32), axis=1, keepdims=True)
        delta = jnp.where(lane == h, term, delta)
    delta_ref[...] = delta.T
    for j in range(parts):
        to = lax.rem(place_ref[0] + j, parts)
        rows = delta_ref[pl.ds(pl.multiple_of(to * share, share), share), :]
        high = rows.astype(BF16).astype(F32)
        rows = jnp.concatenate([high, rows - high], axis=0).astype(BF16)
        if j == 0:
            own_ref[...] = rows
            continue
        message_ref = message_refs[j - 1]
        cols = pl.ds(pl.multiple_of(to * width, width), width)
        message_ref[0:QBLK, :] = q_ref[:, cols]
        message_ref[QBLK : 2 * QBLK, :] = g_ref[:, cols]
        message_ref[2 * QBLK :, :] = jnp.zeros((2 * share, width), BF16)
        message_ref[2 * QBLK :, 0:DH] = rows


def main_kernel(place_ref, slots_ref, lists_ref, lengths_ref, incoming_ref, q_ref, g_ref, own_delta_ref, *rest):
    parts, list_len = lists_ref.shape
    message_refs = rest[: parts - 1]
    query_grad_ref, dq_ref, out_ref, own_ref, own_dq_ref, k_ref, v_ref, terms_ref, bias_ref, own_sems, out_sems = rest[parts - 1 :]
    plen = incoming_ref.shape[1] // 2
    width = own_ref.shape[1]
    share = width // DH
    scale = DH ** (-0.5)
    heads = [slice(h * DH, (h + 1) * DH) for h in range(share)]
    own_cols = pl.ds(pl.multiple_of(place_ref[0] * width, width), width)
    own_copies = [
        pltpu.make_async_copy(q_ref.at[:, own_cols], own_ref.at[0:QBLK, :], own_sems.at[0]),
        pltpu.make_async_copy(g_ref.at[:, own_cols], own_ref.at[QBLK : 2 * QBLK, :], own_sems.at[1]),
    ]
    for copy in own_copies:
        copy.start()
    slot_row = lax.broadcasted_iota(jnp.int32, (plen, DH), 0)
    rows_refs = list(message_refs) + [own_ref]
    delta_refs = [ref.at[2 * QBLK :, 0:DH] for ref in message_refs] + [own_delta_ref]
    result_refs = [dq_ref.at[j] for j in range(parts - 1)] + [own_dq_ref]
    all_slots = []
    for j in range(parts):
        block = lax.rem(place_ref[0] + parts - 1 - j, parts)
        all_slots.append([slots_ref[block, p] for p in range(list_len)])
        for p, slot in enumerate(all_slots[j]):
            rows = slice(p * plen, (p + 1) * plen)
            k_ref[j, rows, :] = incoming_ref[slot, 0:plen, :]
            v_ref[j, rows, :] = incoming_ref[slot, plen : 2 * plen, :]
            bias_ref[j, rows, :] = jnp.where(slot_row < lengths_ref[lists_ref[block, p]], 0.0, MASKED)

    def products(j):
        if j == parts - 1:
            for copy in own_copies:
                copy.wait()
        queries = jnp.concatenate([rows_refs[j][0:QBLK, c] for c in heads], axis=0)
        grads = jnp.concatenate([rows_refs[j][QBLK : 2 * QBLK, c] for c in heads], axis=0)
        scores = lax.dot_general(k_ref[j], queries, NT, preferred_element_type=F32)
        weight_grads = lax.dot_general(v_ref[j], grads, NT, preferred_element_type=F32)
        return queries, grads, scores, weight_grads

    stores = []
    ahead = products(0)
    for j in range(parts):
        queries, grads, scores, weight_grads = ahead
        if j + 1 < parts:
            ahead = products(j + 1)
        delta = delta_refs[j][...].astype(F32)
        delta = delta[:share] + delta[share:]
        delta = jnp.concatenate([delta[h : h + 1] for h in range(share)], axis=1)
        scores = scores * (scale * LOG2E) + jnp.concatenate([bias_ref[j]] * share, axis=1)
        weights = jnp.exp2(scores - jnp.max(scores, axis=0, keepdims=True))
        weights = weights * (1.0 / jnp.sum(weights, axis=0, keepdims=True))
        score_grads = (weights * (weight_grads - delta)).astype(BF16)
        value_term = jnp.dot(weights.astype(BF16), grads, preferred_element_type=F32)
        key_term = jnp.dot(score_grads, queries, preferred_element_type=F32) * scale
        terms_ref[j, :, 0:plen, :] = key_term.astype(BF16).reshape(list_len, plen, DH)
        terms_ref[j, :, plen : 2 * plen, :] = value_term.astype(BF16).reshape(list_len, plen, DH)
        for p, slot in enumerate(all_slots[j]):
            copy = pltpu.make_async_copy(terms_ref.at[j, p], out_ref.at[slot], out_sems.at[j, p])
            copy.start()
            stores.append(copy)
        query_part = lax.dot_general(k_ref[j], score_grads, TN, preferred_element_type=F32) * scale
        for c in heads:
            result_refs[j][:, c] = query_part[:, c].T.astype(BF16)
    copy = pltpu.make_async_copy(own_dq_ref, query_grad_ref.at[:, own_cols], own_sems.at[0])
    copy.start()
    stores.append(copy)
    for copy in stores:
        copy.wait()


def place_kernel(place_ref, own_ref, *rest):
    del own_ref
    *piece_refs, out_ref, sems = rest
    parts = len(piece_refs) + 1
    width = out_ref.shape[1] // parts
    copies = []
    for j, piece_ref in enumerate(piece_refs):
        to = lax.rem(place_ref[0] + j + 1, parts)
        cols = pl.ds(pl.multiple_of(to * width, width), width)
        copies.append(pltpu.make_async_copy(piece_ref, out_ref.at[:, cols], sems.at[j]))
    for copy in copies:
        copy.start()
    for copy in copies:
        copy.wait()


def sum_kernel(pick_ref, terms_ref, keys_ref, values_ref, total_ref):
    pass_dev, plen, _ = keys_ref.shape
    shards = terms_ref.shape[0]
    blocks = pick_ref.shape[1] // shards
    ways = total_ref.shape[0]
    total_ref[...] = jnp.zeros_like(total_ref)
    for n in range(shards):
        total_ref[n % ways, pick_ref[0, n * blocks]] += terms_ref[slot_of(n)].astype(F32)
    for i in range(pass_dev):
        total = total_ref[0, i + 1]
        for w in range(1, ways):
            total = total + total_ref[w, i + 1]
        keys_ref[i] = total[:plen].astype(BF16)
        values_ref[i] = total[plen:].astype(BF16)


def local(queries, grad_out, attn_out, passage_keys, passage_values, block_lists, passage_lengths):
    shards = lax.axis_size(SHARD_AXES)
    parts = lax.axis_size("tensor")
    my_shard = lax.axis_index(SHARD_AXES)
    place = lax.axis_index("tensor").astype(jnp.int32).reshape(1)
    pass_dev, plen, _ = passage_keys.shape
    rows, columns = queries.shape
    width = columns // parts
    list_len = block_lists.shape[1]
    all_shape = jax.ShapeDtypeStruct((shards, 2 * plen, DH), BF16)

    share = width // DH
    message = jax.ShapeDtypeStruct((2 * QBLK + 2 * share, width), BF16)
    own_shape = jax.ShapeDtypeStruct((2 * share, QBLK), BF16)
    *messages, own_delta = pl.pallas_call(
        prep_kernel,
        out_shape=[message] * (parts - 1) + [own_shape],
        in_specs=[smem(), vmem(), vmem(), vmem()],
        out_specs=[vmem()] * parts,
        scratch_shapes=[pltpu.VMEM((DH, QBLK), F32)],
        compiler_params=params(),
        cost_estimate=pl.CostEstimate(flops=2 * rows * columns, bytes_accessed=10 * rows * columns, transcendentals=0),
        name="prep",
    )(place, queries, grad_out, attn_out)

    def shift(piece, by):
        if by == 0:
            return piece
        return lax.ppermute(piece, "tensor", [(i, (i + by) % parts) for i in range(parts)])

    base = (my_shard * pass_dev).astype(jnp.int32).reshape(1)
    outgoing, pick = pl.pallas_call(
        send_kernel,
        out_shape=[all_shape, jax.ShapeDtypeStruct((1, shards * parts), jnp.int32)],
        in_specs=[smem(), vmem(), vmem(), vmem()],
        out_specs=[vmem(), vmem()],
        compiler_params=params(LARGE_VMEM),
        name="send",
    )(base, block_lists.T, passage_keys, passage_values)
    incoming = exchange(outgoing)
    messages = [shift(piece, j + 1) for j, piece in enumerate(messages)]
    own_lists = lax.dynamic_slice_in_dim(block_lists, my_shard * parts, parts, 0)

    own_slots = slot_of(own_lists // pass_dev)
    keys = list_len * plen
    pairs = parts * QBLK * share * keys
    any_place = pl.BlockSpec(memory_space=pl.ANY)
    full_shape = jax.ShapeDtypeStruct((rows, columns), BF16)
    query_grad, query_parts, outgoing_grads = pl.pallas_call(
        main_kernel,
        out_shape=[full_shape, jax.ShapeDtypeStruct((parts - 1, QBLK, width), BF16), all_shape],
        in_specs=[smem()] * 4 + [vmem()] + [any_place] * 2 + [vmem()] * parts,
        out_specs=[hbm(), vmem(), hbm()],
        scratch_shapes=[
            pltpu.VMEM((2 * QBLK, width), BF16),
            pltpu.VMEM((QBLK, width), BF16),
            pltpu.VMEM((parts, keys, DH), BF16),
            pltpu.VMEM((parts, keys, DH), BF16),
            pltpu.VMEM((parts, list_len, 2 * plen, DH), BF16),
            pltpu.VMEM((parts, keys, DH), F32),
            pltpu.SemaphoreType.DMA((2,)),
            pltpu.SemaphoreType.DMA((parts, list_len)),
        ],
        compiler_params=params(),
        cost_estimate=pl.CostEstimate(flops=10 * pairs * DH, bytes_accessed=8 * rows * columns, transcendentals=pairs),
        name="attention",
    )(place, own_slots, own_lists, passage_lengths, incoming, queries, grad_out, own_delta, *messages)

    returned = exchange(outgoing_grads)
    query_parts = [shift(query_parts[j], parts - 1 - j) for j in range(parts - 1)]
    query_grad = pl.pallas_call(
        place_kernel,
        out_shape=full_shape,
        in_specs=[smem(), hbm()] + [vmem()] * (parts - 1),
        out_specs=hbm(),
        scratch_shapes=[pltpu.SemaphoreType.DMA((parts - 1,))],
        input_output_aliases={1: 0},
        compiler_params=params(),
        cost_estimate=pl.CostEstimate(flops=0, bytes_accessed=4 * rows * columns, transcendentals=0),
        name="place",
    )(place, query_grad, *query_parts)
    grad_shape = jax.ShapeDtypeStruct(passage_keys.shape, BF16)
    key_grad, value_grad = pl.pallas_call(
        sum_kernel,
        out_shape=[grad_shape, grad_shape],
        in_specs=[smem(), vmem()],
        out_specs=[vmem(), vmem()],
        scratch_shapes=[pltpu.VMEM((4, pass_dev + 1, 2 * plen, DH), F32)],
        compiler_params=params(),
        name="sum",
    )(pick, returned)
    return query_grad, key_grad, value_grad


def solution(mesh):
    parts = mesh.shape["tensor"]
    fine = Mesh(mesh.devices.reshape((2,) * len(SHARD_AXES) + (parts,)), SHARD_AXES + ("tensor",))
    tokens = P(SHARD_AXES + ("tensor",), None)
    passages = P(SHARD_AXES, None, "tensor")
    return jax.shard_map(
        local,
        mesh=fine,
        in_specs=(tokens, tokens, tokens, passages, passages, P(), P()),
        out_specs=(tokens, passages, passages),
        check_vma=False,
    )
```

time: 116 us -> 113 us (0.974)
  waiting for transfers between devices: 41.8 us -> 39.4 us
  Pallas kernels: 14.8 us -> 13.1 us
    ppermute x6, waiting for transfers between devices: 32.4 us -> 26.7 us  [shift(): lax.ppermute(piece, 'tensor', [(i, (i + by) % parts) for i in range(parts)])]
    all_to_all x2, waiting for transfers between devices: 9.4 us -> 12.7 us  [exchange(): lax.all_to_all(pieces, EXCHANGE_AXES, split_axis=0, concat_axis=0, tiled=...]
    unnamed x19 -> x17, local copies, waits for them, and re-layouts: 3.29 us -> 3.19 us
  transfers between devices with their start and end apart: 8 -> 8, of which waited for: 7 -> 6; matrix products, arithmetic and copies ran while one was open for 0% -> 1% of each run, Pallas kernels for 3% -> 2%
where the time goes in v4:
time: 113 us
  starting transfers between devices  55.3 us (49%)
  waiting for transfers between devices  39.4 us (35%)
  Pallas kernels  13.1 us (12%)
  local copies, waits for them, and re-layouts  4.02 us (4%)
    all_to_all x2, starting transfers between devices, exchange(): lax.all_to_all(pieces, EXCHANGE_AXES, split_axis=0, concat_axis=0, tiled=...  34.2 us
    ppermute x6, waiting for transfers between devices, shift(): lax.ppermute(piece, 'tensor', [(i, (i + by) % parts) for i in range(parts)])  26.7 us
    ppermute x6, starting transfers between devices, shift(): lax.ppermute(piece, 'tensor', [(i, (i + by) % parts) for i in range(parts)])  21.1 us
    all_to_all x2, waiting for transfers between devices, exchange(): lax.all_to_all(pieces, EXCHANGE_AXES, split_axis=0, concat_axis=0, tiled=...  12.7 us
    pallas_call x1, Pallas kernels, local(): pl.pallas_call(main_kernel, out_shape=[full_shape, jax.ShapeDtypeStruct((...  6.57 us
    unnamed x17, local copies, waits for them, and re-layouts  3.19 us
  transfers between devices with their start and end apart: 8, of which 6 were waited for; matrix products, arithmetic and copies ran while one was open for 1% of the time, Pallas kernels for 2%

profile of v4, /device:TPU:1, one launch (start us, length us, event | category | flops | bytes accessed | tf_op | source)
XLA Modules:
  0.0 112.6 jit_solution(9722214763967475022)
XLA Ops:
  0.6 2.2 %send.1 = (bf16[128,32,128]{2,1,0:T(8,128)(2,1)}, s32[1,512]{1,0:T(1,128)}) custom-call(s32[1]{0:T(128)} %bitcast.1.base_ref, s32[16,512]{1,0:T(8,128)} %bitcast.9, bf16[4,16,128]{2,1,0:T(8,128)(2,1)} %keys_ref.1, bf16[4,16,128]{2,1,0:T(8,128)(2,1)} %values_ref.1), custom_call_target="tpu_custom_call" | custom-call | tf_op jit(solution)/shard_map/send/pallas_call | solution.py:236
  2.8 0.0 copy-start
  2.8 0.0 copy-start.1
  2.8 19.3 %all-to-all-start = ((bf16[128,32,128]{2,1,0:T(8,128)(2,1)}), bf16[128,32,128]{2,1,0:T(8,128)(2,1)}, u32[]{:S(2)}, u32[]{:S(2)}) async-start(bf16[128,32,128]{2,1,0:T(8,128)(2,1)} %get-tuple-element.14), calls=%async_computation | async-start | bytes 2097152 | tf_op jit(solution)/shard_map/all_to_all | solution.py:35
  22.2 0.0 copy-done
  22.2 0.0 copy-done.1
  22.2 0.0 copy-start.2
  22.2 1.2 %copy-done.2 = bf16[128,4096]{1,0:T(8,128)(2,1)S(1)} copy-done((bf16[128,4096]{1,0:T(8,128)(2,1)S(1)}, bf16[128,4096]{1,0:T(8,128)(2,1)}, u32[]{:S(2)}) %copy-start.2) | copy-done | bytes 1048600
  23.4 0.0 copy-start.3
  23.4 1.8 %prep.1 = (bf16[272,1024]{1,0:T(8,128)(2,1)}, bf16[272,1024]{1,0:T(8,128)(2,1)}, bf16[272,1024]{1,0:T(8,128)(2,1)}, bf16[16,128]{1,0:T(8,128)(2,1)S(1)}) custom-call(s32[1]{0:T(128)} %bitcast.place_ref, bf16[128,4096]{1,0:T(8,128)(2,1)S(1)} %copy-done.1, bf16[128,4096]{1,0:T(8,128)(2,1)S(1)} %copy-done.2, bf16[128,4096]{1,0:T(8,128)(2,1)S(1)} %copy-done), custom_call_target="tpu_custom_call" | custom-call | flops 1048576 | bytes 5242880 | tf_op jit(solution)/shard_map/prep/pallas_call | solution.py:219
  25.3 3.1 %collective-permute-start = (bf16[272,1024]{1,0:T(8,128)(2,1)}, bf16[272,1024]{1,0:T(8,128)(2,1)S(1)}, u32[]{:S(2)}, u32[]{:S(2)}) collective-permute-start(bf16[272,1024]{1,0:T(8,128)(2,1)} %get-tuple-element.16), channel_id=1, source_target_pairs={{0,1},{1,2},{2,3},{3,0},{4,5},{5,6},{6,7},{7,4},{8,9},{9,10},{10,1... | collective-permute-start | bytes 1671176 | tf_op jit(solution)/shard_map/ppermute | solution.py:233
  28.4 4.4 %collective-permute-start.1 = (bf16[272,1024]{1,0:T(8,128)(2,1)}, bf16[272,1024]{1,0:T(8,128)(2,1)S(1)}, u32[]{:S(2)}, u32[]{:S(2)}) collective-permute-start(bf16[272,1024]{1,0:T(8,128)(2,1)} %get-tuple-element.17), channel_id=1, source_target_pairs={{0,2},{1,3},{2,0},{3,1},{4,6},{5,7},{6,4},{7,5},{8,10},{9,11},{10,... | collective-permute-start | bytes 1671176 | tf_op jit(solution)/shard_map/ppermute | solution.py:233
  32.8 3.1 %collective-permute-start.2 = (bf16[272,1024]{1,0:T(8,128)(2,1)}, bf16[272,1024]{1,0:T(8,128)(2,1)}, u32[]{:S(2)}, u32[]{:S(2)}) collective-permute-start(bf16[272,1024]{1,0:T(8,128)(2,1)} %get-tuple-element.18), channel_id=1, source_target_pairs={{0,3},{1,0},{2,1},{3,2},{4,7},{5,4},{6,5},{7,6},{8,11},{9,8},{10,9... | collective-permute-start | bytes 1671176 | tf_op jit(solution)/shard_map/ppermute | solution.py:233
  35.8 0.8 constant_dynamic-slice_fusion
  36.6 0.1 copy.12.lists_ref
  36.7 0.0 copy-start.7
  36.7 5.5 %collective-permute-done.rest_0_ = bf16[272,1024]{1,0:T(8,128)(2,1)S(1)} collective-permute-done((bf16[272,1024]{1,0:T(8,128)(2,1)}, bf16[272,1024]{1,0:T(8,128)(2,1)S(1)}, u32[]{:S(2)}, u32[]{:S(2)}) %collective-permute-start) | collective-permute-done | bytes 557088 | tf_op jit(solution)/shard_map/ppermute | solution.py:233
  42.2 12.8 %collective-permute-done.1.rest_1_ = bf16[272,1024]{1,0:T(8,128)(2,1)S(1)} collective-permute-done((bf16[272,1024]{1,0:T(8,128)(2,1)}, bf16[272,1024]{1,0:T(8,128)(2,1)S(1)}, u32[]{:S(2)}, u32[]{:S(2)}) %collective-permute-start.1) | collective-permute-done | bytes 557088 | tf_op jit(solution)/shard_map/ppermute | solution.py:233
  55.0 0.0 copy-start.5
  55.0 0.8 copy-done.5
  55.8 0.8 collective-permute-done.2.rest_2_
  56.6 0.0 all-to-all-done.incoming_ref
  56.6 0.0 copy-done.3
  56.6 0.0 copy-done.7
  56.7 0.0 copy-start.6
  56.7 1.0 copy-done.6
  57.7 6.6 %attention.1 = (bf16[128,4096]{1,0:T(8,128)(2,1)}, bf16[3,128,1024]{2,1,0:T(8,128)(2,1)S(1)}, bf16[128,32,128]{2,1,0:T(8,128)(2,1)}) custom-call(s32[1]{0:T(128)} %bitcast.place_ref, s32[4,16]{1,0:T(4,128)S(1)} %shift-left_or_fusion.slots_ref, s32[4,16]{1,0:T(4,128)S(1)} %copy.12.lists_ref, s32[512]{0:T(512)S(1)} %copy-done.7, ...), custom_call_target="tpu_custom_call" | custom-call | flops 1342177280 | bytes 4194304 | tf_op jit(solution)/shard_map/attention/pallas_call | solution.py:253
  64.3 14.9 %all-to-all-start.1 = ((bf16[128,32,128]{2,1,0:T(8,128)(2,1)}), bf16[128,32,128]{2,1,0:T(8,128)(2,1)S(1)}, u32[]{:S(2)}, u32[]{:S(2)}) async-start(bf16[128,32,128]{2,1,0:T(8,128)(2,1)} %get-tuple-element.22), calls=%async_computation.1 | async-start | bytes 2097152 | tf_op jit(solution)/shard_map/all_to_all | solution.py:35
  79.2 0.1 slice_bitcast_fusion
  79.2 4.0 %collective-permute-start.5 = (bf16[128,1024]{1,0:T(8,128)(2,1)S(1)}, bf16[128,1024]{1,0:T(8,128)(2,1)S(1)}, u32[]{:S(2)}, u32[]{:S(2)}) collective-permute-start(bf16[128,1024]{1,0:T(8,128)(2,1)S(1)} %get-tuple-element.25), channel_id=1, source_target_pairs={{0,1},{1,2},{2,3},{3,0},{4,5},{5,6},{6,7},{7,4},{8,9},{9,10},{10,1... | collective-permute-start | bytes 786440 | tf_op jit(solution)/shard_map/ppermute | solution.py:233
  83.2 3.3 %collective-permute-start.4 = (bf16[128,1024]{1,0:T(8,128)(2,1)S(1)}, bf16[128,1024]{1,0:T(8,128)(2,1)S(1)}, u32[]{:S(2)}, u32[]{:S(2)}) collective-permute-start(bf16[128,1024]{1,0:T(8,128)(2,1)S(1)} %get-tuple-element.26), channel_id=1, source_target_pairs={{0,2},{1,3},{2,0},{3,1},{4,6},{5,7},{6,4},{7,5},{8,10},{9,11},{10,... | collective-permute-start | bytes 786440 | tf_op jit(solution)/shard_map/ppermute | solution.py:233
  86.6 3.2 %collective-permute-start.3 = (bf16[128,1024]{1,0:T(8,128)(2,1)S(1)}, bf16[128,1024]{1,0:T(8,128)(2,1)S(1)}, u32[]{:S(2)}, u32[]{:S(2)}) collective-permute-start(bf16[128,1024]{1,0:T(8,128)(2,1)S(1)} %get-tuple-element.27), channel_id=1, source_target_pairs={{0,3},{1,0},{2,1},{3,2},{4,7},{5,4},{6,5},{7,6},{8,11},{9,8},{10,9... | collective-permute-start | bytes 786440 | tf_op jit(solution)/shard_map/ppermute | solution.py:233
  89.8 0.0 collective-permute-done.5.rest_2_
  89.8 6.3 %collective-permute-done.4.rest_1_ = bf16[128,1024]{1,0:T(8,128)(2,1)S(1)} collective-permute-done((bf16[128,1024]{1,0:T(8,128)(2,1)S(1)}, bf16[128,1024]{1,0:T(8,128)(2,1)S(1)}, u32[]{:S(2)}, u32[]{:S(2)}) %collective-permute-start.4) | collective-permute-done | bytes 262176 | tf_op jit(solution)/shard_map/ppermute | solution.py:233
  96.1 1.3 %collective-permute-done.3.rest_0_ = bf16[128,1024]{1,0:T(8,128)(2,1)S(1)} collective-permute-done((bf16[128,1024]{1,0:T(8,128)(2,1)S(1)}, bf16[128,1024]{1,0:T(8,128)(2,1)S(1)}, u32[]{:S(2)}, u32[]{:S(2)}) %collective-permute-start.3) | collective-permute-done | bytes 262176 | tf_op jit(solution)/shard_map/ppermute | solution.py:233
  97.4 0.0 copy-start.4
  97.4 0.9 place.1
  98.3 12.7 %all-to-all-done.1.terms_ref = bf16[128,32,128]{2,1,0:T(8,128)(2,1)S(1)} async-done(((bf16[128,32,128]{2,1,0:T(8,128)(2,1)}), bf16[128,32,128]{2,1,0:T(8,128)(2,1)S(1)}, u32[]{:S(2)}, u32[]{:S(2)}) %all-to-all-start.1) | async-done | bytes 1048608 | tf_op jit(solution)/shard_map/all_to_all | solution.py:35
  111.0 0.0 copy-done.4
  111.0 1.6 %sum.1 = (bf16[4,16,128]{2,1,0:T(8,128)(2,1)}, bf16[4,16,128]{2,1,0:T(8,128)(2,1)}) custom-call(s32[1,512]{1,0:T(1,128)S(1)} %copy-done.4, bf16[128,32,128]{2,1,0:T(8,128)(2,1)S(1)} %all-to-all-done.1.terms_ref), custom_call_target="tpu_custom_call" | custom-call | tf_op jit(solution)/shard_map/sum/pallas_call | solution.py:287
  (1 shorter events, 0.0 us)
Async XLA Ops:
  2.8 19.3 %copy-start = (bf16[128,4096]{1,0:T(8,128)(2,1)S(1)}, bf16[128,4096]{1,0:T(8,128)(2,1)}, u32[]{:S(2)}) copy-start(bf16[128,4096]{1,0:T(8,128)(2,1)} %o_ref.1) | copy-start | bytes 3145732
  2.8 19.4 %copy-start.1 = (bf16[128,4096]{1,0:T(8,128)(2,1)S(1)}, bf16[128,4096]{1,0:T(8,128)(2,1)}, u32[]{:S(2)}) copy-start(bf16[128,4096]{1,0:T(8,128)(2,1)} %q_ref.3) | copy-start | bytes 3145732
  2.8 53.8 %all-to-all-start = ((bf16[128,32,128]{2,1,0:T(8,128)(2,1)}), bf16[128,32,128]{2,1,0:T(8,128)(2,1)}, u32[]{:S(2)}, u32[]{:S(2)}) async-start(bf16[128,32,128]{2,1,0:T(8,128)(2,1)} %get-tuple-element.14), calls=%async_computation | async-start | bytes 2097152 | tf_op jit(solution)/shard_map/all_to_all | solution.py:35
  22.2 1.2 %copy-start.2 = (bf16[128,4096]{1,0:T(8,128)(2,1)S(1)}, bf16[128,4096]{1,0:T(8,128)(2,1)}, u32[]{:S(2)}) copy-start(bf16[128,4096]{1,0:T(8,128)(2,1)} %g_ref.3) | copy-start | bytes 3145732
  23.4 33.2 %copy-start.3 = (bf16[128,4096]{1,0:T(8,128)(2,1)S(1)}, bf16[128,4096]{1,0:T(8,128)(2,1)}, u32[]{:S(2)}) copy-start(bf16[128,4096]{1,0:T(8,128)(2,1)} %g_ref.3) | copy-start | bytes 3145732
  25.3 16.9 %collective-permute-start = (bf16[272,1024]{1,0:T(8,128)(2,1)}, bf16[272,1024]{1,0:T(8,128)(2,1)S(1)}, u32[]{:S(2)}, u32[]{:S(2)}) collective-permute-start(bf16[272,1024]{1,0:T(8,128)(2,1)} %get-tuple-element.16), channel_id=1, source_target_pairs={{0,1},{1,2},{2,3},{3,0},{4,5},{5,6},{6,7},{7,4},{8,9},{9,10},{10,1... | collective-permute-start | bytes 1671176 | tf_op jit(solution)/shard_map/ppermute | solution.py:233
  28.4 26.6 %collective-permute-start.1 = (bf16[272,1024]{1,0:T(8,128)(2,1)}, bf16[272,1024]{1,0:T(8,128)(2,1)S(1)}, u32[]{:S(2)}, u32[]{:S(2)}) collective-permute-start(bf16[272,1024]{1,0:T(8,128)(2,1)} %get-tuple-element.17), channel_id=1, source_target_pairs={{0,2},{1,3},{2,0},{3,1},{4,6},{5,7},{6,4},{7,5},{8,10},{9,11},{10,... | collective-permute-start | bytes 1671176 | tf_op jit(solution)/shard_map/ppermute | solution.py:233
  32.8 23.9 %collective-permute-start.2 = (bf16[272,1024]{1,0:T(8,128)(2,1)}, bf16[272,1024]{1,0:T(8,128)(2,1)}, u32[]{:S(2)}, u32[]{:S(2)}) collective-permute-start(bf16[272,1024]{1,0:T(8,128)(2,1)} %get-tuple-element.18), channel_id=1, source_target_pairs={{0,3},{1,0},{2,1},{3,2},{4,7},{5,4},{6,5},{7,6},{8,11},{9,8},{10,9... | collective-permute-start | bytes 1671176 | tf_op jit(solution)/shard_map/ppermute | solution.py:233
  36.7 20.0 %copy-start.7 = (s32[512]{0:T(512)S(1)}, s32[512]{0:T(512)}, u32[]{:S(2)}) copy-start(s32[512]{0:T(512)} %lengths_ref.1) | copy-start | bytes 6148
  55.0 0.8 copy-start.5
  56.7 1.1 copy-start.6
  64.3 46.7 %all-to-all-start.1 = ((bf16[128,32,128]{2,1,0:T(8,128)(2,1)}), bf16[128,32,128]{2,1,0:T(8,128)(2,1)S(1)}, u32[]{:S(2)}, u32[]{:S(2)}) async-start(bf16[128,32,128]{2,1,0:T(8,128)(2,1)} %get-tuple-element.22), calls=%async_computation.1 | async-start | bytes 2097152 | tf_op jit(solution)/shard_map/all_to_all | solution.py:35
  79.2 10.6 %collective-permute-start.5 = (bf16[128,1024]{1,0:T(8,128)(2,1)S(1)}, bf16[128,1024]{1,0:T(8,128)(2,1)S(1)}, u32[]{:S(2)}, u32[]{:S(2)}) collective-permute-start(bf16[128,1024]{1,0:T(8,128)(2,1)S(1)} %get-tuple-element.25), channel_id=1, source_target_pairs={{0,1},{1,2},{2,3},{3,0},{4,5},{5,6},{6,7},{7,4},{8,9},{9,10},{10,1... | collective-permute-start | bytes 786440 | tf_op jit(solution)/shard_map/ppermute | solution.py:233
  83.2 12.9 %collective-permute-start.4 = (bf16[128,1024]{1,0:T(8,128)(2,1)S(1)}, bf16[128,1024]{1,0:T(8,128)(2,1)S(1)}, u32[]{:S(2)}, u32[]{:S(2)}) collective-permute-start(bf16[128,1024]{1,0:T(8,128)(2,1)S(1)} %get-tuple-element.26), channel_id=1, source_target_pairs={{0,2},{1,3},{2,0},{3,1},{4,6},{5,7},{6,4},{7,5},{8,10},{9,11},{10,... | collective-permute-start | bytes 786440 | tf_op jit(solution)/shard_map/ppermute | solution.py:233
  86.6 10.8 %collective-permute-start.3 = (bf16[128,1024]{1,0:T(8,128)(2,1)S(1)}, bf16[128,1024]{1,0:T(8,128)(2,1)S(1)}, u32[]{:S(2)}, u32[]{:S(2)}) collective-permute-start(bf16[128,1024]{1,0:T(8,128)(2,1)S(1)} %get-tuple-element.27), channel_id=1, source_target_pairs={{0,3},{1,0},{2,1},{3,2},{4,7},{5,4},{6,5},{7,6},{8,11},{9,8},{10,9... | collective-permute-start | bytes 786440 | tf_op jit(solution)/shard_map/ppermute | solution.py:233
  97.4 13.6 %copy-start.4 = (s32[1,512]{1,0:T(1,128)S(1)}, s32[1,512]{1,0:T(1,128)}, u32[]{:S(2)}) copy-start(s32[1,512]{1,0:T(1,128)} %get-tuple-element.21.pick_ref) | copy-start | bytes 6148

commit v5 on v4

--- a/solution.py
+++ b/solution.py
@@ -35,8 +35,17 @@
     return lax.all_to_all(pieces, EXCHANGE_AXES, split_axis=0, concat_axis=0, tiled=True)
 
 
+def shifts(parts):
+    far = parts // 2
+    return (far,) + tuple(by for by in range(1, parts) if by != far)
+
+
 def vmem():
     return pl.BlockSpec(memory_space=pltpu.VMEM)
+
+
+def in_hbm(array):
+    return pltpu.with_memory_space_constraint(array, pltpu.HBM)
 
 
 def hbm():
@@ -84,7 +93,7 @@
         delta = jnp.where(lane == h, term, delta)
     delta_ref[...] = delta.T
     for j in range(parts):
-        to = lax.rem(place_ref[0] + j, parts)
+        to = lax.rem(place_ref[0] + (0 if j == 0 else shifts(parts)[j - 1]), parts)
         rows = delta_ref[pl.ds(pl.multiple_of(to * share, share), share), :]
         high = rows.astype(BF16).astype(F32)
         rows = jnp.concatenate([high, rows - high], axis=0).astype(BF16)
@@ -102,26 +111,32 @@
 def main_kernel(place_ref, slots_ref, lists_ref, lengths_ref, incoming_ref, q_ref, g_ref, own_delta_ref, *rest):
     parts, list_len = lists_ref.shape
     message_refs = rest[: parts - 1]
-    query_grad_ref, dq_ref, out_ref, own_ref, own_dq_ref, k_ref, v_ref, terms_ref, bias_ref, own_sems, out_sems = rest[parts - 1 :]
+    query_grad_ref, dq_ref, out_ref, own_ref, held_ref, own_dq_ref, k_ref, v_ref, terms_ref, bias_ref, own_sems, held_sems, out_sems = rest[parts - 1 :]
     plen = incoming_ref.shape[1] // 2
     width = own_ref.shape[1]
     share = width // DH
     scale = DH ** (-0.5)
     heads = [slice(h * DH, (h + 1) * DH) for h in range(share)]
     own_cols = pl.ds(pl.multiple_of(place_ref[0] * width, width), width)
-    own_copies = [
-        pltpu.make_async_copy(q_ref.at[:, own_cols], own_ref.at[0:QBLK, :], own_sems.at[0]),
-        pltpu.make_async_copy(g_ref.at[:, own_cols], own_ref.at[QBLK : 2 * QBLK, :], own_sems.at[1]),
+    distances = (0,) + shifts(parts)
+    loads = [
+        [
+            pltpu.make_async_copy(q_ref.at[:, own_cols], own_ref.at[0:QBLK, :], own_sems.at[0]),
+            pltpu.make_async_copy(g_ref.at[:, own_cols], own_ref.at[QBLK : 2 * QBLK, :], own_sems.at[1]),
+        ]
     ]
-    for copy in own_copies:
-        copy.start()
+    for i, message_ref in enumerate(message_refs):
+        loads.append([pltpu.make_async_copy(message_ref, held_ref.at[i], held_sems.at[i])])
+    for copies in loads:
+        for copy in copies:
+            copy.start()
     slot_row = lax.broadcasted_iota(jnp.int32, (plen, DH), 0)
-    rows_refs = list(message_refs) + [own_ref]
-    delta_refs = [ref.at[2 * QBLK :, 0:DH] for ref in message_refs] + [own_delta_ref]
-    result_refs = [dq_ref.at[j] for j in range(parts - 1)] + [own_dq_ref]
+    rows_refs = [own_ref] + [held_ref.at[i] for i in range(parts - 1)]
+    delta_refs = [own_delta_ref] + [held_ref.at[i, 2 * QBLK :, 0:DH] for i in range(parts - 1)]
+    result_refs = [own_dq_ref] + [dq_ref.at[i] for i in range(parts - 1)]
     all_slots = []
     for j in range(parts):
-        block = lax.rem(place_ref[0] + parts - 1 - j, parts)
+        block = lax.rem(place_ref[0] + parts - distances[j], parts)
         all_slots.append([slots_ref[block, p] for p in range(list_len)])
         for p, slot in enumerate(all_slots[j]):
             rows = slice(p * plen, (p + 1) * plen)
@@ -130,9 +145,8 @@
             bias_ref[j, rows, :] = jnp.where(slot_row < lengths_ref[lists_ref[block, p]], 0.0, MASKED)
 
     def products(j):
-        if j == parts - 1:
-            for copy in own_copies:
-                copy.wait()
+        for copy in loads[j]:
+            copy.wait()
         queries = jnp.concatenate([rows_refs[j][0:QBLK, c] for c in heads], axis=0)
         grads = jnp.concatenate([rows_refs[j][QBLK : 2 * QBLK, c] for c in heads], axis=0)
         scores = lax.dot_general(k_ref[j], queries, NT, preferred_element_type=F32)
@@ -163,9 +177,10 @@
         query_part = lax.dot_general(k_ref[j], score_grads, TN, preferred_element_type=F32) * scale
         for c in heads:
             result_refs[j][:, c] = query_part[:, c].T.astype(BF16)
-    copy = pltpu.make_async_copy(own_dq_ref, query_grad_ref.at[:, own_cols], own_sems.at[0])
-    copy.start()
-    stores.append(copy)
+        if j == 0:
+            copy = pltpu.make_async_copy(own_dq_ref, query_grad_ref.at[:, own_cols], own_sems.at[0])
+            copy.start()
+            stores.append(copy)
     for copy in stores:
         copy.wait()
 
@@ -177,7 +192,7 @@
     width = out_ref.shape[1] // parts
     copies = []
     for j, piece_ref in enumerate(piece_refs):
-        to = lax.rem(place_ref[0] + j + 1, parts)
+        to = lax.rem(place_ref[0] + shifts(parts)[j], parts)
         cols = pl.ds(pl.multiple_of(to * width, width), width)
         copies.append(pltpu.make_async_copy(piece_ref, out_ref.at[:, cols], sems.at[j]))
     for copy in copies:
@@ -242,36 +257,37 @@
         name="send",
     )(base, block_lists.T, passage_keys, passage_values)
     incoming = exchange(outgoing)
-    messages = [shift(piece, j + 1) for j, piece in enumerate(messages)]
+    messages = [shift(piece, by) for piece, by in zip(messages, shifts(parts))]
     own_lists = lax.dynamic_slice_in_dim(block_lists, my_shard * parts, parts, 0)
 
     own_slots = slot_of(own_lists // pass_dev)
     keys = list_len * plen
     pairs = parts * QBLK * share * keys
-    any_place = pl.BlockSpec(memory_space=pl.ANY)
     full_shape = jax.ShapeDtypeStruct((rows, columns), BF16)
     query_grad, query_parts, outgoing_grads = pl.pallas_call(
         main_kernel,
         out_shape=[full_shape, jax.ShapeDtypeStruct((parts - 1, QBLK, width), BF16), all_shape],
-        in_specs=[smem()] * 4 + [vmem()] + [any_place] * 2 + [vmem()] * parts,
+        in_specs=[smem()] * 4 + [vmem(), hbm(), hbm(), vmem()] + [hbm()] * (parts - 1),
         out_specs=[hbm(), vmem(), hbm()],
         scratch_shapes=[
             pltpu.VMEM((2 * QBLK, width), BF16),
+            pltpu.VMEM((parts - 1,) + message.shape, BF16),
             pltpu.VMEM((QBLK, width), BF16),
             pltpu.VMEM((parts, keys, DH), BF16),
             pltpu.VMEM((parts, keys, DH), BF16),
             pltpu.VMEM((parts, list_len, 2 * plen, DH), BF16),
             pltpu.VMEM((parts, keys, DH), F32),
             pltpu.SemaphoreType.DMA((2,)),
+            pltpu.SemaphoreType.DMA((parts - 1,)),
             pltpu.SemaphoreType.DMA((parts, list_len)),
         ],
         compiler_params=params(),
         cost_estimate=pl.CostEstimate(flops=10 * pairs * DH, bytes_accessed=8 * rows * columns, transcendentals=pairs),
         name="attention",
-    )(place, own_slots, own_lists, passage_lengths, incoming, queries, grad_out, own_delta, *messages)
+    )(place, own_slots, own_lists, passage_lengths, incoming, in_hbm(queries), in_hbm(grad_out), own_delta, *[in_hbm(piece) for piece in messages])
 
     returned = exchange(outgoing_grads)
-    query_parts = [shift(query_parts[j], parts - 1 - j) for j in range(parts - 1)]
+    query_parts = [shift(query_parts[j], parts - by) for j, by in enumerate(shifts(parts))]
     query_grad = pl.pallas_call(
         place_kernel,
         out_shape=full_shape,

time: 113 us -> 111 us (0.982)
  starting transfers between devices: 55.3 us -> 53.7 us
    ppermute x6, waiting for transfers between devices: 26.7 us -> 24.7 us  [shift(): lax.ppermute(piece, 'tensor', [(i, (i + by) % parts) for i in range(parts)])]
    all_to_all x2, waiting for transfers between devices: 12.7 us -> 14.3 us  [exchange(): lax.all_to_all(pieces, EXCHANGE_AXES, split_axis=0, concat_axis=0, tiled=...]
    all_to_all x2, starting transfers between devices: 34.2 us -> 32.7 us  [exchange(): lax.all_to_all(pieces, EXCHANGE_AXES, split_axis=0, concat_axis=0, tiled=...]
  transfers between devices with their start and end apart: 8 -> 8, of which waited for: 6 -> 6; matrix products, arithmetic and copies ran while one was open for 1% -> 1% of each run, Pallas kernels for 2% -> 3%
where the time goes in v5:
time: 111 us
  starting transfers between devices  53.7 us (48%)
  waiting for transfers between devices  39 us (35%)
  Pallas kernels  14 us (13%)
  local copies, waits for them, and re-layouts  3.13 us (3%)
    all_to_all x2, starting transfers between devices, exchange(): lax.all_to_all(pieces, EXCHANGE_AXES, split_axis=0, concat_axis=0, tiled=...  32.7 us
    ppermute x6, waiting for transfers between devices, shift(): lax.ppermute(piece, 'tensor', [(i, (i + by) % parts) for i in range(parts)])  24.7 us
    ppermute x6, starting transfers between devices, shift(): lax.ppermute(piece, 'tensor', [(i, (i + by) % parts) for i in range(parts)])  21 us
    all_to_all x2, waiting for transfers between devices, exchange(): lax.all_to_all(pieces, EXCHANGE_AXES, split_axis=0, concat_axis=0, tiled=...  14.3 us
    pallas_call x1, Pallas kernels, local(): pl.pallas_call(main_kernel, out_shape=[full_shape, jax.ShapeDtypeStruct((...  7.39 us
    unnamed x17, local copies, waits for them, and re-layouts  2.3 us
  transfers between devices with their start and end apart: 8, of which 6 were waited for; matrix products, arithmetic and copies ran while one was open for 1% of the time, Pallas kernels for 3%

profile of v5, /device:TPU:1, one launch (start us, length us, event | category | flops | bytes accessed | tf_op | source)
XLA Modules:
  0.0 110.6 jit_solution(16118312980172356746)
XLA Ops:
  0.6 2.2 %send.1 = (bf16[128,32,128]{2,1,0:T(8,128)(2,1)}, s32[1,512]{1,0:T(1,128)}) custom-call(s32[1]{0:T(128)} %bitcast.1.base_ref, s32[16,512]{1,0:T(8,128)} %bitcast.9, bf16[4,16,128]{2,1,0:T(8,128)(2,1)} %keys_ref.1, bf16[4,16,128]{2,1,0:T(8,128)(2,1)} %values_ref.1), custom_call_target="tpu_custom_call" | custom-call | tf_op jit(solution)/shard_map/send/pallas_call | solution.py:251
  2.8 0.0 copy-start
  2.8 0.0 copy-start.1
  2.8 18.9 %all-to-all-start = ((bf16[128,32,128]{2,1,0:T(8,128)(2,1)}), bf16[128,32,128]{2,1,0:T(8,128)(2,1)S(1)}, u32[]{:S(2)}, u32[]{:S(2)}) async-start(bf16[128,32,128]{2,1,0:T(8,128)(2,1)} %get-tuple-element.14), calls=%async_computation | async-start | bytes 2097152 | tf_op jit(solution)/shard_map/all_to_all | solution.py:35
  21.7 0.0 copy-done
  21.7 0.0 copy-done.1
  21.8 0.0 copy-start.2
  21.8 1.2 %copy-done.2 = bf16[128,4096]{1,0:T(8,128)(2,1)S(1)} copy-done((bf16[128,4096]{1,0:T(8,128)(2,1)S(1)}, bf16[128,4096]{1,0:T(8,128)(2,1)}, u32[]{:S(2)}) %copy-start.2) | copy-done | bytes 1048600
  23.0 1.9 %prep.1 = (bf16[272,1024]{1,0:T(8,128)(2,1)}, bf16[272,1024]{1,0:T(8,128)(2,1)}, bf16[272,1024]{1,0:T(8,128)(2,1)}, bf16[16,128]{1,0:T(8,128)(2,1)S(1)}) custom-call(s32[1]{0:T(128)} %bitcast.place_ref, bf16[128,4096]{1,0:T(8,128)(2,1)S(1)} %copy-done.1, bf16[128,4096]{1,0:T(8,128)(2,1)S(1)} %copy-done.2, bf16[128,4096]{1,0:T(8,128)(2,1)S(1)} %copy-done), custom_call_target="tpu_custom_call" | custom-call | flops 1048576 | bytes 5242880 | tf_op jit(solution)/shard_map/prep/pallas_call | solution.py:234
  24.9 4.6 %collective-permute-start = (bf16[272,1024]{1,0:T(8,128)(2,1)}, bf16[272,1024]{1,0:T(8,128)(2,1)S(1)}, u32[]{:S(2)}, u32[]{:S(2)}) collective-permute-start(bf16[272,1024]{1,0:T(8,128)(2,1)} %get-tuple-element.16), channel_id=1, source_target_pairs={{0,2},{1,3},{2,0},{3,1},{4,6},{5,7},{6,4},{7,5},{8,10},{9,11},{10,... | collective-permute-start | bytes 1671176 | tf_op jit(solution)/shard_map/ppermute | solution.py:248
  29.5 2.2 %collective-permute-start.1 = (bf16[272,1024]{1,0:T(8,128)(2,1)}, bf16[272,1024]{1,0:T(8,128)(2,1)S(1)}, u32[]{:S(2)}, u32[]{:S(2)}) collective-permute-start(bf16[272,1024]{1,0:T(8,128)(2,1)} %get-tuple-element.17), channel_id=1, source_target_pairs={{0,1},{1,2},{2,3},{3,0},{4,5},{5,6},{6,7},{7,4},{8,9},{9,10},{10,1... | collective-permute-start | bytes 1671176 | tf_op jit(solution)/shard_map/ppermute | solution.py:248
  31.8 4.3 %collective-permute-start.2 = (bf16[272,1024]{1,0:T(8,128)(2,1)}, bf16[272,1024]{1,0:T(8,128)(2,1)S(1)}, u32[]{:S(2)}, u32[]{:S(2)}) collective-permute-start(bf16[272,1024]{1,0:T(8,128)(2,1)} %get-tuple-element.18), channel_id=1, source_target_pairs={{0,3},{1,0},{2,1},{3,2},{4,7},{5,4},{6,5},{7,6},{8,11},{9,8},{10,9... | collective-permute-start | bytes 1671176 | tf_op jit(solution)/shard_map/ppermute | solution.py:248
  36.0 0.8 constant_dynamic-slice_fusion
  36.8 0.1 copy.12.lists_ref
  36.9 0.0 copy-start.4
  36.9 5.2 %collective-permute-done.rest_0_ = bf16[272,1024]{1,0:T(8,128)(2,1)S(1)} collective-permute-done((bf16[272,1024]{1,0:T(8,128)(2,1)}, bf16[272,1024]{1,0:T(8,128)(2,1)S(1)}, u32[]{:S(2)}, u32[]{:S(2)}) %collective-permute-start) | collective-permute-done | bytes 557088 | tf_op jit(solution)/shard_map/ppermute | solution.py:248
  42.1 0.0 copy-start.5
  42.1 12.8 %collective-permute-done.1.rest_1_ = bf16[272,1024]{1,0:T(8,128)(2,1)S(1)} collective-permute-done((bf16[272,1024]{1,0:T(8,128)(2,1)}, bf16[272,1024]{1,0:T(8,128)(2,1)S(1)}, u32[]{:S(2)}, u32[]{:S(2)}) %collective-permute-start.1) | collective-permute-done | bytes 557088 | tf_op jit(solution)/shard_map/ppermute | solution.py:248
  55.0 0.0 copy-start.6
  55.0 0.0 collective-permute-done.2.rest_2_
  55.0 0.0 copy-start.7
  55.0 0.0 all-to-all-done.incoming_ref
  55.0 0.0 copy-done.5
  55.0 0.8 copy-done.6
  55.8 0.2 copy-done.7
  56.0 0.0 copy-done.4
  56.0 7.4 %attention.1 = (bf16[128,4096]{1,0:T(8,128)(2,1)}, bf16[3,128,1024]{2,1,0:T(8,128)(2,1)S(1)}, bf16[128,32,128]{2,1,0:T(8,128)(2,1)}) custom-call(s32[1]{0:T(128)} %bitcast.place_ref, s32[4,16]{1,0:T(4,128)S(1)} %shift-left_or_fusion.slots_ref, s32[4,16]{1,0:T(4,128)S(1)} %copy.12.lists_ref, s32[512]{0:T(512)S(1)} %copy-done.4, ...), custom_call_target="tpu_custom_call" | custom-call | flops 1342177280 | bytes 4194304 | tf_op jit(solution)/shard_map/attention/pallas_call | solution.py:267
  63.4 13.8 %all-to-all-start.1 = ((bf16[128,32,128]{2,1,0:T(8,128)(2,1)}), bf16[128,32,128]{2,1,0:T(8,128)(2,1)S(1)}, u32[]{:S(2)}, u32[]{:S(2)}) async-start(bf16[128,32,128]{2,1,0:T(8,128)(2,1)} %get-tuple-element.22), calls=%async_computation.1 | async-start | bytes 2097152 | tf_op jit(solution)/shard_map/all_to_all | solution.py:35
  77.2 0.1 slice_bitcast_fusion
  77.2 3.2 %collective-permute-start.5 = (bf16[128,1024]{1,0:T(8,128)(2,1)S(1)}, bf16[128,1024]{1,0:T(8,128)(2,1)S(1)}, u32[]{:S(2)}, u32[]{:S(2)}) collective-permute-start(bf16[128,1024]{1,0:T(8,128)(2,1)S(1)} %get-tuple-element.25), channel_id=1, source_target_pairs={{0,1},{1,2},{2,3},{3,0},{4,5},{5,6},{6,7},{7,4},{8,9},{9,10},{10,1... | collective-permute-start | bytes 786440 | tf_op jit(solution)/shard_map/ppermute | solution.py:248
  80.5 3.3 %collective-permute-start.4 = (bf16[128,1024]{1,0:T(8,128)(2,1)S(1)}, bf16[128,1024]{1,0:T(8,128)(2,1)S(1)}, u32[]{:S(2)}, u32[]{:S(2)}) collective-permute-start(bf16[128,1024]{1,0:T(8,128)(2,1)S(1)} %get-tuple-element.26), channel_id=1, source_target_pairs={{0,3},{1,0},{2,1},{3,2},{4,7},{5,4},{6,5},{7,6},{8,11},{9,8},{10,9... | collective-permute-start | bytes 786440 | tf_op jit(solution)/shard_map/ppermute | solution.py:248
  83.8 3.4 %collective-permute-start.3 = (bf16[128,1024]{1,0:T(8,128)(2,1)S(1)}, bf16[128,1024]{1,0:T(8,128)(2,1)S(1)}, u32[]{:S(2)}, u32[]{:S(2)}) collective-permute-start(bf16[128,1024]{1,0:T(8,128)(2,1)S(1)} %get-tuple-element.27), channel_id=1, source_target_pairs={{0,2},{1,3},{2,0},{3,1},{4,6},{5,7},{6,4},{7,5},{8,10},{9,11},{10,... | collective-permute-start | bytes 786440 | tf_op jit(solution)/shard_map/ppermute | solution.py:248
  87.2 0.5 collective-permute-done.5.rest_2_
  87.6 1.7 %collective-permute-done.4.rest_1_ = bf16[128,1024]{1,0:T(8,128)(2,1)S(1)} collective-permute-done((bf16[128,1024]{1,0:T(8,128)(2,1)S(1)}, bf16[128,1024]{1,0:T(8,128)(2,1)S(1)}, u32[]{:S(2)}, u32[]{:S(2)}) %collective-permute-start.4) | collective-permute-done | bytes 262176 | tf_op jit(solution)/shard_map/ppermute | solution.py:248
  89.3 4.5 %collective-permute-done.3.rest_0_ = bf16[128,1024]{1,0:T(8,128)(2,1)S(1)} collective-permute-done((bf16[128,1024]{1,0:T(8,128)(2,1)S(1)}, bf16[128,1024]{1,0:T(8,128)(2,1)S(1)}, u32[]{:S(2)}, u32[]{:S(2)}) %collective-permute-start.3) | collective-permute-done | bytes 262176 | tf_op jit(solution)/shard_map/ppermute | solution.py:248
  93.8 0.0 copy-start.3
  93.8 0.9 place.1
  94.7 14.3 %all-to-all-done.1.terms_ref = bf16[128,32,128]{2,1,0:T(8,128)(2,1)S(1)} async-done(((bf16[128,32,128]{2,1,0:T(8,128)(2,1)}), bf16[128,32,128]{2,1,0:T(8,128)(2,1)S(1)}, u32[]{:S(2)}, u32[]{:S(2)}) %all-to-all-start.1) | async-done | bytes 1048608 | tf_op jit(solution)/shard_map/all_to_all | solution.py:35
  109.0 0.0 copy-done.3
  109.0 1.6 %sum.1 = (bf16[4,16,128]{2,1,0:T(8,128)(2,1)}, bf16[4,16,128]{2,1,0:T(8,128)(2,1)}) custom-call(s32[1,512]{1,0:T(1,128)S(1)} %copy-done.3, bf16[128,32,128]{2,1,0:T(8,128)(2,1)S(1)} %all-to-all-done.1.terms_ref), custom_call_target="tpu_custom_call" | custom-call | tf_op jit(solution)/shard_map/sum/pallas_call | solution.py:303
  (1 shorter events, 0.0 us)
Async XLA Ops:
  2.8 18.9 %copy-start = (bf16[128,4096]{1,0:T(8,128)(2,1)S(1)}, bf16[128,4096]{1,0:T(8,128)(2,1)}, u32[]{:S(2)}) copy-start(bf16[128,4096]{1,0:T(8,128)(2,1)} %o_ref.1) | copy-start | bytes 3145732
  2.8 18.9 %copy-start.1 = (bf16[128,4096]{1,0:T(8,128)(2,1)S(1)}, bf16[128,4096]{1,0:T(8,128)(2,1)}, u32[]{:S(2)}) copy-start(bf16[128,4096]{1,0:T(8,128)(2,1)} %q_ref.3) | copy-start | bytes 3145732
  2.8 52.1 %all-to-all-start = ((bf16[128,32,128]{2,1,0:T(8,128)(2,1)}), bf16[128,32,128]{2,1,0:T(8,128)(2,1)S(1)}, u32[]{:S(2)}, u32[]{:S(2)}) async-start(bf16[128,32,128]{2,1,0:T(8,128)(2,1)} %get-tuple-element.14), calls=%async_computation | async-start | bytes 2097152 | tf_op jit(solution)/shard_map/all_to_all | solution.py:35
  21.8 1.2 %copy-start.2 = (bf16[128,4096]{1,0:T(8,128)(2,1)S(1)}, bf16[128,4096]{1,0:T(8,128)(2,1)}, u32[]{:S(2)}) copy-start(bf16[128,4096]{1,0:T(8,128)(2,1)} %g_ref.3) | copy-start | bytes 3145732
  24.9 17.2 %collective-permute-start = (bf16[272,1024]{1,0:T(8,128)(2,1)}, bf16[272,1024]{1,0:T(8,128)(2,1)S(1)}, u32[]{:S(2)}, u32[]{:S(2)}) collective-permute-start(bf16[272,1024]{1,0:T(8,128)(2,1)} %get-tuple-element.16), channel_id=1, source_target_pairs={{0,2},{1,3},{2,0},{3,1},{4,6},{5,7},{6,4},{7,5},{8,10},{9,11},{10,... | collective-permute-start | bytes 1671176 | tf_op jit(solution)/shard_map/ppermute | solution.py:248
  29.5 25.4 %collective-permute-start.1 = (bf16[272,1024]{1,0:T(8,128)(2,1)}, bf16[272,1024]{1,0:T(8,128)(2,1)S(1)}, u32[]{:S(2)}, u32[]{:S(2)}) collective-permute-start(bf16[272,1024]{1,0:T(8,128)(2,1)} %get-tuple-element.17), channel_id=1, source_target_pairs={{0,1},{1,2},{2,3},{3,0},{4,5},{5,6},{6,7},{7,4},{8,9},{9,10},{10,1... | collective-permute-start | bytes 1671176 | tf_op jit(solution)/shard_map/ppermute | solution.py:248
  31.8 23.2 %collective-permute-start.2 = (bf16[272,1024]{1,0:T(8,128)(2,1)}, bf16[272,1024]{1,0:T(8,128)(2,1)S(1)}, u32[]{:S(2)}, u32[]{:S(2)}) collective-permute-start(bf16[272,1024]{1,0:T(8,128)(2,1)} %get-tuple-element.18), channel_id=1, source_target_pairs={{0,3},{1,0},{2,1},{3,2},{4,7},{5,4},{6,5},{7,6},{8,11},{9,8},{10,9... | collective-permute-start | bytes 1671176 | tf_op jit(solution)/shard_map/ppermute | solution.py:248
  36.9 19.1 %copy-start.4 = (s32[512]{0:T(512)S(1)}, s32[512]{0:T(512)}, u32[]{:S(2)}) copy-start(s32[512]{0:T(512)} %lengths_ref.1) | copy-start | bytes 6148
  42.1 12.8 %copy-start.5 = (bf16[272,1024]{1,0:T(8,128)(2,1)}, bf16[272,1024]{1,0:T(8,128)(2,1)S(1)}, u32[]{:S(2)}) copy-start(bf16[272,1024]{1,0:T(8,128)(2,1)S(1)} %collective-permute-done.rest_0_) | copy-start | bytes 1671172
  55.0 0.8 copy-start.6
  55.0 1.0 copy-start.7
  63.4 45.6 %all-to-all-start.1 = ((bf16[128,32,128]{2,1,0:T(8,128)(2,1)}), bf16[128,32,128]{2,1,0:T(8,128)(2,1)S(1)}, u32[]{:S(2)}, u32[]{:S(2)}) async-start(bf16[128,32,128]{2,1,0:T(8,128)(2,1)} %get-tuple-element.22), calls=%async_computation.1 | async-start | bytes 2097152 | tf_op jit(solution)/shard_map/all_to_all | solution.py:35
  77.2 10.4 %collective-permute-start.5 = (bf16[128,1024]{1,0:T(8,128)(2,1)S(1)}, bf16[128,1024]{1,0:T(8,128)(2,1)S(1)}, u32[]{:S(2)}, u32[]{:S(2)}) collective-permute-start(bf16[128,1024]{1,0:T(8,128)(2,1)S(1)} %get-tuple-element.25), channel_id=1, source_target_pairs={{0,1},{1,2},{2,3},{3,0},{4,5},{5,6},{6,7},{7,4},{8,9},{9,10},{10,1... | collective-permute-start | bytes 786440 | tf_op jit(solution)/shard_map/ppermute | solution.py:248
  80.5 8.9 %collective-permute-start.4 = (bf16[128,1024]{1,0:T(8,128)(2,1)S(1)}, bf16[128,1024]{1,0:T(8,128)(2,1)S(1)}, u32[]{:S(2)}, u32[]{:S(2)}) collective-permute-start(bf16[128,1024]{1,0:T(8,128)(2,1)S(1)} %get-tuple-element.26), channel_id=1, source_target_pairs={{0,3},{1,0},{2,1},{3,2},{4,7},{5,4},{6,5},{7,6},{8,11},{9,8},{10,9... | collective-permute-start | bytes 786440 | tf_op jit(solution)/shard_map/ppermute | solution.py:248
  83.8 10.1 %collective-permute-start.3 = (bf16[128,1024]{1,0:T(8,128)(2,1)S(1)}, bf16[128,1024]{1,0:T(8,128)(2,1)S(1)}, u32[]{:S(2)}, u32[]{:S(2)}) collective-permute-start(bf16[128,1024]{1,0:T(8,128)(2,1)S(1)} %get-tuple-element.27), channel_id=1, source_target_pairs={{0,2},{1,3},{2,0},{3,1},{4,6},{5,7},{6,4},{7,5},{8,10},{9,11},{10,... | collective-permute-start | bytes 786440 | tf_op jit(solution)/shard_map/ppermute | solution.py:248
  93.8 15.2 %copy-start.3 = (s32[1,512]{1,0:T(1,128)S(1)}, s32[1,512]{1,0:T(1,128)}, u32[]{:S(2)}) copy-start(s32[1,512]{1,0:T(1,128)} %get-tuple-element.21.pick_ref) | copy-start | bytes 6148

commit v6 on v5

--- a/solution.py
+++ b/solution.py
@@ -108,35 +108,15 @@
         message_ref[2 * QBLK :, 0:DH] = rows
 
 
-def main_kernel(place_ref, slots_ref, lists_ref, lengths_ref, incoming_ref, q_ref, g_ref, own_delta_ref, *rest):
-    parts, list_len = lists_ref.shape
-    message_refs = rest[: parts - 1]
-    query_grad_ref, dq_ref, out_ref, own_ref, held_ref, own_dq_ref, k_ref, v_ref, terms_ref, bias_ref, own_sems, held_sems, out_sems = rest[parts - 1 :]
+def attend(slots_ref, lists_ref, lengths_ref, incoming_ref, blocks, pieces, out_ref, k_ref, v_ref, terms_ref, bias_ref, sems):
+    list_len = lists_ref.shape[1]
     plen = incoming_ref.shape[1] // 2
-    width = own_ref.shape[1]
-    share = width // DH
+    share = pieces[0][0].shape[1] // DH
     scale = DH ** (-0.5)
     heads = [slice(h * DH, (h + 1) * DH) for h in range(share)]
-    own_cols = pl.ds(pl.multiple_of(place_ref[0] * width, width), width)
-    distances = (0,) + shifts(parts)
-    loads = [
-        [
-            pltpu.make_async_copy(q_ref.at[:, own_cols], own_ref.at[0:QBLK, :], own_sems.at[0]),
-            pltpu.make_async_copy(g_ref.at[:, own_cols], own_ref.at[QBLK : 2 * QBLK, :], own_sems.at[1]),
-        ]
-    ]
-    for i, message_ref in enumerate(message_refs):
-        loads.append([pltpu.make_async_copy(message_ref, held_ref.at[i], held_sems.at[i])])
-    for copies in loads:
-        for copy in copies:
-            copy.start()
     slot_row = lax.broadcasted_iota(jnp.int32, (plen, DH), 0)
-    rows_refs = [own_ref] + [held_ref.at[i] for i in range(parts - 1)]
-    delta_refs = [own_delta_ref] + [held_ref.at[i, 2 * QBLK :, 0:DH] for i in range(parts - 1)]
-    result_refs = [own_dq_ref] + [dq_ref.at[i] for i in range(parts - 1)]
     all_slots = []
-    for j in range(parts):
-        block = lax.rem(place_ref[0] + parts - distances[j], parts)
+    for j, block in enumerate(blocks):
         all_slots.append([slots_ref[block, p] for p in range(list_len)])
         for p, slot in enumerate(all_slots[j]):
             rows = slice(p * plen, (p + 1) * plen)
@@ -145,21 +125,23 @@
             bias_ref[j, rows, :] = jnp.where(slot_row < lengths_ref[lists_ref[block, p]], 0.0, MASKED)
 
     def products(j):
-        for copy in loads[j]:
+        rows_ref, _, _, loads = pieces[j]
+        for copy in loads:
             copy.wait()
-        queries = jnp.concatenate([rows_refs[j][0:QBLK, c] for c in heads], axis=0)
-        grads = jnp.concatenate([rows_refs[j][QBLK : 2 * QBLK, c] for c in heads], axis=0)
+        queries = jnp.concatenate([rows_ref[0:QBLK, c] for c in heads], axis=0)
+        grads = jnp.concatenate([rows_ref[QBLK : 2 * QBLK, c] for c in heads], axis=0)
         scores = lax.dot_general(k_ref[j], queries, NT, preferred_element_type=F32)
         weight_grads = lax.dot_general(v_ref[j], grads, NT, preferred_element_type=F32)
         return queries, grads, scores, weight_grads
 
     stores = []
     ahead = products(0)
-    for j in range(parts):
+    for j in range(len(blocks)):
         queries, grads, scores, weight_grads = ahead
-        if j + 1 < parts:
+        if j + 1 < len(blocks):
             ahead = products(j + 1)
-        delta = delta_refs[j][...].astype(F32)
+        _, delta_ref, result_ref, _ = pieces[j]
+        delta = delta_ref[...].astype(F32)
         delta = delta[:share] + delta[share:]
         delta = jnp.concatenate([delta[h : h + 1] for h in range(share)], axis=1)
         scores = scores * (scale * LOG2E) + jnp.concatenate([bias_ref[j]] * share, axis=1)
@@ -171,18 +153,61 @@
         terms_ref[j, :, 0:plen, :] = key_term.astype(BF16).reshape(list_len, plen, DH)
         terms_ref[j, :, plen : 2 * plen, :] = value_term.astype(BF16).reshape(list_len, plen, DH)
         for p, slot in enumerate(all_slots[j]):
-            copy = pltpu.make_async_copy(terms_ref.at[j, p], out_ref.at[slot], out_sems.at[j, p])
+            copy = pltpu.make_async_copy(terms_ref.at[j, p], out_ref.at[slot], sems.at[j, p])
             copy.start()
             stores.append(copy)
         query_part = lax.dot_general(k_ref[j], score_grads, TN, preferred_element_type=F32) * scale
         for c in heads:
-            result_refs[j][:, c] = query_part[:, c].T.astype(BF16)
-        if j == 0:
-            copy = pltpu.make_async_copy(own_dq_ref, query_grad_ref.at[:, own_cols], own_sems.at[0])
+            result_ref[:, c] = query_part[:, c].T.astype(BF16)
+    return stores
+
+
+def first_kernel(place_ref, slots_ref, lists_ref, lengths_ref, incoming_ref, q_ref, g_ref, own_delta_ref, *rest):
+    held = len(rest) - 13
+    message_refs = rest[:held]
+    query_grad_ref, dq_ref, out_ref, own_ref, held_ref, own_dq_ref = rest[held : held + 6]
+    own_sems, held_sems = rest[held + 6 : held + 8]
+    scratch = rest[held + 8 :]
+    parts = lists_ref.shape[0]
+    share = own_ref.shape[1] // DH
+    width = own_ref.shape[1]
+    own_cols = pl.ds(pl.multiple_of(place_ref[0] * width, width), width)
+    loads = [
+        pltpu.make_async_copy(q_ref.at[:, own_cols], own_ref.at[0:QBLK, :], own_sems.at[0]),
+        pltpu.make_async_copy(g_ref.at[:, own_cols], own_ref.at[QBLK : 2 * QBLK, :], own_sems.at[1]),
+    ]
+    blocks = [place_ref[0]]
+    pieces = [(own_ref, own_delta_ref, own_dq_ref, loads)]
+    for i, message_ref in enumerate(message_refs):
+        load = pltpu.make_async_copy(message_ref, held_ref.at[i], held_sems.at[i])
+        blocks.append(lax.rem(place_ref[0] + parts - shifts(parts)[i], parts))
+        pieces.append((held_ref.at[i], held_ref.at[i, 2 * QBLK : 2 * QBLK + 2 * share, 0:DH], dq_ref.at[i], [load]))
+    for piece in pieces:
+        for copy in piece[3]:
             copy.start()
-            stores.append(copy)
-    for copy in stores:
-        copy.wait()
+    stores = attend(slots_ref, lists_ref, lengths_ref, incoming_ref, blocks, pieces, out_ref, *scratch)
+    copy = pltpu.make_async_copy(own_dq_ref, query_grad_ref.at[:, own_cols], own_sems.at[0])
+    copy.start()
+    for store in stores:
+        store.wait()
+    copy.wait()
+
+
+def last_kernel(place_ref, slots_ref, lists_ref, lengths_ref, incoming_ref, *rest):
+    late = len(rest) - 8
+    message_refs = rest[:late]
+    _, dq_ref, out_ref = rest[late : late + 3]
+    scratch = rest[late + 3 :]
+    parts = lists_ref.shape[0]
+    share = message_refs[0].shape[1] // DH
+    blocks, pieces = [], []
+    for i, message_ref in enumerate(message_refs):
+        by = shifts(parts)[parts - 1 - late + i]
+        blocks.append(lax.rem(place_ref[0] + parts - by, parts))
+        pieces.append((message_ref, message_ref.at[2 * QBLK : 2 * QBLK + 2 * share, 0:DH], dq_ref.at[i], []))
+    stores = attend(slots_ref, lists_ref, lengths_ref, incoming_ref, blocks, pieces, out_ref, *scratch)
+    for store in stores:
+        store.wait()
 
 
 def place_kernel(place_ref, own_ref, *rest):
@@ -264,30 +289,68 @@
     keys = list_len * plen
     pairs = parts * QBLK * share * keys
     full_shape = jax.ShapeDtypeStruct((rows, columns), BF16)
+    piece_shape = (QBLK, width)
+    early = parts // 2 - 1
+    late = parts - 1 - early
+
+    def scratch(blocks):
+        return [
+            pltpu.VMEM((blocks, keys, DH), BF16),
+            pltpu.VMEM((blocks, keys, DH), BF16),
+            pltpu.VMEM((blocks, list_len, 2 * plen, DH), BF16),
+            pltpu.VMEM((blocks, keys, DH), F32),
+            pltpu.SemaphoreType.DMA((blocks, list_len)),
+        ]
+
+    def cost(blocks):
+        return pl.CostEstimate(
+            flops=10 * pairs * DH * blocks // parts,
+            bytes_accessed=8 * rows * width * blocks,
+            transcendentals=pairs * blocks // parts,
+        )
+
     query_grad, query_parts, outgoing_grads = pl.pallas_call(
-        main_kernel,
-        out_shape=[full_shape, jax.ShapeDtypeStruct((parts - 1, QBLK, width), BF16), all_shape],
-        in_specs=[smem()] * 4 + [vmem(), hbm(), hbm(), vmem()] + [hbm()] * (parts - 1),
+        first_kernel,
+        out_shape=[full_shape, jax.ShapeDtypeStruct((early,) + piece_shape, BF16), all_shape],
+        in_specs=[smem()] * 4 + [vmem(), hbm(), hbm(), vmem()] + [hbm()] * early,
         out_specs=[hbm(), vmem(), hbm()],
         scratch_shapes=[
             pltpu.VMEM((2 * QBLK, width), BF16),
-            pltpu.VMEM((parts - 1,) + message.shape, BF16),
-            pltpu.VMEM((QBLK, width), BF16),
-            pltpu.VMEM((parts, keys, DH), BF16),
-            pltpu.VMEM((parts, keys, DH), BF16),
-            pltpu.VMEM((parts, list_len, 2 * plen, DH), BF16),
-            pltpu.VMEM((parts, keys, DH), F32),
+            pltpu.VMEM((early,) + message.shape, BF16),
+            pltpu.VMEM(piece_shape, BF16),
             pltpu.SemaphoreType.DMA((2,)),
-            pltpu.SemaphoreType.DMA((parts - 1,)),
-            pltpu.SemaphoreType.DMA((parts, list_len)),
-        ],
-        compiler_params=params(),
-        cost_estimate=pl.CostEstimate(flops=10 * pairs * DH, bytes_accessed=8 * rows * columns, transcendentals=pairs),
-        name="attention",
-    )(place, own_slots, own_lists, passage_lengths, incoming, in_hbm(queries), in_hbm(grad_out), own_delta, *[in_hbm(piece) for piece in messages])
+            pltpu.SemaphoreType.DMA((early,)),
+        ]
+        + scratch(early + 1),
+        compiler_params=params(),
+        cost_estimate=cost(early + 1),
+        name="attention_first",
+    )(
+        place,
+        own_slots,
+        own_lists,
+        passage_lengths,
+        incoming,
+        in_hbm(queries),
+        in_hbm(grad_out),
+        own_delta,
+        *[in_hbm(piece) for piece in messages[:early]],
+    )
+    late_parts, outgoing_grads = pl.pallas_call(
+        last_kernel,
+        out_shape=[jax.ShapeDtypeStruct((late,) + piece_shape, BF16), all_shape],
+        in_specs=[smem()] * 4 + [vmem()] * (1 + late) + [hbm()],
+        out_specs=[vmem(), hbm()],
+        scratch_shapes=scratch(late),
+        input_output_aliases={5 + late: 1},
+        compiler_params=params(),
+        cost_estimate=cost(late),
+        name="attention_last",
+    )(place, own_slots, own_lists, passage_lengths, incoming, *messages[early:], outgoing_grads)
 
     returned = exchange(outgoing_grads)
-    query_parts = [shift(query_parts[j], parts - by) for j, by in enumerate(shifts(parts))]
+    query_parts = [query_parts[i] for i in range(early)] + [late_parts[i] for i in range(late)]
+    query_parts = [shift(piece, parts - by) for piece, by in zip(query_parts, shifts(parts))]
     query_grad = pl.pallas_call(
         place_kernel,
         out_shape=full_shape,

time: 111 us -> 106 us (0.955)
  starting transfers between devices: 53.7 us -> 50.3 us
  waiting for transfers between devices: 39 us -> 37.7 us
    ppermute x6, waiting for transfers between devices: 24.7 us -> 12.1 us  [shift(): lax.ppermute(piece, 'tensor', [(i, (i + by) % parts) for i in range(parts)])]
    all_to_all x2, waiting for transfers between devices: 14.3 us -> 25.6 us  [exchange(): lax.all_to_all(pieces, EXCHANGE_AXES, split_axis=0, concat_axis=0, tiled=...]
    all_to_all x2, starting transfers between devices: 32.7 us -> 29.4 us  [exchange(): lax.all_to_all(pieces, EXCHANGE_AXES, split_axis=0, concat_axis=0, tiled=...]
    unnamed x17 -> x11, local copies, waits for them, and re-layouts: 2.3 us -> 1.32 us
    pallas_call x1 -> x2, Pallas kernels: 7.39 us -> 8.1 us  [the longest x1 4.77 us: local(): pl.pallas_call(first_kernel, out_shape=[full_shape, jax.ShapeDtypeStruct(...]
  transfers between devices with their start and end apart: 8 -> 8, of which waited for: 6 -> 6; matrix products, arithmetic and copies ran while one was open for 1% -> 1% of each run, Pallas kernels for 3% -> 7%
where the time goes in v6:
time: 106 us
  starting transfers between devices  50.3 us (47%)
  waiting for transfers between devices  37.7 us (36%)
  Pallas kernels  14.6 us (14%)
  local copies, waits for them, and re-layouts  2.13 us (2%)
    all_to_all x2, starting transfers between devices, exchange(): lax.all_to_all(pieces, EXCHANGE_AXES, split_axis=0, concat_axis=0, tiled=...  29.4 us
    all_to_all x2, waiting for transfers between devices, exchange(): lax.all_to_all(pieces, EXCHANGE_AXES, split_axis=0, concat_axis=0, tiled=...  25.6 us
    ppermute x6, starting transfers between devices, shift(): lax.ppermute(piece, 'tensor', [(i, (i + by) % parts) for i in range(parts)])  20.9 us
    ppermute x6, waiting for transfers between devices, shift(): lax.ppermute(piece, 'tensor', [(i, (i + by) % parts) for i in range(parts)])  12.1 us
    pallas_call x1, Pallas kernels, local(): pl.pallas_call(first_kernel, out_shape=[full_shape, jax.ShapeDtypeStruct(...  4.77 us
    pallas_call x1, Pallas kernels, local(): pl.pallas_call(last_kernel, out_shape=[jax.ShapeDtypeStruct((late,) + pie...  3.32 us
    pallas_call x1, Pallas kernels, local(): pl.pallas_call(send_kernel, out_shape=[all_shape, jax.ShapeDtypeStruct((1...  2.2 us
  transfers between devices with their start and end apart: 8, of which 6 were waited for; matrix products, arithmetic and copies ran while one was open for 1% of the time, Pallas kernels for 7%

profile of v6, /device:TPU:1, one launch (start us, length us, event | category | flops | bytes accessed | tf_op | source)
XLA Modules:
  0.0 105.6 jit_solution(1953160243059402658)
XLA Ops:
  0.6 2.2 %send.1 = (bf16[128,32,128]{2,1,0:T(8,128)(2,1)}, s32[1,512]{1,0:T(1,128)}) custom-call(s32[1]{0:T(128)} %bitcast.1.base_ref, s32[16,512]{1,0:T(8,128)} %bitcast.9, bf16[4,16,128]{2,1,0:T(8,128)(2,1)} %keys_ref.1, bf16[4,16,128]{2,1,0:T(8,128)(2,1)} %values_ref.1), custom_call_target="tpu_custom_call" | custom-call | tf_op jit(solution)/shard_map/send/pallas_call | solution.py:276
  2.8 0.0 copy-start
  2.8 0.0 copy-start.1
  2.8 18.9 %all-to-all-start = ((bf16[128,32,128]{2,1,0:T(8,128)(2,1)}), bf16[128,32,128]{2,1,0:T(8,128)(2,1)S(1)}, u32[]{:S(2)}, u32[]{:S(2)}) async-start(bf16[128,32,128]{2,1,0:T(8,128)(2,1)} %get-tuple-element.16), calls=%async_computation | async-start | bytes 2097152 | tf_op jit(solution)/shard_map/all_to_all | solution.py:35
  21.7 0.0 copy-done
  21.7 0.0 copy-done.1
  21.8 0.0 copy-start.2
  21.8 1.2 %copy-done.2 = bf16[128,4096]{1,0:T(8,128)(2,1)S(1)} copy-done((bf16[128,4096]{1,0:T(8,128)(2,1)S(1)}, bf16[128,4096]{1,0:T(8,128)(2,1)}, u32[]{:S(2)}) %copy-start.2) | copy-done | bytes 1048600
  23.0 1.8 %prep.1 = (bf16[272,1024]{1,0:T(8,128)(2,1)}, bf16[272,1024]{1,0:T(8,128)(2,1)}, bf16[272,1024]{1,0:T(8,128)(2,1)}, bf16[16,128]{1,0:T(8,128)(2,1)S(1)}) custom-call(s32[1]{0:T(128)} %bitcast.place_ref, bf16[128,4096]{1,0:T(8,128)(2,1)S(1)} %copy-done, bf16[128,4096]{1,0:T(8,128)(2,1)S(1)} %copy-done.1, bf16[128,4096]{1,0:T(8,128)(2,1)S(1)} %copy-done.2), custom_call_target="tpu_custom_call" | custom-call | flops 1048576 | bytes 5242880 | tf_op jit(solution)/shard_map/prep/pallas_call | solution.py:259
  24.8 4.6 %collective-permute-start = (bf16[272,1024]{1,0:T(8,128)(2,1)}, bf16[272,1024]{1,0:T(8,128)(2,1)}, u32[]{:S(2)}, u32[]{:S(2)}) collective-permute-start(bf16[272,1024]{1,0:T(8,128)(2,1)} %get-tuple-element.18), channel_id=1, source_target_pairs={{0,2},{1,3},{2,0},{3,1},{4,6},{5,7},{6,4},{7,5},{8,10},{9,11},{10,... | collective-permute-start | bytes 1671176 | tf_op jit(solution)/shard_map/ppermute | solution.py:273
  29.5 2.2 %collective-permute-start.2 = (bf16[272,1024]{1,0:T(8,128)(2,1)}, bf16[272,1024]{1,0:T(8,128)(2,1)S(1)}, u32[]{:S(2)}, u32[]{:S(2)}) collective-permute-start(bf16[272,1024]{1,0:T(8,128)(2,1)} %get-tuple-element.21), channel_id=1, source_target_pairs={{0,1},{1,2},{2,3},{3,0},{4,5},{5,6},{6,7},{7,4},{8,9},{9,10},{10,1... | collective-permute-start | bytes 1671176 | tf_op jit(solution)/shard_map/ppermute | solution.py:273
  31.7 4.3 %collective-permute-start.3 = (bf16[272,1024]{1,0:T(8,128)(2,1)}, bf16[272,1024]{1,0:T(8,128)(2,1)S(1)}, u32[]{:S(2)}, u32[]{:S(2)}) collective-permute-start(bf16[272,1024]{1,0:T(8,128)(2,1)} %get-tuple-element.22), channel_id=1, source_target_pairs={{0,3},{1,0},{2,1},{3,2},{4,7},{5,4},{6,5},{7,6},{8,11},{9,8},{10,9... | collective-permute-start | bytes 1671176 | tf_op jit(solution)/shard_map/ppermute | solution.py:273
  36.0 0.8 constant_dynamic-slice_fusion
  36.8 0.1 copy.13.lists_ref
  36.8 0.0 copy-start.3
  36.9 5.3 %collective-permute-done.rest_0_ = bf16[272,1024]{1,0:T(8,128)(2,1)} collective-permute-done((bf16[272,1024]{1,0:T(8,128)(2,1)}, bf16[272,1024]{1,0:T(8,128)(2,1)}, u32[]{:S(2)}, u32[]{:S(2)}) %collective-permute-start) | collective-permute-done | bytes 557088 | tf_op jit(solution)/shard_map/ppermute | solution.py:273
  42.2 11.4 %all-to-all-done.incoming_ref = bf16[128,32,128]{2,1,0:T(8,128)(2,1)S(1)} async-done(((bf16[128,32,128]{2,1,0:T(8,128)(2,1)}), bf16[128,32,128]{2,1,0:T(8,128)(2,1)S(1)}, u32[]{:S(2)}, u32[]{:S(2)}) %all-to-all-start) | async-done | bytes 1048608 | tf_op jit(solution)/shard_map/all_to_all | solution.py:35
  53.5 0.0 copy-done.3
  53.5 4.8 %attention_first.1 = (bf16[128,4096]{1,0:T(8,128)(2,1)}, bf16[1,128,1024]{2,1,0:T(8,128)(2,1)S(1)}, bf16[128,32,128]{2,1,0:T(8,128)(2,1)}) custom-call(s32[1]{0:T(128)} %bitcast.place_ref, s32[4,16]{1,0:T(4,128)S(1)} %shift-left_or_fusion.slots_ref, s32[4,16]{1,0:T(4,128)S(1)} %copy.13.lists_ref, s32[512]{0:T(512)S(1)} %copy-done.3, ...), custom_call_target="tpu_custom_call" | custom-call | flops 671088640 | bytes 2097152 | tf_op jit(solution)/shard_map/attention_first/pallas_call | solution.py:312
  58.3 0.0 collective-permute-done.2.rest_0_
  58.3 0.0 collective-permute-done.3.rest_1_
  58.3 3.3 %attention_last.1 = (bf16[2,128,1024]{2,1,0:T(8,128)(2,1)S(1)}, bf16[128,32,128]{2,1,0:T(8,128)(2,1)}) custom-call(s32[1]{0:T(128)} %bitcast.place_ref, s32[4,16]{1,0:T(4,128)S(1)} %shift-left_or_fusion.slots_ref, s32[4,16]{1,0:T(4,128)S(1)} %copy.13.lists_ref, s32[512]{0:T(512)S(1)} %copy-done.3, ...), custom_call_target="tpu_custom_call", output_to_operand_aliasing={{1}: (7, {})} | custom-call | flops 671088640 | bytes 2097152 | tf_op jit(solution)/shard_map/attention_last/pallas_call | solution.py:339
  61.7 10.5 %all-to-all-start.1 = ((bf16[128,32,128]{2,1,0:T(8,128)(2,1)}), bf16[128,32,128]{2,1,0:T(8,128)(2,1)S(1)}, u32[]{:S(2)}, u32[]{:S(2)}) async-start(bf16[128,32,128]{2,1,0:T(8,128)(2,1)} %get-tuple-element.26), calls=%async_computation.1 | async-start | bytes 2097152 | tf_op jit(solution)/shard_map/all_to_all | solution.py:35
  72.2 3.0 %collective-permute-start.5 = (bf16[128,1024]{1,0:T(8,128)(2,1)S(1)}, bf16[128,1024]{1,0:T(8,128)(2,1)S(1)}, u32[]{:S(2)}, u32[]{:S(2)}) collective-permute-start(bf16[128,1024]{1,0:T(8,128)(2,1)S(1)} %get-tuple-element.29), channel_id=1, source_target_pairs={{0,1},{1,2},{2,3},{3,0},{4,5},{5,6},{6,7},{7,4},{8,9},{9,10},{10,1... | collective-permute-start | bytes 786440 | tf_op jit(solution)/shard_map/ppermute | solution.py:273
  75.3 3.5 %collective-permute-start.4 = (bf16[128,1024]{1,0:T(8,128)(2,1)S(1)}, bf16[128,1024]{1,0:T(8,128)(2,1)S(1)}, u32[]{:S(2)}, u32[]{:S(2)}) collective-permute-start(bf16[128,1024]{1,0:T(8,128)(2,1)S(1)} %get-tuple-element.30), channel_id=1, source_target_pairs={{0,3},{1,0},{2,1},{3,2},{4,7},{5,4},{6,5},{7,6},{8,11},{9,8},{10,9... | collective-permute-start | bytes 786440 | tf_op jit(solution)/shard_map/ppermute | solution.py:273
  78.7 3.3 %collective-permute-start.1 = (bf16[128,1024]{1,0:T(8,128)(2,1)S(1)}, bf16[128,1024]{1,0:T(8,128)(2,1)S(1)}, u32[]{:S(2)}, u32[]{:S(2)}) collective-permute-start(bf16[128,1024]{1,0:T(8,128)(2,1)S(1)} %bitcast.8), channel_id=1, source_target_pairs={{0,2},{1,3},{2,0},{3,1},{4,6},{5,7},{6,4},{7,5},{8,10},{9,11},{10,... | collective-permute-start | bytes 786440 | tf_op jit(solution)/shard_map/ppermute | solution.py:273
  82.0 0.6 collective-permute-done.5.rest_2_
  82.6 1.5 %collective-permute-done.4.rest_1_ = bf16[128,1024]{1,0:T(8,128)(2,1)S(1)} collective-permute-done((bf16[128,1024]{1,0:T(8,128)(2,1)S(1)}, bf16[128,1024]{1,0:T(8,128)(2,1)S(1)}, u32[]{:S(2)}, u32[]{:S(2)}) %collective-permute-start.4) | collective-permute-done | bytes 262176 | tf_op jit(solution)/shard_map/ppermute | solution.py:273
  84.1 4.7 %collective-permute-done.1.rest_0_ = bf16[128,1024]{1,0:T(8,128)(2,1)S(1)} collective-permute-done((bf16[128,1024]{1,0:T(8,128)(2,1)S(1)}, bf16[128,1024]{1,0:T(8,128)(2,1)S(1)}, u32[]{:S(2)}, u32[]{:S(2)}) %collective-permute-start.1) | collective-permute-done | bytes 262176 | tf_op jit(solution)/shard_map/ppermute | solution.py:273
  88.8 0.0 copy-start.4
  88.8 0.9 place.1
  89.7 14.3 %all-to-all-done.1.terms_ref = bf16[128,32,128]{2,1,0:T(8,128)(2,1)S(1)} async-done(((bf16[128,32,128]{2,1,0:T(8,128)(2,1)}), bf16[128,32,128]{2,1,0:T(8,128)(2,1)S(1)}, u32[]{:S(2)}, u32[]{:S(2)}) %all-to-all-start.1) | async-done | bytes 1048608 | tf_op jit(solution)/shard_map/all_to_all | solution.py:35
  104.0 0.0 copy-done.4
  104.0 1.6 %sum.1 = (bf16[4,16,128]{2,1,0:T(8,128)(2,1)}, bf16[4,16,128]{2,1,0:T(8,128)(2,1)}) custom-call(s32[1,512]{1,0:T(1,128)S(1)} %copy-done.4, bf16[128,32,128]{2,1,0:T(8,128)(2,1)S(1)} %all-to-all-done.1.terms_ref), custom_call_target="tpu_custom_call" | custom-call | tf_op jit(solution)/shard_map/sum/pallas_call | solution.py:366
  (2 shorter events, 0.1 us)
Async XLA Ops:
  2.8 18.9 %copy-start = (bf16[128,4096]{1,0:T(8,128)(2,1)S(1)}, bf16[128,4096]{1,0:T(8,128)(2,1)}, u32[]{:S(2)}) copy-start(bf16[128,4096]{1,0:T(8,128)(2,1)} %q_ref.3) | copy-start | bytes 3145732
  2.8 18.9 %copy-start.1 = (bf16[128,4096]{1,0:T(8,128)(2,1)S(1)}, bf16[128,4096]{1,0:T(8,128)(2,1)}, u32[]{:S(2)}) copy-start(bf16[128,4096]{1,0:T(8,128)(2,1)} %g_ref.3) | copy-start | bytes 3145732
  2.8 50.7 %all-to-all-start = ((bf16[128,32,128]{2,1,0:T(8,128)(2,1)}), bf16[128,32,128]{2,1,0:T(8,128)(2,1)S(1)}, u32[]{:S(2)}, u32[]{:S(2)}) async-start(bf16[128,32,128]{2,1,0:T(8,128)(2,1)} %get-tuple-element.16), calls=%async_computation | async-start | bytes 2097152 | tf_op jit(solution)/shard_map/all_to_all | solution.py:35
  21.8 1.2 %copy-start.2 = (bf16[128,4096]{1,0:T(8,128)(2,1)S(1)}, bf16[128,4096]{1,0:T(8,128)(2,1)}, u32[]{:S(2)}) copy-start(bf16[128,4096]{1,0:T(8,128)(2,1)} %o_ref.1) | copy-start | bytes 3145732
  24.8 17.4 %collective-permute-start = (bf16[272,1024]{1,0:T(8,128)(2,1)}, bf16[272,1024]{1,0:T(8,128)(2,1)}, u32[]{:S(2)}, u32[]{:S(2)}) collective-permute-start(bf16[272,1024]{1,0:T(8,128)(2,1)} %get-tuple-element.18), channel_id=1, source_target_pairs={{0,2},{1,3},{2,0},{3,1},{4,6},{5,7},{6,4},{7,5},{8,10},{9,11},{10,... | collective-permute-start | bytes 1671176 | tf_op jit(solution)/shard_map/ppermute | solution.py:273
  29.5 28.9 %collective-permute-start.2 = (bf16[272,1024]{1,0:T(8,128)(2,1)}, bf16[272,1024]{1,0:T(8,128)(2,1)S(1)}, u32[]{:S(2)}, u32[]{:S(2)}) collective-permute-start(bf16[272,1024]{1,0:T(8,128)(2,1)} %get-tuple-element.21), channel_id=1, source_target_pairs={{0,1},{1,2},{2,3},{3,0},{4,5},{5,6},{6,7},{7,4},{8,9},{9,10},{10,1... | collective-permute-start | bytes 1671176 | tf_op jit(solution)/shard_map/ppermute | solution.py:273
  31.7 26.6 %collective-permute-start.3 = (bf16[272,1024]{1,0:T(8,128)(2,1)}, bf16[272,1024]{1,0:T(8,128)(2,1)S(1)}, u32[]{:S(2)}, u32[]{:S(2)}) collective-permute-start(bf16[272,1024]{1,0:T(8,128)(2,1)} %get-tuple-element.22), channel_id=1, source_target_pairs={{0,3},{1,0},{2,1},{3,2},{4,7},{5,4},{6,5},{7,6},{8,11},{9,8},{10,9... | collective-permute-start | bytes 1671176 | tf_op jit(solution)/shard_map/ppermute | solution.py:273
  36.8 16.7 %copy-start.3 = (s32[512]{0:T(512)S(1)}, s32[512]{0:T(512)}, u32[]{:S(2)}) copy-start(s32[512]{0:T(512)} %lengths_ref.3) | copy-start | bytes 6148
  61.7 42.3 %all-to-all-start.1 = ((bf16[128,32,128]{2,1,0:T(8,128)(2,1)}), bf16[128,32,128]{2,1,0:T(8,128)(2,1)S(1)}, u32[]{:S(2)}, u32[]{:S(2)}) async-start(bf16[128,32,128]{2,1,0:T(8,128)(2,1)} %get-tuple-element.26), calls=%async_computation.1 | async-start | bytes 2097152 | tf_op jit(solution)/shard_map/all_to_all | solution.py:35
  72.2 10.4 %collective-permute-start.5 = (bf16[128,1024]{1,0:T(8,128)(2,1)S(1)}, bf16[128,1024]{1,0:T(8,128)(2,1)S(1)}, u32[]{:S(2)}, u32[]{:S(2)}) collective-permute-start(bf16[128,1024]{1,0:T(8,128)(2,1)S(1)} %get-tuple-element.29), channel_id=1, source_target_pairs={{0,1},{1,2},{2,3},{3,0},{4,5},{5,6},{6,7},{7,4},{8,9},{9,10},{10,1... | collective-permute-start | bytes 786440 | tf_op jit(solution)/shard_map/ppermute | solution.py:273
  75.3 8.9 %collective-permute-start.4 = (bf16[128,1024]{1,0:T(8,128)(2,1)S(1)}, bf16[128,1024]{1,0:T(8,128)(2,1)S(1)}, u32[]{:S(2)}, u32[]{:S(2)}) collective-permute-start(bf16[128,1024]{1,0:T(8,128)(2,1)S(1)} %get-tuple-element.30), channel_id=1, source_target_pairs={{0,3},{1,0},{2,1},{3,2},{4,7},{5,4},{6,5},{7,6},{8,11},{9,8},{10,9... | collective-permute-start | bytes 786440 | tf_op jit(solution)/shard_map/ppermute | solution.py:273
  78.7 10.1 %collective-permute-start.1 = (bf16[128,1024]{1,0:T(8,128)(2,1)S(1)}, bf16[128,1024]{1,0:T(8,128)(2,1)S(1)}, u32[]{:S(2)}, u32[]{:S(2)}) collective-permute-start(bf16[128,1024]{1,0:T(8,128)(2,1)S(1)} %bitcast.8), channel_id=1, source_target_pairs={{0,2},{1,3},{2,0},{3,1},{4,6},{5,7},{6,4},{7,5},{8,10},{9,11},{10,... | collective-permute-start | bytes 786440 | tf_op jit(solution)/shard_map/ppermute | solution.py:273
  88.8 15.2 %copy-start.4 = (s32[1,512]{1,0:T(1,128)S(1)}, s32[1,512]{1,0:T(1,128)}, u32[]{:S(2)}) copy-start(s32[1,512]{1,0:T(1,128)} %get-tuple-element.25.pick_ref) | copy-start | bytes 6148

commit v7 on v6

--- a/solution.py
+++ b/solution.py
@@ -80,32 +80,32 @@
         out_ref[slot_of(n)] = tile
 
 
-def prep_kernel(place_ref, q_ref, g_ref, o_ref, *rest):
-    *message_refs, own_ref, delta_ref = rest
+def cut_kernel(place_ref, q_ref, g_ref, *message_refs):
     parts = len(message_refs) + 1
     width = q_ref.shape[1] // parts
-    share = width // DH
+    for by, message_ref in zip(shifts(parts), message_refs):
+        cols = pl.ds(pl.multiple_of(lax.rem(place_ref[0] + by, parts) * width, width), width)
+        message_ref[0:QBLK, :] = q_ref[:, cols]
+        message_ref[QBLK : 2 * QBLK, :] = g_ref[:, cols]
+
+
+def delta_kernel(place_ref, g_ref, o_ref, *rest):
+    *tile_refs, delta_ref = rest
+    parts = len(tile_refs)
+    heads = g_ref.shape[1] // DH
+    share = heads // parts
     lane = lax.broadcasted_iota(jnp.int32, (QBLK, DH), 1)
     delta = jnp.zeros((QBLK, DH), F32)
-    for h in range(parts * share):
+    for h in range(heads):
         cols = slice(h * DH, (h + 1) * DH)
         term = jnp.sum(g_ref[:, cols].astype(F32) * o_ref[:, cols].astype(F32), axis=1, keepdims=True)
         delta = jnp.where(lane == h, term, delta)
     delta_ref[...] = delta.T
-    for j in range(parts):
-        to = lax.rem(place_ref[0] + (0 if j == 0 else shifts(parts)[j - 1]), parts)
+    for by, tile_ref in zip((0,) + shifts(parts), tile_refs):
+        to = lax.rem(place_ref[0] + by, parts)
         rows = delta_ref[pl.ds(pl.multiple_of(to * share, share), share), :]
         high = rows.astype(BF16).astype(F32)
-        rows = jnp.concatenate([high, rows - high], axis=0).astype(BF16)
-        if j == 0:
-            own_ref[...] = rows
-            continue
-        message_ref = message_refs[j - 1]
-        cols = pl.ds(pl.multiple_of(to * width, width), width)
-        message_ref[0:QBLK, :] = q_ref[:, cols]
-        message_ref[QBLK : 2 * QBLK, :] = g_ref[:, cols]
-        message_ref[2 * QBLK :, :] = jnp.zeros((2 * share, width), BF16)
-        message_ref[2 * QBLK :, 0:DH] = rows
+        tile_ref[...] = jnp.concatenate([high, rows - high], axis=0).astype(BF16)
 
 
 def attend(slots_ref, lists_ref, lengths_ref, incoming_ref, blocks, pieces, out_ref, k_ref, v_ref, terms_ref, bias_ref, sems):
@@ -163,28 +163,27 @@
 
 
 def first_kernel(place_ref, slots_ref, lists_ref, lengths_ref, incoming_ref, q_ref, g_ref, own_delta_ref, *rest):
-    held = len(rest) - 13
-    message_refs = rest[:held]
-    query_grad_ref, dq_ref, out_ref, own_ref, held_ref, own_dq_ref = rest[held : held + 6]
-    own_sems, held_sems = rest[held + 6 : held + 8]
-    scratch = rest[held + 8 :]
+    early = (len(rest) - 12) // 2
+    message_refs, delta_refs = rest[:early], rest[early : 2 * early]
+    query_grad_ref, dq_ref, out_ref, own_ref, own_dq_ref, own_sems, held_ref, held_sems = rest[2 * early : 2 * early + 8]
+    scratch = rest[2 * early + 8 :]
     parts = lists_ref.shape[0]
-    share = own_ref.shape[1] // DH
     width = own_ref.shape[1]
     own_cols = pl.ds(pl.multiple_of(place_ref[0] * width, width), width)
     loads = [
         pltpu.make_async_copy(q_ref.at[:, own_cols], own_ref.at[0:QBLK, :], own_sems.at[0]),
         pltpu.make_async_copy(g_ref.at[:, own_cols], own_ref.at[QBLK : 2 * QBLK, :], own_sems.at[1]),
     ]
-    blocks = [place_ref[0]]
-    pieces = [(own_ref, own_delta_ref, own_dq_ref, loads)]
-    for i, message_ref in enumerate(message_refs):
-        load = pltpu.make_async_copy(message_ref, held_ref.at[i], held_sems.at[i])
+    blocks, pieces = [], []
+    for i in range(early):
+        load = pltpu.make_async_copy(message_refs[i], held_ref.at[i], held_sems.at[i])
+        load.start()
         blocks.append(lax.rem(place_ref[0] + parts - shifts(parts)[i], parts))
-        pieces.append((held_ref.at[i], held_ref.at[i, 2 * QBLK : 2 * QBLK + 2 * share, 0:DH], dq_ref.at[i], [load]))
-    for piece in pieces:
-        for copy in piece[3]:
-            copy.start()
+        pieces.append((held_ref.at[i], delta_refs[i], dq_ref.at[i], [load]))
+    for load in loads:
+        load.start()
+    blocks.append(place_ref[0])
+    pieces.append((own_ref, own_delta_ref, own_dq_ref, loads))
     stores = attend(slots_ref, lists_ref, lengths_ref, incoming_ref, blocks, pieces, out_ref, *scratch)
     copy = pltpu.make_async_copy(own_dq_ref, query_grad_ref.at[:, own_cols], own_sems.at[0])
     copy.start()
@@ -194,17 +193,18 @@
 
 
 def last_kernel(place_ref, slots_ref, lists_ref, lengths_ref, incoming_ref, *rest):
-    late = len(rest) - 8
-    message_refs = rest[:late]
-    _, dq_ref, out_ref = rest[late : late + 3]
-    scratch = rest[late + 3 :]
+    late = (len(rest) - 10) // 2
+    message_refs, delta_refs = rest[:late], rest[late : 2 * late]
+    _, dq_ref, out_ref, held_ref, held_sems = rest[2 * late : 2 * late + 5]
+    scratch = rest[2 * late + 5 :]
     parts = lists_ref.shape[0]
-    share = message_refs[0].shape[1] // DH
     blocks, pieces = [], []
-    for i, message_ref in enumerate(message_refs):
+    for i in range(late):
+        load = pltpu.make_async_copy(message_refs[i], held_ref.at[i], held_sems.at[i])
+        load.start()
         by = shifts(parts)[parts - 1 - late + i]
         blocks.append(lax.rem(place_ref[0] + parts - by, parts))
-        pieces.append((message_ref, message_ref.at[2 * QBLK : 2 * QBLK + 2 * share, 0:DH], dq_ref.at[i], []))
+        pieces.append((held_ref.at[i], delta_refs[i], dq_ref.at[i], [load]))
     stores = attend(slots_ref, lists_ref, lengths_ref, incoming_ref, blocks, pieces, out_ref, *scratch)
     for store in stores:
         store.wait()
@@ -254,18 +254,26 @@
     all_shape = jax.ShapeDtypeStruct((shards, 2 * plen, DH), BF16)
 
     share = width // DH
-    message = jax.ShapeDtypeStruct((2 * QBLK + 2 * share, width), BF16)
-    own_shape = jax.ShapeDtypeStruct((2 * share, QBLK), BF16)
-    *messages, own_delta = pl.pallas_call(
-        prep_kernel,
-        out_shape=[message] * (parts - 1) + [own_shape],
-        in_specs=[smem(), vmem(), vmem(), vmem()],
+    message = jax.ShapeDtypeStruct((2 * QBLK, width), BF16)
+    messages = pl.pallas_call(
+        cut_kernel,
+        out_shape=[message] * (parts - 1),
+        in_specs=[smem(), vmem(), vmem()],
+        out_specs=[vmem()] * (parts - 1),
+        compiler_params=params(),
+        cost_estimate=pl.CostEstimate(flops=0, bytes_accessed=8 * rows * columns, transcendentals=0),
+        name="cut",
+    )(place, queries, grad_out)
+    own_delta, *deltas = pl.pallas_call(
+        delta_kernel,
+        out_shape=[jax.ShapeDtypeStruct((2 * share, QBLK), BF16)] * parts,
+        in_specs=[smem(), vmem(), vmem()],
         out_specs=[vmem()] * parts,
         scratch_shapes=[pltpu.VMEM((DH, QBLK), F32)],
         compiler_params=params(),
-        cost_estimate=pl.CostEstimate(flops=2 * rows * columns, bytes_accessed=10 * rows * columns, transcendentals=0),
-        name="prep",
-    )(place, queries, grad_out, attn_out)
+        cost_estimate=pl.CostEstimate(flops=2 * rows * columns, bytes_accessed=4 * rows * columns, transcendentals=0),
+        name="delta",
+    )(place, grad_out, attn_out)
 
     def shift(piece, by):
         if by == 0:
@@ -283,6 +291,7 @@
     )(base, block_lists.T, passage_keys, passage_values)
     incoming = exchange(outgoing)
     messages = [shift(piece, by) for piece, by in zip(messages, shifts(parts))]
+    deltas = [shift(tile, by) for tile, by in zip(deltas, shifts(parts))]
     own_lists = lax.dynamic_slice_in_dim(block_lists, my_shard * parts, parts, 0)
 
     own_slots = slot_of(own_lists // pass_dev)
@@ -292,6 +301,9 @@
     piece_shape = (QBLK, width)
     early = parts // 2 - 1
     late = parts - 1 - early
+
+    def held(blocks):
+        return [pltpu.VMEM((blocks,) + message.shape, BF16), pltpu.SemaphoreType.DMA((blocks,))]
 
     def scratch(blocks):
         return [
@@ -312,15 +324,14 @@
     query_grad, query_parts, outgoing_grads = pl.pallas_call(
         first_kernel,
         out_shape=[full_shape, jax.ShapeDtypeStruct((early,) + piece_shape, BF16), all_shape],
-        in_specs=[smem()] * 4 + [vmem(), hbm(), hbm(), vmem()] + [hbm()] * early,
+        in_specs=[smem()] * 4 + [vmem(), hbm(), hbm(), vmem()] + [hbm()] * early + [vmem()] * early,
         out_specs=[hbm(), vmem(), hbm()],
         scratch_shapes=[
             pltpu.VMEM((2 * QBLK, width), BF16),
-            pltpu.VMEM((early,) + message.shape, BF16),
             pltpu.VMEM(piece_shape, BF16),
             pltpu.SemaphoreType.DMA((2,)),
-            pltpu.SemaphoreType.DMA((early,)),
         ]
+        + held(early)
         + scratch(early + 1),
         compiler_params=params(),
         cost_estimate=cost(early + 1),
@@ -331,22 +342,23 @@
         own_lists,
         passage_lengths,
         incoming,
-        in_hbm(queries),
-        in_hbm(grad_out),
+        queries,
+        grad_out,
         own_delta,
-        *[in_hbm(piece) for piece in messages[:early]],
+        *messages[:early],
+        *deltas[:early],
     )
     late_parts, outgoing_grads = pl.pallas_call(
         last_kernel,
         out_shape=[jax.ShapeDtypeStruct((late,) + piece_shape, BF16), all_shape],
-        in_specs=[smem()] * 4 + [vmem()] * (1 + late) + [hbm()],
+        in_specs=[smem()] * 4 + [vmem()] + [hbm()] * late + [vmem()] * late + [hbm()],
         out_specs=[vmem(), hbm()],
-        scratch_shapes=scratch(late),
-        input_output_aliases={5 + late: 1},
+        scratch_shapes=held(late) + scratch(late),
+        input_output_aliases={5 + 2 * late: 1},
         compiler_params=params(),
         cost_estimate=cost(late),
         name="attention_last",
-    )(place, own_slots, own_lists, passage_lengths, incoming, *messages[early:], outgoing_grads)
+    )(place, own_slots, own_lists, passage_lengths, incoming, *messages[early:], *deltas[early:], outgoing_grads)
 
     returned = exchange(outgoing_grads)
     query_parts = [query_parts[i] for i in range(early)] + [late_parts[i] for i in range(late)]

time: 106 us -> 114 us (1.075)
  starting transfers between devices: 50.3 us -> 62.2 us
  waiting for transfers between devices: 37.7 us -> 33.1 us
  Pallas kernels: 14.6 us -> 16.2 us
  local copies, waits for them, and re-layouts: 2.13 us -> 0.92 us
    all_to_all x2, waiting for transfers between devices: 25.6 us -> 14.3 us  [exchange(): lax.all_to_all(pieces, EXCHANGE_AXES, split_axis=0, concat_axis=0, tiled=...]
    ppermute x6 -> x9, starting transfers between devices: 20.9 us -> 28.3 us  [shift(): lax.ppermute(piece, 'tensor', [(i, (i + by) % parts) for i in range(parts)])]
    ppermute x6 -> x9, waiting for transfers between devices: 12.1 us -> 18.8 us  [shift(): lax.ppermute(piece, 'tensor', [(i, (i + by) % parts) for i in range(parts)])]
    all_to_all x2, starting transfers between devices: 29.4 us -> 33.9 us  [exchange(): lax.all_to_all(pieces, EXCHANGE_AXES, split_axis=0, concat_axis=0, tiled=...]
    pallas_call x1, Pallas kernels: 3.32 us -> 4.71 us  [local(): pl.pallas_call(last_kernel, out_shape=[jax.ShapeDtypeStruct((late,) + pie...]
    unnamed x11, local copies, waits for them, and re-layouts: 1.32 us -> 0.11 us
  transfers between devices with their start and end apart: 8 -> 11, of which waited for: 6 -> 5; matrix products, arithmetic and copies ran while one was open for 1% -> 1% of each run, Pallas kernels for 7% -> 7%
where the time goes in v7:
time: 114 us; the launch traced here: 113 us
  starting transfers between devices  62.2 us (55%)
  waiting for transfers between devices  33.1 us (29%)
  Pallas kernels  16.2 us (14%)
    all_to_all x2, starting transfers between devices, exchange(): lax.all_to_all(pieces, EXCHANGE_AXES, split_axis=0, concat_axis=0, tiled=...  33.9 us
    ppermute x9, starting transfers between devices, shift(): lax.ppermute(piece, 'tensor', [(i, (i + by) % parts) for i in range(parts)])  28.3 us
    ppermute x9, waiting for transfers between devices, shift(): lax.ppermute(piece, 'tensor', [(i, (i + by) % parts) for i in range(parts)])  18.8 us
    all_to_all x2, waiting for transfers between devices, exchange(): lax.all_to_all(pieces, EXCHANGE_AXES, split_axis=0, concat_axis=0, tiled=...  14.3 us
    pallas_call x1, Pallas kernels, local(): pl.pallas_call(first_kernel, out_shape=[full_shape, jax.ShapeDtypeStruct(...  4.87 us
    pallas_call x1, Pallas kernels, local(): pl.pallas_call(last_kernel, out_shape=[jax.ShapeDtypeStruct((late,) + pie...  4.71 us
  transfers between devices with their start and end apart: 11, of which 5 were waited for; matrix products, arithmetic and copies ran while one was open for 1% of the time, Pallas kernels for 7%

profile of v7, /device:TPU:1, one launch (start us, length us, event | category | flops | bytes accessed | tf_op | source)
XLA Modules:
  0.0 113.4 jit_solution(15819269447661088420)
XLA Ops:
  0.6 2.2 %send.1 = (bf16[128,32,128]{2,1,0:T(8,128)(2,1)}, s32[1,512]{1,0:T(1,128)}) custom-call(s32[1]{0:T(128)} %bitcast.1.base_ref, s32[16,512]{1,0:T(8,128)} %bitcast.9, bf16[4,16,128]{2,1,0:T(8,128)(2,1)} %keys_ref.1, bf16[4,16,128]{2,1,0:T(8,128)(2,1)} %values_ref.1), custom_call_target="tpu_custom_call" | custom-call | tf_op jit(solution)/shard_map/send/pallas_call | solution.py:284
  2.8 0.0 copy-start
  2.8 0.0 copy-start.1
  2.8 18.9 %all-to-all-start = ((bf16[128,32,128]{2,1,0:T(8,128)(2,1)}), bf16[128,32,128]{2,1,0:T(8,128)(2,1)S(1)}, u32[]{:S(2)}, u32[]{:S(2)}) async-start(bf16[128,32,128]{2,1,0:T(8,128)(2,1)} %get-tuple-element.19), calls=%async_computation | async-start | bytes 2097152 | tf_op jit(solution)/shard_map/all_to_all | solution.py:35
  21.7 0.0 copy-done
  21.7 0.0 copy-done.1
  21.8 0.0 copy-start.2
  21.8 1.3 %cut.1 = (bf16[256,1024]{1,0:T(8,128)(2,1)}, bf16[256,1024]{1,0:T(8,128)(2,1)}, bf16[256,1024]{1,0:T(8,128)(2,1)}) custom-call(s32[1]{0:T(128)} %bitcast.place_ref, bf16[128,4096]{1,0:T(8,128)(2,1)S(1)} %copy-done.1, bf16[128,4096]{1,0:T(8,128)(2,1)S(1)} %copy-done), custom_call_target="tpu_custom_call" | custom-call | bytes 4194304 | tf_op jit(solution)/shard_map/cut/pallas_call | solution.py:258
  23.0 4.6 %collective-permute-start = (bf16[256,1024]{1,0:T(8,128)(2,1)}, bf16[256,1024]{1,0:T(8,128)(2,1)}, u32[]{:S(2)}, u32[]{:S(2)}) collective-permute-start(bf16[256,1024]{1,0:T(8,128)(2,1)} %get-tuple-element.21), channel_id=1, source_target_pairs={{0,2},{1,3},{2,0},{3,1},{4,6},{5,7},{6,4},{7,5},{8,10},{9,11},{10,... | collective-permute-start | bytes 1572872 | tf_op jit(solution)/shard_map/ppermute | solution.py:281
  27.7 2.2 %collective-permute-start.3 = (bf16[256,1024]{1,0:T(8,128)(2,1)}, bf16[256,1024]{1,0:T(8,128)(2,1)}, u32[]{:S(2)}, u32[]{:S(2)}) collective-permute-start(bf16[256,1024]{1,0:T(8,128)(2,1)} %get-tuple-element.25), channel_id=1, source_target_pairs={{0,1},{1,2},{2,3},{3,0},{4,5},{5,6},{6,7},{7,4},{8,9},{9,10},{10,1... | collective-permute-start | bytes 1572872 | tf_op jit(solution)/shard_map/ppermute | solution.py:281
  29.9 4.3 %collective-permute-start.4 = (bf16[256,1024]{1,0:T(8,128)(2,1)}, bf16[256,1024]{1,0:T(8,128)(2,1)}, u32[]{:S(2)}, u32[]{:S(2)}) collective-permute-start(bf16[256,1024]{1,0:T(8,128)(2,1)} %get-tuple-element.26), channel_id=1, source_target_pairs={{0,3},{1,0},{2,1},{3,2},{4,7},{5,4},{6,5},{7,6},{8,11},{9,8},{10,9... | collective-permute-start | bytes 1572872 | tf_op jit(solution)/shard_map/ppermute | solution.py:281
  34.2 0.0 copy-done.2
  34.2 0.7 delta.1
  34.9 1.9 %collective-permute-start.1 = (bf16[16,128]{1,0:T(8,128)(2,1)S(1)}, bf16[16,128]{1,0:T(8,128)(2,1)S(1)}, u32[]{:S(2)}, u32[]{:S(2)}) collective-permute-start(bf16[16,128]{1,0:T(8,128)(2,1)S(1)} %get-tuple-element.22), channel_id=1, source_target_pairs={{0,2},{1,3},{2,0},{3,1},{4,6},{5,7},{6,4},{7,5},{8,10},{9,11},{10,... | collective-permute-start | bytes 12296 | tf_op jit(solution)/shard_map/ppermute | solution.py:281
  36.8 2.5 %collective-permute-start.5 = (bf16[16,128]{1,0:T(8,128)(2,1)S(1)}, bf16[16,128]{1,0:T(8,128)(2,1)S(1)}, u32[]{:S(2)}, u32[]{:S(2)}) collective-permute-start(bf16[16,128]{1,0:T(8,128)(2,1)S(1)} %get-tuple-element.27), channel_id=1, source_target_pairs={{0,1},{1,2},{2,3},{3,0},{4,5},{5,6},{6,7},{7,4},{8,9},{9,10},{10,1... | collective-permute-start | bytes 12296 | tf_op jit(solution)/shard_map/ppermute | solution.py:281
  39.3 0.8 constant_dynamic-slice_fusion
  40.1 0.1 copy.13.lists_ref
  40.2 0.0 copy-start.3
  40.2 10.7 %collective-permute-done.1.rest_1_ = bf16[16,128]{1,0:T(8,128)(2,1)S(1)} collective-permute-done((bf16[16,128]{1,0:T(8,128)(2,1)S(1)}, bf16[16,128]{1,0:T(8,128)(2,1)S(1)}, u32[]{:S(2)}, u32[]{:S(2)}) %collective-permute-start.1) | collective-permute-done | bytes 4128 | tf_op jit(solution)/shard_map/ppermute | solution.py:281
  50.9 4.4 %collective-permute-start.6 = (bf16[16,128]{1,0:T(8,128)(2,1)S(1)}, bf16[16,128]{1,0:T(8,128)(2,1)S(1)}, u32[]{:S(2)}, u32[]{:S(2)}) collective-permute-start(bf16[16,128]{1,0:T(8,128)(2,1)S(1)} %get-tuple-element.28), channel_id=1, source_target_pairs={{0,3},{1,0},{2,1},{3,2},{4,7},{5,4},{6,5},{7,6},{8,11},{9,8},{10,9... | collective-permute-start | bytes 12296 | tf_op jit(solution)/shard_map/ppermute | solution.py:281
  55.3 0.0 collective-permute-done.rest_0_
  55.3 0.0 all-to-all-done.incoming_ref
  55.3 0.0 copy-done.3
  55.3 4.9 %attention_first.1 = (bf16[128,4096]{1,0:T(8,128)(2,1)}, bf16[1,128,1024]{2,1,0:T(8,128)(2,1)S(1)}, bf16[128,32,128]{2,1,0:T(8,128)(2,1)}) custom-call(s32[1]{0:T(128)} %bitcast.place_ref, s32[4,16]{1,0:T(4,128)S(1)} %shift-left_or_fusion.slots_ref, s32[4,16]{1,0:T(4,128)S(1)} %copy.13.lists_ref, s32[512]{0:T(512)S(1)} %copy-done.3, ...), custom_call_target="tpu_custom_call" | custom-call | flops 671088640 | bytes 2097152 | tf_op jit(solution)/shard_map/attention_first/pallas_call | solution.py:324
  60.2 0.0 collective-permute-done.5.rest_2_
  60.2 0.0 collective-permute-done.6.rest_3_
  60.2 0.0 collective-permute-done.3.rest_0_
  60.2 0.0 collective-permute-done.4.rest_1_
  60.2 4.7 %attention_last.1 = (bf16[2,128,1024]{2,1,0:T(8,128)(2,1)S(1)}, bf16[128,32,128]{2,1,0:T(8,128)(2,1)}) custom-call(s32[1]{0:T(128)} %bitcast.place_ref, s32[4,16]{1,0:T(4,128)S(1)} %shift-left_or_fusion.slots_ref, s32[4,16]{1,0:T(4,128)S(1)} %copy.13.lists_ref, s32[512]{0:T(512)S(1)} %copy-done.3, ...), custom_call_target="tpu_custom_call", output_to_operand_aliasing={{1}: (9, {})} | custom-call | flops 671088640 | bytes 2097152 | tf_op jit(solution)/shard_map/attention_last/pallas_call | solution.py:351
  64.9 15.0 %all-to-all-start.1 = ((bf16[128,32,128]{2,1,0:T(8,128)(2,1)}), bf16[128,32,128]{2,1,0:T(8,128)(2,1)S(1)}, u32[]{:S(2)}, u32[]{:S(2)}) async-start(bf16[128,32,128]{2,1,0:T(8,128)(2,1)} %get-tuple-element.32), calls=%async_computation.1 | async-start | bytes 2097152 | tf_op jit(solution)/shard_map/all_to_all | solution.py:35
  80.0 1.9 %collective-permute-start.8 = (bf16[128,1024]{1,0:T(8,128)(2,1)S(1)}, bf16[128,1024]{1,0:T(8,128)(2,1)S(1)}, u32[]{:S(2)}, u32[]{:S(2)}) collective-permute-start(bf16[128,1024]{1,0:T(8,128)(2,1)S(1)} %get-tuple-element.35), channel_id=1, source_target_pairs={{0,1},{1,2},{2,3},{3,0},{4,5},{5,6},{6,7},{7,4},{8,9},{9,10},{10,1... | collective-permute-start | bytes 786440 | tf_op jit(solution)/shard_map/ppermute | solution.py:281
  81.9 4.6 %collective-permute-start.7 = (bf16[128,1024]{1,0:T(8,128)(2,1)S(1)}, bf16[128,1024]{1,0:T(8,128)(2,1)S(1)}, u32[]{:S(2)}, u32[]{:S(2)}) collective-permute-start(bf16[128,1024]{1,0:T(8,128)(2,1)S(1)} %get-tuple-element.36), channel_id=1, source_target_pairs={{0,3},{1,0},{2,1},{3,2},{4,7},{5,4},{6,5},{7,6},{8,11},{9,8},{10,9... | collective-permute-start | bytes 786440 | tf_op jit(solution)/shard_map/ppermute | solution.py:281
  86.5 1.9 %collective-permute-start.2 = (bf16[128,1024]{1,0:T(8,128)(2,1)S(1)}, bf16[128,1024]{1,0:T(8,128)(2,1)S(1)}, u32[]{:S(2)}, u32[]{:S(2)}) collective-permute-start(bf16[128,1024]{1,0:T(8,128)(2,1)S(1)} %bitcast.8), channel_id=1, source_target_pairs={{0,2},{1,3},{2,0},{3,1},{4,6},{5,7},{6,4},{7,5},{8,10},{9,11},{10,... | collective-permute-start | bytes 786440 | tf_op jit(solution)/shard_map/ppermute | solution.py:281
  88.4 2.0 %collective-permute-done.8.rest_2_ = bf16[128,1024]{1,0:T(8,128)(2,1)S(1)} collective-permute-done((bf16[128,1024]{1,0:T(8,128)(2,1)S(1)}, bf16[128,1024]{1,0:T(8,128)(2,1)S(1)}, u32[]{:S(2)}, u32[]{:S(2)}) %collective-permute-start.8) | collective-permute-done | bytes 262176 | tf_op jit(solution)/shard_map/ppermute | solution.py:281
  90.4 1.5 %collective-permute-done.7.rest_1_ = bf16[128,1024]{1,0:T(8,128)(2,1)S(1)} collective-permute-done((bf16[128,1024]{1,0:T(8,128)(2,1)S(1)}, bf16[128,1024]{1,0:T(8,128)(2,1)S(1)}, u32[]{:S(2)}, u32[]{:S(2)}) %collective-permute-start.7) | collective-permute-done | bytes 262176 | tf_op jit(solution)/shard_map/ppermute | solution.py:281
  91.9 4.7 %collective-permute-done.2.rest_0_ = bf16[128,1024]{1,0:T(8,128)(2,1)S(1)} collective-permute-done((bf16[128,1024]{1,0:T(8,128)(2,1)S(1)}, bf16[128,1024]{1,0:T(8,128)(2,1)S(1)}, u32[]{:S(2)}, u32[]{:S(2)}) %collective-permute-start.2) | collective-permute-done | bytes 262176 | tf_op jit(solution)/shard_map/ppermute | solution.py:281
  96.6 0.0 copy-start.4
  96.6 0.9 place.1
  97.5 14.3 %all-to-all-done.1.terms_ref = bf16[128,32,128]{2,1,0:T(8,128)(2,1)S(1)} async-done(((bf16[128,32,128]{2,1,0:T(8,128)(2,1)}), bf16[128,32,128]{2,1,0:T(8,128)(2,1)S(1)}, u32[]{:S(2)}, u32[]{:S(2)}) %all-to-all-start.1) | async-done | bytes 1048608 | tf_op jit(solution)/shard_map/all_to_all | solution.py:35
  111.8 0.0 copy-done.4
  111.8 1.6 %sum.1 = (bf16[4,16,128]{2,1,0:T(8,128)(2,1)}, bf16[4,16,128]{2,1,0:T(8,128)(2,1)}) custom-call(s32[1,512]{1,0:T(1,128)S(1)} %copy-done.4, bf16[128,32,128]{2,1,0:T(8,128)(2,1)S(1)} %all-to-all-done.1.terms_ref), custom_call_target="tpu_custom_call" | custom-call | tf_op jit(solution)/shard_map/sum/pallas_call | solution.py:378
  (2 shorter events, 0.1 us)
Async XLA Ops:
  2.8 18.9 %copy-start = (bf16[128,4096]{1,0:T(8,128)(2,1)S(1)}, bf16[128,4096]{1,0:T(8,128)(2,1)}, u32[]{:S(2)}) copy-start(bf16[128,4096]{1,0:T(8,128)(2,1)} %g_ref.5) | copy-start | bytes 3145732
  2.8 18.9 %copy-start.1 = (bf16[128,4096]{1,0:T(8,128)(2,1)S(1)}, bf16[128,4096]{1,0:T(8,128)(2,1)}, u32[]{:S(2)}) copy-start(bf16[128,4096]{1,0:T(8,128)(2,1)} %q_ref.3) | copy-start | bytes 3145732
  2.8 52.4 %all-to-all-start = ((bf16[128,32,128]{2,1,0:T(8,128)(2,1)}), bf16[128,32,128]{2,1,0:T(8,128)(2,1)S(1)}, u32[]{:S(2)}, u32[]{:S(2)}) async-start(bf16[128,32,128]{2,1,0:T(8,128)(2,1)} %get-tuple-element.19), calls=%async_computation | async-start | bytes 2097152 | tf_op jit(solution)/shard_map/all_to_all | solution.py:35
  21.8 12.4 %copy-start.2 = (bf16[128,4096]{1,0:T(8,128)(2,1)S(1)}, bf16[128,4096]{1,0:T(8,128)(2,1)}, u32[]{:S(2)}) copy-start(bf16[128,4096]{1,0:T(8,128)(2,1)} %o_ref.1) | copy-start | bytes 3145732
  23.0 32.3 %collective-permute-start = (bf16[256,1024]{1,0:T(8,128)(2,1)}, bf16[256,1024]{1,0:T(8,128)(2,1)}, u32[]{:S(2)}, u32[]{:S(2)}) collective-permute-start(bf16[256,1024]{1,0:T(8,128)(2,1)} %get-tuple-element.21), channel_id=1, source_target_pairs={{0,2},{1,3},{2,0},{3,1},{4,6},{5,7},{6,4},{7,5},{8,10},{9,11},{10,... | collective-permute-start | bytes 1572872 | tf_op jit(solution)/shard_map/ppermute | solution.py:281
  27.7 32.5 %collective-permute-start.3 = (bf16[256,1024]{1,0:T(8,128)(2,1)}, bf16[256,1024]{1,0:T(8,128)(2,1)}, u32[]{:S(2)}, u32[]{:S(2)}) collective-permute-start(bf16[256,1024]{1,0:T(8,128)(2,1)} %get-tuple-element.25), channel_id=1, source_target_pairs={{0,1},{1,2},{2,3},{3,0},{4,5},{5,6},{6,7},{7,4},{8,9},{9,10},{10,1... | collective-permute-start | bytes 1572872 | tf_op jit(solution)/shard_map/ppermute | solution.py:281
  29.9 30.3 %collective-permute-start.4 = (bf16[256,1024]{1,0:T(8,128)(2,1)}, bf16[256,1024]{1,0:T(8,128)(2,1)}, u32[]{:S(2)}, u32[]{:S(2)}) collective-permute-start(bf16[256,1024]{1,0:T(8,128)(2,1)} %get-tuple-element.26), channel_id=1, source_target_pairs={{0,3},{1,0},{2,1},{3,2},{4,7},{5,4},{6,5},{7,6},{8,11},{9,8},{10,9... | collective-permute-start | bytes 1572872 | tf_op jit(solution)/shard_map/ppermute | solution.py:281
  34.9 16.0 %collective-permute-start.1 = (bf16[16,128]{1,0:T(8,128)(2,1)S(1)}, bf16[16,128]{1,0:T(8,128)(2,1)S(1)}, u32[]{:S(2)}, u32[]{:S(2)}) collective-permute-start(bf16[16,128]{1,0:T(8,128)(2,1)S(1)} %get-tuple-element.22), channel_id=1, source_target_pairs={{0,2},{1,3},{2,0},{3,1},{4,6},{5,7},{6,4},{7,5},{8,10},{9,11},{10,... | collective-permute-start | bytes 12296 | tf_op jit(solution)/shard_map/ppermute | solution.py:281
  36.8 23.4 %collective-permute-start.5 = (bf16[16,128]{1,0:T(8,128)(2,1)S(1)}, bf16[16,128]{1,0:T(8,128)(2,1)S(1)}, u32[]{:S(2)}, u32[]{:S(2)}) collective-permute-start(bf16[16,128]{1,0:T(8,128)(2,1)S(1)} %get-tuple-element.27), channel_id=1, source_target_pairs={{0,1},{1,2},{2,3},{3,0},{4,5},{5,6},{6,7},{7,4},{8,9},{9,10},{10,1... | collective-permute-start | bytes 12296 | tf_op jit(solution)/shard_map/ppermute | solution.py:281
  40.2 15.1 %copy-start.3 = (s32[512]{0:T(512)S(1)}, s32[512]{0:T(512)}, u32[]{:S(2)}) copy-start(s32[512]{0:T(512)} %lengths_ref.3) | copy-start | bytes 6148
  50.9 9.3 %collective-permute-start.6 = (bf16[16,128]{1,0:T(8,128)(2,1)S(1)}, bf16[16,128]{1,0:T(8,128)(2,1)S(1)}, u32[]{:S(2)}, u32[]{:S(2)}) collective-permute-start(bf16[16,128]{1,0:T(8,128)(2,1)S(1)} %get-tuple-element.28), channel_id=1, source_target_pairs={{0,3},{1,0},{2,1},{3,2},{4,7},{5,4},{6,5},{7,6},{8,11},{9,8},{10,9... | collective-permute-start | bytes 12296 | tf_op jit(solution)/shard_map/ppermute | solution.py:281
  64.9 46.8 %all-to-all-start.1 = ((bf16[128,32,128]{2,1,0:T(8,128)(2,1)}), bf16[128,32,128]{2,1,0:T(8,128)(2,1)S(1)}, u32[]{:S(2)}, u32[]{:S(2)}) async-start(bf16[128,32,128]{2,1,0:T(8,128)(2,1)} %get-tuple-element.32), calls=%async_computation.1 | async-start | bytes 2097152 | tf_op jit(solution)/shard_map/all_to_all | solution.py:35
  80.0 10.4 %collective-permute-start.8 = (bf16[128,1024]{1,0:T(8,128)(2,1)S(1)}, bf16[128,1024]{1,0:T(8,128)(2,1)S(1)}, u32[]{:S(2)}, u32[]{:S(2)}) collective-permute-start(bf16[128,1024]{1,0:T(8,128)(2,1)S(1)} %get-tuple-element.35), channel_id=1, source_target_pairs={{0,1},{1,2},{2,3},{3,0},{4,5},{5,6},{6,7},{7,4},{8,9},{9,10},{10,1... | collective-permute-start | bytes 786440 | tf_op jit(solution)/shard_map/ppermute | solution.py:281
  81.9 10.0 %collective-permute-start.7 = (bf16[128,1024]{1,0:T(8,128)(2,1)S(1)}, bf16[128,1024]{1,0:T(8,128)(2,1)S(1)}, u32[]{:S(2)}, u32[]{:S(2)}) collective-permute-start(bf16[128,1024]{1,0:T(8,128)(2,1)S(1)} %get-tuple-element.36), channel_id=1, source_target_pairs={{0,3},{1,0},{2,1},{3,2},{4,7},{5,4},{6,5},{7,6},{8,11},{9,8},{10,9... | collective-permute-start | bytes 786440 | tf_op jit(solution)/shard_map/ppermute | solution.py:281
  86.5 10.1 %collective-permute-start.2 = (bf16[128,1024]{1,0:T(8,128)(2,1)S(1)}, bf16[128,1024]{1,0:T(8,128)(2,1)S(1)}, u32[]{:S(2)}, u32[]{:S(2)}) collective-permute-start(bf16[128,1024]{1,0:T(8,128)(2,1)S(1)} %bitcast.8), channel_id=1, source_target_pairs={{0,2},{1,3},{2,0},{3,1},{4,6},{5,7},{6,4},{7,5},{8,10},{9,11},{10,... | collective-permute-start | bytes 786440 | tf_op jit(solution)/shard_map/ppermute | solution.py:281
  96.6 15.2 %copy-start.4 = (s32[1,512]{1,0:T(1,128)S(1)}, s32[1,512]{1,0:T(1,128)}, u32[]{:S(2)}) copy-start(s32[1,512]{1,0:T(1,128)} %get-tuple-element.31.pick_ref) | copy-start | bytes 6148

commit v8 on v6

--- a/solution.py
+++ b/solution.py
@@ -163,28 +163,26 @@
 
 
 def first_kernel(place_ref, slots_ref, lists_ref, lengths_ref, incoming_ref, q_ref, g_ref, own_delta_ref, *rest):
-    held = len(rest) - 13
-    message_refs = rest[:held]
-    query_grad_ref, dq_ref, out_ref, own_ref, held_ref, own_dq_ref = rest[held : held + 6]
-    own_sems, held_sems = rest[held + 6 : held + 8]
-    scratch = rest[held + 8 :]
+    early = len(rest) - 11
+    message_refs = rest[:early]
+    query_grad_ref, dq_ref, out_ref, own_ref, own_dq_ref, own_sems = rest[early : early + 6]
+    scratch = rest[early + 6 :]
     parts = lists_ref.shape[0]
-    share = own_ref.shape[1] // DH
     width = own_ref.shape[1]
+    share = width // DH
     own_cols = pl.ds(pl.multiple_of(place_ref[0] * width, width), width)
     loads = [
         pltpu.make_async_copy(q_ref.at[:, own_cols], own_ref.at[0:QBLK, :], own_sems.at[0]),
         pltpu.make_async_copy(g_ref.at[:, own_cols], own_ref.at[QBLK : 2 * QBLK, :], own_sems.at[1]),
     ]
-    blocks = [place_ref[0]]
-    pieces = [(own_ref, own_delta_ref, own_dq_ref, loads)]
+    for load in loads:
+        load.start()
+    blocks, pieces = [], []
     for i, message_ref in enumerate(message_refs):
-        load = pltpu.make_async_copy(message_ref, held_ref.at[i], held_sems.at[i])
         blocks.append(lax.rem(place_ref[0] + parts - shifts(parts)[i], parts))
-        pieces.append((held_ref.at[i], held_ref.at[i, 2 * QBLK : 2 * QBLK + 2 * share, 0:DH], dq_ref.at[i], [load]))
-    for piece in pieces:
-        for copy in piece[3]:
-            copy.start()
+        pieces.append((message_ref, message_ref.at[2 * QBLK : 2 * QBLK + 2 * share, 0:DH], dq_ref.at[i], []))
+    blocks.append(place_ref[0])
+    pieces.append((own_ref, own_delta_ref, own_dq_ref, loads))
     stores = attend(slots_ref, lists_ref, lengths_ref, incoming_ref, blocks, pieces, out_ref, *scratch)
     copy = pltpu.make_async_copy(own_dq_ref, query_grad_ref.at[:, own_cols], own_sems.at[0])
     copy.start()
@@ -312,14 +310,12 @@
     query_grad, query_parts, outgoing_grads = pl.pallas_call(
         first_kernel,
         out_shape=[full_shape, jax.ShapeDtypeStruct((early,) + piece_shape, BF16), all_shape],
-        in_specs=[smem()] * 4 + [vmem(), hbm(), hbm(), vmem()] + [hbm()] * early,
+        in_specs=[smem()] * 4 + [vmem(), hbm(), hbm()] + [vmem()] * (1 + early),
         out_specs=[hbm(), vmem(), hbm()],
         scratch_shapes=[
             pltpu.VMEM((2 * QBLK, width), BF16),
-            pltpu.VMEM((early,) + message.shape, BF16),
             pltpu.VMEM(piece_shape, BF16),
             pltpu.SemaphoreType.DMA((2,)),
-            pltpu.SemaphoreType.DMA((early,)),
         ]
         + scratch(early + 1),
         compiler_params=params(),
@@ -334,7 +330,7 @@
         in_hbm(queries),
         in_hbm(grad_out),
         own_delta,
-        *[in_hbm(piece) for piece in messages[:early]],
+        *messages[:early],
     )
     late_parts, outgoing_grads = pl.pallas_call(
         last_kernel,

time: 106 us -> 106 us (level)
  no operation moved by 1% of the time
where the time goes in v8:
time: 106 us
  starting transfers between devices  50.5 us (48%)
  waiting for transfers between devices  37.7 us (36%)
  Pallas kernels  14.4 us (14%)
  local copies, waits for them, and re-layouts  2.13 us (2%)
    all_to_all x2, starting transfers between devices, exchange(): lax.all_to_all(pieces, EXCHANGE_AXES, split_axis=0, concat_axis=0, tiled=...  29.6 us
    all_to_all x2, waiting for transfers between devices, exchange(): lax.all_to_all(pieces, EXCHANGE_AXES, split_axis=0, concat_axis=0, tiled=...  25.7 us
    ppermute x6, starting transfers between devices, shift(): lax.ppermute(piece, 'tensor', [(i, (i + by) % parts) for i in range(parts)])  20.9 us
    ppermute x6, waiting for transfers between devices, shift(): lax.ppermute(piece, 'tensor', [(i, (i + by) % parts) for i in range(parts)])  12 us
    pallas_call x1, Pallas kernels, local(): pl.pallas_call(first_kernel, out_shape=[full_shape, jax.ShapeDtypeStruct(...  4.59 us
    pallas_call x1, Pallas kernels, local(): pl.pallas_call(last_kernel, out_shape=[jax.ShapeDtypeStruct((late,) + pie...  3.31 us
    pallas_call x1, Pallas kernels, local(): pl.pallas_call(send_kernel, out_shape=[all_shape, jax.ShapeDtypeStruct((1...  2.2 us
  transfers between devices with their start and end apart: 8, of which 6 were waited for; matrix products, arithmetic and copies ran while one was open for 1% of the time, Pallas kernels for 7%

profile of v8, /device:TPU:1, one launch (start us, length us, event | category | flops | bytes accessed | tf_op | source)
XLA Modules:
  0.0 105.6 jit_solution(12728037613798452401)
XLA Ops:
  0.6 2.2 %send.1 = (bf16[128,32,128]{2,1,0:T(8,128)(2,1)}, s32[1,512]{1,0:T(1,128)}) custom-call(s32[1]{0:T(128)} %bitcast.1.base_ref, s32[16,512]{1,0:T(8,128)} %bitcast.9, bf16[4,16,128]{2,1,0:T(8,128)(2,1)} %keys_ref.1, bf16[4,16,128]{2,1,0:T(8,128)(2,1)} %values_ref.1), custom_call_target="tpu_custom_call" | custom-call | tf_op jit(solution)/shard_map/send/pallas_call | solution.py:274
  2.8 0.0 copy-start
  2.8 0.0 copy-start.1
  2.8 18.9 %all-to-all-start = ((bf16[128,32,128]{2,1,0:T(8,128)(2,1)}), bf16[128,32,128]{2,1,0:T(8,128)(2,1)S(1)}, u32[]{:S(2)}, u32[]{:S(2)}) async-start(bf16[128,32,128]{2,1,0:T(8,128)(2,1)} %get-tuple-element.16), calls=%async_computation | async-start | bytes 2097152 | tf_op jit(solution)/shard_map/all_to_all | solution.py:35
  21.7 0.0 copy-done
  21.7 0.0 copy-done.1
  21.8 0.0 copy-start.2
  21.8 1.2 %copy-done.2 = bf16[128,4096]{1,0:T(8,128)(2,1)S(1)} copy-done((bf16[128,4096]{1,0:T(8,128)(2,1)S(1)}, bf16[128,4096]{1,0:T(8,128)(2,1)}, u32[]{:S(2)}) %copy-start.2) | copy-done | bytes 1048600
  23.0 1.8 %prep.1 = (bf16[272,1024]{1,0:T(8,128)(2,1)}, bf16[272,1024]{1,0:T(8,128)(2,1)}, bf16[272,1024]{1,0:T(8,128)(2,1)}, bf16[16,128]{1,0:T(8,128)(2,1)S(1)}) custom-call(s32[1]{0:T(128)} %bitcast.place_ref, bf16[128,4096]{1,0:T(8,128)(2,1)S(1)} %copy-done, bf16[128,4096]{1,0:T(8,128)(2,1)S(1)} %copy-done.1, bf16[128,4096]{1,0:T(8,128)(2,1)S(1)} %copy-done.2), custom_call_target="tpu_custom_call" | custom-call | flops 1048576 | bytes 5242880 | tf_op jit(solution)/shard_map/prep/pallas_call | solution.py:257
  24.8 4.6 %collective-permute-start = (bf16[272,1024]{1,0:T(8,128)(2,1)}, bf16[272,1024]{1,0:T(8,128)(2,1)S(1)}, u32[]{:S(2)}, u32[]{:S(2)}) collective-permute-start(bf16[272,1024]{1,0:T(8,128)(2,1)} %get-tuple-element.18), channel_id=1, source_target_pairs={{0,2},{1,3},{2,0},{3,1},{4,6},{5,7},{6,4},{7,5},{8,10},{9,11},{10,... | collective-permute-start | bytes 1671176 | tf_op jit(solution)/shard_map/ppermute | solution.py:271
  29.5 2.2 %collective-permute-start.2 = (bf16[272,1024]{1,0:T(8,128)(2,1)}, bf16[272,1024]{1,0:T(8,128)(2,1)S(1)}, u32[]{:S(2)}, u32[]{:S(2)}) collective-permute-start(bf16[272,1024]{1,0:T(8,128)(2,1)} %get-tuple-element.21), channel_id=1, source_target_pairs={{0,1},{1,2},{2,3},{3,0},{4,5},{5,6},{6,7},{7,4},{8,9},{9,10},{10,1... | collective-permute-start | bytes 1671176 | tf_op jit(solution)/shard_map/ppermute | solution.py:271
  31.7 4.3 %collective-permute-start.3 = (bf16[272,1024]{1,0:T(8,128)(2,1)}, bf16[272,1024]{1,0:T(8,128)(2,1)S(1)}, u32[]{:S(2)}, u32[]{:S(2)}) collective-permute-start(bf16[272,1024]{1,0:T(8,128)(2,1)} %get-tuple-element.22), channel_id=1, source_target_pairs={{0,3},{1,0},{2,1},{3,2},{4,7},{5,4},{6,5},{7,6},{8,11},{9,8},{10,9... | collective-permute-start | bytes 1671176 | tf_op jit(solution)/shard_map/ppermute | solution.py:271
  36.0 0.8 constant_dynamic-slice_fusion
  36.8 0.1 copy.13.lists_ref
  36.8 0.0 copy-start.3
  36.9 5.2 %collective-permute-done.rest_0_ = bf16[272,1024]{1,0:T(8,128)(2,1)S(1)} collective-permute-done((bf16[272,1024]{1,0:T(8,128)(2,1)}, bf16[272,1024]{1,0:T(8,128)(2,1)S(1)}, u32[]{:S(2)}, u32[]{:S(2)}) %collective-permute-start) | collective-permute-done | bytes 557088 | tf_op jit(solution)/shard_map/ppermute | solution.py:271
  42.1 11.5 %all-to-all-done.incoming_ref = bf16[128,32,128]{2,1,0:T(8,128)(2,1)S(1)} async-done(((bf16[128,32,128]{2,1,0:T(8,128)(2,1)}), bf16[128,32,128]{2,1,0:T(8,128)(2,1)S(1)}, u32[]{:S(2)}, u32[]{:S(2)}) %all-to-all-start) | async-done | bytes 1048608 | tf_op jit(solution)/shard_map/all_to_all | solution.py:35
  53.5 0.0 copy-done.3
  53.5 4.6 %attention_first.1 = (bf16[128,4096]{1,0:T(8,128)(2,1)}, bf16[1,128,1024]{2,1,0:T(8,128)(2,1)S(1)}, bf16[128,32,128]{2,1,0:T(8,128)(2,1)}) custom-call(s32[1]{0:T(128)} %bitcast.place_ref, s32[4,16]{1,0:T(4,128)S(1)} %shift-left_or_fusion.slots_ref, s32[4,16]{1,0:T(4,128)S(1)} %copy.13.lists_ref, s32[512]{0:T(512)S(1)} %copy-done.3, ...), custom_call_target="tpu_custom_call" | custom-call | flops 671088640 | bytes 2097152 | tf_op jit(solution)/shard_map/attention_first/pallas_call | solution.py:310
  58.1 0.0 collective-permute-done.2.rest_0_
  58.1 0.0 collective-permute-done.3.rest_1_
  58.2 3.3 %attention_last.1 = (bf16[2,128,1024]{2,1,0:T(8,128)(2,1)S(1)}, bf16[128,32,128]{2,1,0:T(8,128)(2,1)}) custom-call(s32[1]{0:T(128)} %bitcast.place_ref, s32[4,16]{1,0:T(4,128)S(1)} %shift-left_or_fusion.slots_ref, s32[4,16]{1,0:T(4,128)S(1)} %copy.13.lists_ref, s32[512]{0:T(512)S(1)} %copy-done.3, ...), custom_call_target="tpu_custom_call", output_to_operand_aliasing={{1}: (7, {})} | custom-call | flops 671088640 | bytes 2097152 | tf_op jit(solution)/shard_map/attention_last/pallas_call | solution.py:335
  61.5 10.7 %all-to-all-start.1 = ((bf16[128,32,128]{2,1,0:T(8,128)(2,1)}), bf16[128,32,128]{2,1,0:T(8,128)(2,1)S(1)}, u32[]{:S(2)}, u32[]{:S(2)}) async-start(bf16[128,32,128]{2,1,0:T(8,128)(2,1)} %get-tuple-element.26), calls=%async_computation.1 | async-start | bytes 2097152 | tf_op jit(solution)/shard_map/all_to_all | solution.py:35
  72.2 3.1 %collective-permute-start.5 = (bf16[128,1024]{1,0:T(8,128)(2,1)S(1)}, bf16[128,1024]{1,0:T(8,128)(2,1)S(1)}, u32[]{:S(2)}, u32[]{:S(2)}) collective-permute-start(bf16[128,1024]{1,0:T(8,128)(2,1)S(1)} %get-tuple-element.29), channel_id=1, source_target_pairs={{0,1},{1,2},{2,3},{3,0},{4,5},{5,6},{6,7},{7,4},{8,9},{9,10},{10,1... | collective-permute-start | bytes 786440 | tf_op jit(solution)/shard_map/ppermute | solution.py:271
  75.3 3.4 %collective-permute-start.4 = (bf16[128,1024]{1,0:T(8,128)(2,1)S(1)}, bf16[128,1024]{1,0:T(8,128)(2,1)S(1)}, u32[]{:S(2)}, u32[]{:S(2)}) collective-permute-start(bf16[128,1024]{1,0:T(8,128)(2,1)S(1)} %get-tuple-element.30), channel_id=1, source_target_pairs={{0,3},{1,0},{2,1},{3,2},{4,7},{5,4},{6,5},{7,6},{8,11},{9,8},{10,9... | collective-permute-start | bytes 786440 | tf_op jit(solution)/shard_map/ppermute | solution.py:271
  78.7 3.3 %collective-permute-start.1 = (bf16[128,1024]{1,0:T(8,128)(2,1)S(1)}, bf16[128,1024]{1,0:T(8,128)(2,1)S(1)}, u32[]{:S(2)}, u32[]{:S(2)}) collective-permute-start(bf16[128,1024]{1,0:T(8,128)(2,1)S(1)} %bitcast.8), channel_id=1, source_target_pairs={{0,2},{1,3},{2,0},{3,1},{4,6},{5,7},{6,4},{7,5},{8,10},{9,11},{10,... | collective-permute-start | bytes 786440 | tf_op jit(solution)/shard_map/ppermute | solution.py:271
  82.0 0.6 collective-permute-done.5.rest_2_
  82.6 1.5 %collective-permute-done.4.rest_1_ = bf16[128,1024]{1,0:T(8,128)(2,1)S(1)} collective-permute-done((bf16[128,1024]{1,0:T(8,128)(2,1)S(1)}, bf16[128,1024]{1,0:T(8,128)(2,1)S(1)}, u32[]{:S(2)}, u32[]{:S(2)}) %collective-permute-start.4) | collective-permute-done | bytes 262176 | tf_op jit(solution)/shard_map/ppermute | solution.py:271
  84.1 4.6 %collective-permute-done.1.rest_0_ = bf16[128,1024]{1,0:T(8,128)(2,1)S(1)} collective-permute-done((bf16[128,1024]{1,0:T(8,128)(2,1)S(1)}, bf16[128,1024]{1,0:T(8,128)(2,1)S(1)}, u32[]{:S(2)}, u32[]{:S(2)}) %collective-permute-start.1) | collective-permute-done | bytes 262176 | tf_op jit(solution)/shard_map/ppermute | solution.py:271
  88.8 0.0 copy-start.4
  88.8 0.9 place.1
  89.7 14.3 %all-to-all-done.1.terms_ref = bf16[128,32,128]{2,1,0:T(8,128)(2,1)S(1)} async-done(((bf16[128,32,128]{2,1,0:T(8,128)(2,1)}), bf16[128,32,128]{2,1,0:T(8,128)(2,1)S(1)}, u32[]{:S(2)}, u32[]{:S(2)}) %all-to-all-start.1) | async-done | bytes 1048608 | tf_op jit(solution)/shard_map/all_to_all | solution.py:35
  104.0 0.0 copy-done.4
  104.0 1.6 %sum.1 = (bf16[4,16,128]{2,1,0:T(8,128)(2,1)}, bf16[4,16,128]{2,1,0:T(8,128)(2,1)}) custom-call(s32[1,512]{1,0:T(1,128)S(1)} %copy-done.4, bf16[128,32,128]{2,1,0:T(8,128)(2,1)S(1)} %all-to-all-done.1.terms_ref), custom_call_target="tpu_custom_call" | custom-call | tf_op jit(solution)/shard_map/sum/pallas_call | solution.py:362
  (2 shorter events, 0.1 us)
Async XLA Ops:
  2.8 18.9 %copy-start = (bf16[128,4096]{1,0:T(8,128)(2,1)S(1)}, bf16[128,4096]{1,0:T(8,128)(2,1)}, u32[]{:S(2)}) copy-start(bf16[128,4096]{1,0:T(8,128)(2,1)} %q_ref.3) | copy-start | bytes 3145732
  2.8 18.9 %copy-start.1 = (bf16[128,4096]{1,0:T(8,128)(2,1)S(1)}, bf16[128,4096]{1,0:T(8,128)(2,1)}, u32[]{:S(2)}) copy-start(bf16[128,4096]{1,0:T(8,128)(2,1)} %g_ref.3) | copy-start | bytes 3145732
  2.8 50.7 %all-to-all-start = ((bf16[128,32,128]{2,1,0:T(8,128)(2,1)}), bf16[128,32,128]{2,1,0:T(8,128)(2,1)S(1)}, u32[]{:S(2)}, u32[]{:S(2)}) async-start(bf16[128,32,128]{2,1,0:T(8,128)(2,1)} %get-tuple-element.16), calls=%async_computation | async-start | bytes 2097152 | tf_op jit(solution)/shard_map/all_to_all | solution.py:35
  21.8 1.2 %copy-start.2 = (bf16[128,4096]{1,0:T(8,128)(2,1)S(1)}, bf16[128,4096]{1,0:T(8,128)(2,1)}, u32[]{:S(2)}) copy-start(bf16[128,4096]{1,0:T(8,128)(2,1)} %o_ref.1) | copy-start | bytes 3145732
  24.8 17.2 %collective-permute-start = (bf16[272,1024]{1,0:T(8,128)(2,1)}, bf16[272,1024]{1,0:T(8,128)(2,1)S(1)}, u32[]{:S(2)}, u32[]{:S(2)}) collective-permute-start(bf16[272,1024]{1,0:T(8,128)(2,1)} %get-tuple-element.18), channel_id=1, source_target_pairs={{0,2},{1,3},{2,0},{3,1},{4,6},{5,7},{6,4},{7,5},{8,10},{9,11},{10,... | collective-permute-start | bytes 1671176 | tf_op jit(solution)/shard_map/ppermute | solution.py:271
  29.5 28.7 %collective-permute-start.2 = (bf16[272,1024]{1,0:T(8,128)(2,1)}, bf16[272,1024]{1,0:T(8,128)(2,1)S(1)}, u32[]{:S(2)}, u32[]{:S(2)}) collective-permute-start(bf16[272,1024]{1,0:T(8,128)(2,1)} %get-tuple-element.21), channel_id=1, source_target_pairs={{0,1},{1,2},{2,3},{3,0},{4,5},{5,6},{6,7},{7,4},{8,9},{9,10},{10,1... | collective-permute-start | bytes 1671176 | tf_op jit(solution)/shard_map/ppermute | solution.py:271
  31.7 26.4 %collective-permute-start.3 = (bf16[272,1024]{1,0:T(8,128)(2,1)}, bf16[272,1024]{1,0:T(8,128)(2,1)S(1)}, u32[]{:S(2)}, u32[]{:S(2)}) collective-permute-start(bf16[272,1024]{1,0:T(8,128)(2,1)} %get-tuple-element.22), channel_id=1, source_target_pairs={{0,3},{1,0},{2,1},{3,2},{4,7},{5,4},{6,5},{7,6},{8,11},{9,8},{10,9... | collective-permute-start | bytes 1671176 | tf_op jit(solution)/shard_map/ppermute | solution.py:271
  36.8 16.7 %copy-start.3 = (s32[512]{0:T(512)S(1)}, s32[512]{0:T(512)}, u32[]{:S(2)}) copy-start(s32[512]{0:T(512)} %lengths_ref.3) | copy-start | bytes 6148
  61.5 42.5 %all-to-all-start.1 = ((bf16[128,32,128]{2,1,0:T(8,128)(2,1)}), bf16[128,32,128]{2,1,0:T(8,128)(2,1)S(1)}, u32[]{:S(2)}, u32[]{:S(2)}) async-start(bf16[128,32,128]{2,1,0:T(8,128)(2,1)} %get-tuple-element.26), calls=%async_computation.1 | async-start | bytes 2097152 | tf_op jit(solution)/shard_map/all_to_all | solution.py:35
  72.2 10.4 %collective-permute-start.5 = (bf16[128,1024]{1,0:T(8,128)(2,1)S(1)}, bf16[128,1024]{1,0:T(8,128)(2,1)S(1)}, u32[]{:S(2)}, u32[]{:S(2)}) collective-permute-start(bf16[128,1024]{1,0:T(8,128)(2,1)S(1)} %get-tuple-element.29), channel_id=1, source_target_pairs={{0,1},{1,2},{2,3},{3,0},{4,5},{5,6},{6,7},{7,4},{8,9},{9,10},{10,1... | collective-permute-start | bytes 786440 | tf_op jit(solution)/shard_map/ppermute | solution.py:271
  75.3 8.9 %collective-permute-start.4 = (bf16[128,1024]{1,0:T(8,128)(2,1)S(1)}, bf16[128,1024]{1,0:T(8,128)(2,1)S(1)}, u32[]{:S(2)}, u32[]{:S(2)}) collective-permute-start(bf16[128,1024]{1,0:T(8,128)(2,1)S(1)} %get-tuple-element.30), channel_id=1, source_target_pairs={{0,3},{1,0},{2,1},{3,2},{4,7},{5,4},{6,5},{7,6},{8,11},{9,8},{10,9... | collective-permute-start | bytes 786440 | tf_op jit(solution)/shard_map/ppermute | solution.py:271
  78.7 10.1 %collective-permute-start.1 = (bf16[128,1024]{1,0:T(8,128)(2,1)S(1)}, bf16[128,1024]{1,0:T(8,128)(2,1)S(1)}, u32[]{:S(2)}, u32[]{:S(2)}) collective-permute-start(bf16[128,1024]{1,0:T(8,128)(2,1)S(1)} %bitcast.8), channel_id=1, source_target_pairs={{0,2},{1,3},{2,0},{3,1},{4,6},{5,7},{6,4},{7,5},{8,10},{9,11},{10,... | collective-permute-start | bytes 786440 | tf_op jit(solution)/shard_map/ppermute | solution.py:271
  88.8 15.2 %copy-start.4 = (s32[1,512]{1,0:T(1,128)S(1)}, s32[1,512]{1,0:T(1,128)}, u32[]{:S(2)}) copy-start(s32[1,512]{1,0:T(1,128)} %get-tuple-element.25.pick_ref) | copy-start | bytes 6148

commit v9 on v8

--- a/solution.py
+++ b/solution.py
@@ -81,31 +81,34 @@
 
 
 def prep_kernel(place_ref, q_ref, g_ref, o_ref, *rest):
-    *message_refs, own_ref, delta_ref = rest
+    *message_refs, own_ref, out_ref, delta_ref, sem = rest
+    load = pltpu.make_async_copy(o_ref, out_ref, sem)
+    load.start()
     parts = len(message_refs) + 1
     width = q_ref.shape[1] // parts
     share = width // DH
+    targets = [lax.rem(place_ref[0] + by, parts) for by in (0,) + shifts(parts)]
+    for to, message_ref in zip(targets[1:], message_refs):
+        cols = pl.ds(pl.multiple_of(to * width, width), width)
+        message_ref[0:QBLK, :] = q_ref[:, cols]
+        message_ref[QBLK : 2 * QBLK, :] = g_ref[:, cols]
+        message_ref[2 * QBLK :, :] = jnp.zeros((2 * share, width), BF16)
+    load.wait()
     lane = lax.broadcasted_iota(jnp.int32, (QBLK, DH), 1)
     delta = jnp.zeros((QBLK, DH), F32)
     for h in range(parts * share):
         cols = slice(h * DH, (h + 1) * DH)
-        term = jnp.sum(g_ref[:, cols].astype(F32) * o_ref[:, cols].astype(F32), axis=1, keepdims=True)
+        term = jnp.sum(g_ref[:, cols].astype(F32) * out_ref[:, cols].astype(F32), axis=1, keepdims=True)
         delta = jnp.where(lane == h, term, delta)
     delta_ref[...] = delta.T
-    for j in range(parts):
-        to = lax.rem(place_ref[0] + (0 if j == 0 else shifts(parts)[j - 1]), parts)
+    for j, to in enumerate(targets):
         rows = delta_ref[pl.ds(pl.multiple_of(to * share, share), share), :]
         high = rows.astype(BF16).astype(F32)
         rows = jnp.concatenate([high, rows - high], axis=0).astype(BF16)
         if j == 0:
             own_ref[...] = rows
-            continue
-        message_ref = message_refs[j - 1]
-        cols = pl.ds(pl.multiple_of(to * width, width), width)
-        message_ref[0:QBLK, :] = q_ref[:, cols]
-        message_ref[QBLK : 2 * QBLK, :] = g_ref[:, cols]
-        message_ref[2 * QBLK :, :] = jnp.zeros((2 * share, width), BF16)
-        message_ref[2 * QBLK :, 0:DH] = rows
+        else:
+            message_refs[j - 1][2 * QBLK :, 0:DH] = rows
 
 
 def attend(slots_ref, lists_ref, lengths_ref, incoming_ref, blocks, pieces, out_ref, k_ref, v_ref, terms_ref, bias_ref, sems):
@@ -257,13 +260,13 @@
     *messages, own_delta = pl.pallas_call(
         prep_kernel,
         out_shape=[message] * (parts - 1) + [own_shape],
-        in_specs=[smem(), vmem(), vmem(), vmem()],
+        in_specs=[smem(), vmem(), vmem(), hbm()],
         out_specs=[vmem()] * parts,
-        scratch_shapes=[pltpu.VMEM((DH, QBLK), F32)],
+        scratch_shapes=[pltpu.VMEM((rows, columns), BF16), pltpu.VMEM((DH, QBLK), F32), pltpu.SemaphoreType.DMA],
         compiler_params=params(),
         cost_estimate=pl.CostEstimate(flops=2 * rows * columns, bytes_accessed=10 * rows * columns, transcendentals=0),
         name="prep",
-    )(place, queries, grad_out, attn_out)
+    )(place, queries, grad_out, in_hbm(attn_out))
 
     def shift(piece, by):
         if by == 0:

time: 106 us -> 106 us (level)
  local copies, waits for them, and re-layouts: 2.13 us -> 0.91 us
  Pallas kernels: 14.4 us -> 15.6 us
    unnamed x11 -> x9, local copies, waits for them, and re-layouts: 1.32 us -> 0.1 us
    pallas_call x1, Pallas kernels: 1.85 us -> 3.06 us  [local(): pl.pallas_call(prep_kernel, out_shape=[message] * (parts - 1) + [own_shap...]
  transfers between devices with their start and end apart: 8 -> 8, of which waited for: 6 -> 6; matrix products, arithmetic and copies ran while one was open for 1% -> 1% of each run, Pallas kernels for 7% -> 8%
where the time goes in v9:
time: 106 us
  starting transfers between devices  50.5 us (48%)
  waiting for transfers between devices  37.7 us (36%)
  Pallas kernels  15.6 us (15%)
    all_to_all x2, starting transfers between devices, exchange(): lax.all_to_all(pieces, EXCHANGE_AXES, split_axis=0, concat_axis=0, tiled=...  29.6 us
    all_to_all x2, waiting for transfers between devices, exchange(): lax.all_to_all(pieces, EXCHANGE_AXES, split_axis=0, concat_axis=0, tiled=...  25.7 us
    ppermute x6, starting transfers between devices, shift(): lax.ppermute(piece, 'tensor', [(i, (i + by) % parts) for i in range(parts)])  20.9 us
    ppermute x6, waiting for transfers between devices, shift(): lax.ppermute(piece, 'tensor', [(i, (i + by) % parts) for i in range(parts)])  12 us
    pallas_call x1, Pallas kernels, local(): pl.pallas_call(first_kernel, out_shape=[full_shape, jax.ShapeDtypeStruct(...  4.59 us
    pallas_call x1, Pallas kernels, local(): pl.pallas_call(last_kernel, out_shape=[jax.ShapeDtypeStruct((late,) + pie...  3.3 us
    pallas_call x1, Pallas kernels, local(): pl.pallas_call(prep_kernel, out_shape=[message] * (parts - 1) + [own_shap...  3.06 us
    pallas_call x1, Pallas kernels, local(): pl.pallas_call(send_kernel, out_shape=[all_shape, jax.ShapeDtypeStruct((1...  2.2 us
  transfers between devices with their start and end apart: 8, of which 6 were waited for; matrix products, arithmetic and copies ran while one was open for 1% of the time, Pallas kernels for 8%

profile of v9, /device:TPU:1, one launch (start us, length us, event | category | flops | bytes accessed | tf_op | source)
XLA Modules:
  0.0 105.6 jit_solution(14322734981206939409)
XLA Ops:
  0.6 2.2 %send.1 = (bf16[128,32,128]{2,1,0:T(8,128)(2,1)}, s32[1,512]{1,0:T(1,128)}) custom-call(s32[1]{0:T(128)} %bitcast.1.base_ref, s32[16,512]{1,0:T(8,128)} %bitcast.9, bf16[4,16,128]{2,1,0:T(8,128)(2,1)} %keys_ref.1, bf16[4,16,128]{2,1,0:T(8,128)(2,1)} %values_ref.1), custom_call_target="tpu_custom_call" | custom-call | tf_op jit(solution)/shard_map/send/pallas_call | solution.py:277
  2.8 0.0 copy-start
  2.8 0.0 copy-start.1
  2.8 18.9 %all-to-all-start = ((bf16[128,32,128]{2,1,0:T(8,128)(2,1)}), bf16[128,32,128]{2,1,0:T(8,128)(2,1)S(1)}, u32[]{:S(2)}, u32[]{:S(2)}) async-start(bf16[128,32,128]{2,1,0:T(8,128)(2,1)} %get-tuple-element.16), calls=%async_computation | async-start | bytes 2097152 | tf_op jit(solution)/shard_map/all_to_all | solution.py:35
  21.7 0.0 copy-done
  21.7 0.0 copy-done.1
  21.8 3.1 %prep.1 = (bf16[272,1024]{1,0:T(8,128)(2,1)}, bf16[272,1024]{1,0:T(8,128)(2,1)}, bf16[272,1024]{1,0:T(8,128)(2,1)}, bf16[16,128]{1,0:T(8,128)(2,1)S(1)}) custom-call(s32[1]{0:T(128)} %bitcast.place_ref, bf16[128,4096]{1,0:T(8,128)(2,1)S(1)} %copy-done, bf16[128,4096]{1,0:T(8,128)(2,1)S(1)} %copy-done.1, bf16[128,4096]{1,0:T(8,128)(2,1)} %o_ref.1), custom_call_target="tpu_custom_call" | custom-call | flops 1048576 | bytes 5242880 | tf_op jit(solution)/shard_map/prep/pallas_call | solution.py:260
  24.8 4.7 %collective-permute-start = (bf16[272,1024]{1,0:T(8,128)(2,1)}, bf16[272,1024]{1,0:T(8,128)(2,1)S(1)}, u32[]{:S(2)}, u32[]{:S(2)}) collective-permute-start(bf16[272,1024]{1,0:T(8,128)(2,1)} %get-tuple-element.18), channel_id=1, source_target_pairs={{0,2},{1,3},{2,0},{3,1},{4,6},{5,7},{6,4},{7,5},{8,10},{9,11},{10,... | collective-permute-start | bytes 1671176 | tf_op jit(solution)/shard_map/ppermute | solution.py:274
  29.5 2.2 %collective-permute-start.2 = (bf16[272,1024]{1,0:T(8,128)(2,1)}, bf16[272,1024]{1,0:T(8,128)(2,1)S(1)}, u32[]{:S(2)}, u32[]{:S(2)}) collective-permute-start(bf16[272,1024]{1,0:T(8,128)(2,1)} %get-tuple-element.21), channel_id=1, source_target_pairs={{0,1},{1,2},{2,3},{3,0},{4,5},{5,6},{6,7},{7,4},{8,9},{9,10},{10,1... | collective-permute-start | bytes 1671176 | tf_op jit(solution)/shard_map/ppermute | solution.py:274
  31.7 4.3 %collective-permute-start.3 = (bf16[272,1024]{1,0:T(8,128)(2,1)}, bf16[272,1024]{1,0:T(8,128)(2,1)S(1)}, u32[]{:S(2)}, u32[]{:S(2)}) collective-permute-start(bf16[272,1024]{1,0:T(8,128)(2,1)} %get-tuple-element.22), channel_id=1, source_target_pairs={{0,3},{1,0},{2,1},{3,2},{4,7},{5,4},{6,5},{7,6},{8,11},{9,8},{10,9... | collective-permute-start | bytes 1671176 | tf_op jit(solution)/shard_map/ppermute | solution.py:274
  36.0 0.8 constant_dynamic-slice_fusion
  36.8 0.1 copy.13.lists_ref
  36.8 0.0 copy-start.2
  36.9 5.2 %collective-permute-done.rest_0_ = bf16[272,1024]{1,0:T(8,128)(2,1)S(1)} collective-permute-done((bf16[272,1024]{1,0:T(8,128)(2,1)}, bf16[272,1024]{1,0:T(8,128)(2,1)S(1)}, u32[]{:S(2)}, u32[]{:S(2)}) %collective-permute-start) | collective-permute-done | bytes 557088 | tf_op jit(solution)/shard_map/ppermute | solution.py:274
  42.1 11.5 %all-to-all-done.incoming_ref = bf16[128,32,128]{2,1,0:T(8,128)(2,1)S(1)} async-done(((bf16[128,32,128]{2,1,0:T(8,128)(2,1)}), bf16[128,32,128]{2,1,0:T(8,128)(2,1)S(1)}, u32[]{:S(2)}, u32[]{:S(2)}) %all-to-all-start) | async-done | bytes 1048608 | tf_op jit(solution)/shard_map/all_to_all | solution.py:35
  53.5 0.0 copy-done.2
  53.5 4.6 %attention_first.1 = (bf16[128,4096]{1,0:T(8,128)(2,1)}, bf16[1,128,1024]{2,1,0:T(8,128)(2,1)S(1)}, bf16[128,32,128]{2,1,0:T(8,128)(2,1)}) custom-call(s32[1]{0:T(128)} %bitcast.place_ref, s32[4,16]{1,0:T(4,128)S(1)} %shift-left_or_fusion.slots_ref, s32[4,16]{1,0:T(4,128)S(1)} %copy.13.lists_ref, s32[512]{0:T(512)S(1)} %copy-done.2, ...), custom_call_target="tpu_custom_call" | custom-call | flops 671088640 | bytes 2097152 | tf_op jit(solution)/shard_map/attention_first/pallas_call | solution.py:313
  58.1 0.0 collective-permute-done.2.rest_0_
  58.1 0.0 collective-permute-done.3.rest_1_
  58.2 3.3 %attention_last.1 = (bf16[2,128,1024]{2,1,0:T(8,128)(2,1)S(1)}, bf16[128,32,128]{2,1,0:T(8,128)(2,1)}) custom-call(s32[1]{0:T(128)} %bitcast.place_ref, s32[4,16]{1,0:T(4,128)S(1)} %shift-left_or_fusion.slots_ref, s32[4,16]{1,0:T(4,128)S(1)} %copy.13.lists_ref, s32[512]{0:T(512)S(1)} %copy-done.2, ...), custom_call_target="tpu_custom_call", output_to_operand_aliasing={{1}: (7, {})} | custom-call | flops 671088640 | bytes 2097152 | tf_op jit(solution)/shard_map/attention_last/pallas_call | solution.py:338
  61.5 10.7 %all-to-all-start.1 = ((bf16[128,32,128]{2,1,0:T(8,128)(2,1)}), bf16[128,32,128]{2,1,0:T(8,128)(2,1)S(1)}, u32[]{:S(2)}, u32[]{:S(2)}) async-start(bf16[128,32,128]{2,1,0:T(8,128)(2,1)} %get-tuple-element.26), calls=%async_computation.1 | async-start | bytes 2097152 | tf_op jit(solution)/shard_map/all_to_all | solution.py:35
  72.2 3.0 %collective-permute-start.5 = (bf16[128,1024]{1,0:T(8,128)(2,1)S(1)}, bf16[128,1024]{1,0:T(8,128)(2,1)S(1)}, u32[]{:S(2)}, u32[]{:S(2)}) collective-permute-start(bf16[128,1024]{1,0:T(8,128)(2,1)S(1)} %get-tuple-element.29), channel_id=1, source_target_pairs={{0,1},{1,2},{2,3},{3,0},{4,5},{5,6},{6,7},{7,4},{8,9},{9,10},{10,1... | collective-permute-start | bytes 786440 | tf_op jit(solution)/shard_map/ppermute | solution.py:274
  75.3 3.5 %collective-permute-start.4 = (bf16[128,1024]{1,0:T(8,128)(2,1)S(1)}, bf16[128,1024]{1,0:T(8,128)(2,1)S(1)}, u32[]{:S(2)}, u32[]{:S(2)}) collective-permute-start(bf16[128,1024]{1,0:T(8,128)(2,1)S(1)} %get-tuple-element.30), channel_id=1, source_target_pairs={{0,3},{1,0},{2,1},{3,2},{4,7},{5,4},{6,5},{7,6},{8,11},{9,8},{10,9... | collective-permute-start | bytes 786440 | tf_op jit(solution)/shard_map/ppermute | solution.py:274
  78.8 3.3 %collective-permute-start.1 = (bf16[128,1024]{1,0:T(8,128)(2,1)S(1)}, bf16[128,1024]{1,0:T(8,128)(2,1)S(1)}, u32[]{:S(2)}, u32[]{:S(2)}) collective-permute-start(bf16[128,1024]{1,0:T(8,128)(2,1)S(1)} %bitcast.8), channel_id=1, source_target_pairs={{0,2},{1,3},{2,0},{3,1},{4,6},{5,7},{6,4},{7,5},{8,10},{9,11},{10,... | collective-permute-start | bytes 786440 | tf_op jit(solution)/shard_map/ppermute | solution.py:274
  82.1 0.6 collective-permute-done.5.rest_2_
  82.6 1.5 %collective-permute-done.4.rest_1_ = bf16[128,1024]{1,0:T(8,128)(2,1)S(1)} collective-permute-done((bf16[128,1024]{1,0:T(8,128)(2,1)S(1)}, bf16[128,1024]{1,0:T(8,128)(2,1)S(1)}, u32[]{:S(2)}, u32[]{:S(2)}) %collective-permute-start.4) | collective-permute-done | bytes 262176 | tf_op jit(solution)/shard_map/ppermute | solution.py:274
  84.1 4.7 %collective-permute-done.1.rest_0_ = bf16[128,1024]{1,0:T(8,128)(2,1)S(1)} collective-permute-done((bf16[128,1024]{1,0:T(8,128)(2,1)S(1)}, bf16[128,1024]{1,0:T(8,128)(2,1)S(1)}, u32[]{:S(2)}, u32[]{:S(2)}) %collective-permute-start.1) | collective-permute-done | bytes 262176 | tf_op jit(solution)/shard_map/ppermute | solution.py:274
  88.8 0.0 copy-start.3
  88.8 0.9 place.1
  89.7 14.3 %all-to-all-done.1.terms_ref = bf16[128,32,128]{2,1,0:T(8,128)(2,1)S(1)} async-done(((bf16[128,32,128]{2,1,0:T(8,128)(2,1)}), bf16[128,32,128]{2,1,0:T(8,128)(2,1)S(1)}, u32[]{:S(2)}, u32[]{:S(2)}) %all-to-all-start.1) | async-done | bytes 1048608 | tf_op jit(solution)/shard_map/all_to_all | solution.py:35
  104.0 0.0 copy-done.3
  104.0 1.6 %sum.1 = (bf16[4,16,128]{2,1,0:T(8,128)(2,1)}, bf16[4,16,128]{2,1,0:T(8,128)(2,1)}) custom-call(s32[1,512]{1,0:T(1,128)S(1)} %copy-done.3, bf16[128,32,128]{2,1,0:T(8,128)(2,1)S(1)} %all-to-all-done.1.terms_ref), custom_call_target="tpu_custom_call" | custom-call | tf_op jit(solution)/shard_map/sum/pallas_call | solution.py:365
  (2 shorter events, 0.1 us)
Async XLA Ops:
  2.8 18.9 %copy-start = (bf16[128,4096]{1,0:T(8,128)(2,1)S(1)}, bf16[128,4096]{1,0:T(8,128)(2,1)}, u32[]{:S(2)}) copy-start(bf16[128,4096]{1,0:T(8,128)(2,1)} %q_ref.3) | copy-start | bytes 3145732
  2.8 18.9 %copy-start.1 = (bf16[128,4096]{1,0:T(8,128)(2,1)S(1)}, bf16[128,4096]{1,0:T(8,128)(2,1)}, u32[]{:S(2)}) copy-start(bf16[128,4096]{1,0:T(8,128)(2,1)} %g_ref.3) | copy-start | bytes 3145732
  2.8 50.7 %all-to-all-start = ((bf16[128,32,128]{2,1,0:T(8,128)(2,1)}), bf16[128,32,128]{2,1,0:T(8,128)(2,1)S(1)}, u32[]{:S(2)}, u32[]{:S(2)}) async-start(bf16[128,32,128]{2,1,0:T(8,128)(2,1)} %get-tuple-element.16), calls=%async_computation | async-start | bytes 2097152 | tf_op jit(solution)/shard_map/all_to_all | solution.py:35
  24.8 17.3 %collective-permute-start = (bf16[272,1024]{1,0:T(8,128)(2,1)}, bf16[272,1024]{1,0:T(8,128)(2,1)S(1)}, u32[]{:S(2)}, u32[]{:S(2)}) collective-permute-start(bf16[272,1024]{1,0:T(8,128)(2,1)} %get-tuple-element.18), channel_id=1, source_target_pairs={{0,2},{1,3},{2,0},{3,1},{4,6},{5,7},{6,4},{7,5},{8,10},{9,11},{10,... | collective-permute-start | bytes 1671176 | tf_op jit(solution)/shard_map/ppermute | solution.py:274
  29.5 28.7 %collective-permute-start.2 = (bf16[272,1024]{1,0:T(8,128)(2,1)}, bf16[272,1024]{1,0:T(8,128)(2,1)S(1)}, u32[]{:S(2)}, u32[]{:S(2)}) collective-permute-start(bf16[272,1024]{1,0:T(8,128)(2,1)} %get-tuple-element.21), channel_id=1, source_target_pairs={{0,1},{1,2},{2,3},{3,0},{4,5},{5,6},{6,7},{7,4},{8,9},{9,10},{10,1... | collective-permute-start | bytes 1671176 | tf_op jit(solution)/shard_map/ppermute | solution.py:274
  31.7 26.4 %collective-permute-start.3 = (bf16[272,1024]{1,0:T(8,128)(2,1)}, bf16[272,1024]{1,0:T(8,128)(2,1)S(1)}, u32[]{:S(2)}, u32[]{:S(2)}) collective-permute-start(bf16[272,1024]{1,0:T(8,128)(2,1)} %get-tuple-element.22), channel_id=1, source_target_pairs={{0,3},{1,0},{2,1},{3,2},{4,7},{5,4},{6,5},{7,6},{8,11},{9,8},{10,9... | collective-permute-start | bytes 1671176 | tf_op jit(solution)/shard_map/ppermute | solution.py:274
  36.8 16.7 %copy-start.2 = (s32[512]{0:T(512)S(1)}, s32[512]{0:T(512)}, u32[]{:S(2)}) copy-start(s32[512]{0:T(512)} %lengths_ref.3) | copy-start | bytes 6148
  61.5 42.6 %all-to-all-start.1 = ((bf16[128,32,128]{2,1,0:T(8,128)(2,1)}), bf16[128,32,128]{2,1,0:T(8,128)(2,1)S(1)}, u32[]{:S(2)}, u32[]{:S(2)}) async-start(bf16[128,32,128]{2,1,0:T(8,128)(2,1)} %get-tuple-element.26), calls=%async_computation.1 | async-start | bytes 2097152 | tf_op jit(solution)/shard_map/all_to_all | solution.py:35
  72.2 10.4 %collective-permute-start.5 = (bf16[128,1024]{1,0:T(8,128)(2,1)S(1)}, bf16[128,1024]{1,0:T(8,128)(2,1)S(1)}, u32[]{:S(2)}, u32[]{:S(2)}) collective-permute-start(bf16[128,1024]{1,0:T(8,128)(2,1)S(1)} %get-tuple-element.29), channel_id=1, source_target_pairs={{0,1},{1,2},{2,3},{3,0},{4,5},{5,6},{6,7},{7,4},{8,9},{9,10},{10,1... | collective-permute-start | bytes 786440 | tf_op jit(solution)/shard_map/ppermute | solution.py:274
  75.3 8.9 %collective-permute-start.4 = (bf16[128,1024]{1,0:T(8,128)(2,1)S(1)}, bf16[128,1024]{1,0:T(8,128)(2,1)S(1)}, u32[]{:S(2)}, u32[]{:S(2)}) collective-permute-start(bf16[128,1024]{1,0:T(8,128)(2,1)S(1)} %get-tuple-element.30), channel_id=1, source_target_pairs={{0,3},{1,0},{2,1},{3,2},{4,7},{5,4},{6,5},{7,6},{8,11},{9,8},{10,9... | collective-permute-start | bytes 786440 | tf_op jit(solution)/shard_map/ppermute | solution.py:274
  78.8 10.1 %collective-permute-start.1 = (bf16[128,1024]{1,0:T(8,128)(2,1)S(1)}, bf16[128,1024]{1,0:T(8,128)(2,1)S(1)}, u32[]{:S(2)}, u32[]{:S(2)}) collective-permute-start(bf16[128,1024]{1,0:T(8,128)(2,1)S(1)} %bitcast.8), channel_id=1, source_target_pairs={{0,2},{1,3},{2,0},{3,1},{4,6},{5,7},{6,4},{7,5},{8,10},{9,11},{10,... | collective-permute-start | bytes 786440 | tf_op jit(solution)/shard_map/ppermute | solution.py:274
  88.8 15.2 %copy-start.3 = (s32[1,512]{1,0:T(1,128)S(1)}, s32[1,512]{1,0:T(1,128)}, u32[]{:S(2)}) copy-start(s32[1,512]{1,0:T(1,128)} %get-tuple-element.25.pick_ref) | copy-start | bytes 6148
